TPU v7x, 1024 devices: a whole 8x8x8 slice. The times are simulated.
1024 devices in a mesh: row: 8 (over z), col: 16 (over y, x_lo), layer: 8 (over x_hi, core).
Axes of the slice: x: 8 (x_hi: 4, x_lo: 2; x = x_hi * 2 + x_lo), y: 8, z: 8, core: 2. Of those that a mesh axis runs over, the one named last changes fastest.
Arguments:
- stored: bfloat16 [8192, 8192], P(('row', 'layer')), may hold values from -0.5 to 0.5
- pattern: int32 [64, 64], replicated, may hold values 0 or 1
Outputs:
- density_square: bfloat16 [8192, 8192], P(('row', 'layer'), 'col')
All inputs are finite; a program needn't handle non-finite values.
Results may differ from a plain program's by a relative error of at most 0.0011.
Values may be sent and summed in bfloat16 or wider, within the bound.
No kernel may reach another device: no remote copies, remote signals or barrier semaphores. Data moves between devices by JAX's collectives and lax.ppermute only.
A program may use at most 32 MiB of HBM per device.

v0:
```python
import jax
import jax.numpy as jnp
from jax import lax
from jax.sharding import PartitionSpec as P


def body(stored, pattern):
    block_size, full_width = stored.shape
    row_group = lax.axis_index(("row", "layer"))
    column_index = lax.axis_index("col")
    column_strip = lax.all_to_all(stored, ("row", "layer"), split_axis=1, concat_axis=0, tiled=True)
    lower_source = column_strip.T
    row_pattern = jnp.repeat(
        lax.dynamic_index_in_dim(pattern, row_group, 0, keepdims=False), block_size
    )
    column_pattern = jnp.repeat(
        lax.dynamic_index_in_dim(pattern, row_group, 1, keepdims=False), block_size
    )
    row_position = row_group * block_size + jnp.arange(block_size, dtype=jnp.int32)[:, None]
    column_position = jnp.arange(full_width, dtype=jnp.int32)[None, :]
    nothing = jnp.zeros_like(stored)
    upper_part = jnp.where(row_pattern[None, :] > 0, stored, nothing)
    lower_part = jnp.where(column_pattern[None, :] > 0, lower_source, nothing)
    full_rows = jnp.where(column_position >= row_position, upper_part, lower_part)
    layer_count = lax.axis_size("layer")
    row_count = lax.axis_size("row")
    panel_width = full_width // lax.axis_size("col")
    column_panel = lax.dynamic_slice_in_dim(full_rows, column_index * panel_width, panel_width, 1)
    grid = full_rows.reshape(block_size, row_count, layer_count, block_size)
    owned = lax.all_to_all(grid, "layer", split_axis=2, concat_axis=0, tiled=True)
    left_side = owned.reshape(layer_count * block_size, row_count * block_size)
    running = lax.dot_general(
        left_side,
        lax.all_gather(column_panel, "layer", axis=0, tiled=True),
        (((0,), (0,)), ((), ())),
        preferred_element_type=jnp.float32,
    )
    summed = lax.psum_scatter(running, "row", scatter_dimension=0, tiled=True)
    return summed.astype(jnp.bfloat16)


def solution(mesh):
    return jax.shard_map(
        body,
        mesh=mesh,
        in_specs=(P(("row", "layer"), None), P()),
        out_specs=P(("row", "layer"), "col"),
        check_vma=False,
    )
```

profile of v0, /device:TPU:1, one launch (start us, length us, event | category | flops | bytes accessed | tf_op | source)
XLA Modules:
  0.0 222.8 jit_solution(2346247754666381098)
XLA Ops:
  6.5 3.2 %copy.8 = bf16[128,8192]{0,1:T(8,128)(2,1)S(1)} copy(bf16[128,8192]{1,0:T(8,128)(2,1)} %param.2) | data formatting | bytes 4194304 | tf_op args[0]
  9.8 2.9 %copy.9 = bf16[128,64,128]{2,0,1:T(8,128)(2,1)} copy(bf16[128,64,128]{0,2,1:T(8,128)(2,1)S(1)} %bitcast.27) | data formatting | bytes 4194304 | tf_op jit(solution)/shard_map/all_to_all | solution.py:11
  12.7 0.0 copy-start
  12.7 23.8 %all-to-all-start = ((bf16[128,64,128]{2,0,1:T(8,128)(2,1)}), bf16[128,64,128]{2,0,1:T(8,128)(2,1)S(1)}, u32[]{:S(2)}, u32[]{:S(2)}) async-start(bf16[128,64,128]{2,0,1:T(8,128)(2,1)} %copy.9), calls=%async_computation | async-start | bytes 4194304 | tf_op jit(solution)/shard_map/all_to_all | solution.py:11
  36.5 0.0 copy-done
  36.5 0.2 fusion.4
  36.7 0.1 broadcast_bitcast_fusion
  36.8 66.5 %all-to-all-done = bf16[128,64,128]{2,0,1:T(8,128)(2,1)S(1)} async-done(((bf16[128,64,128]{2,0,1:T(8,128)(2,1)}), bf16[128,64,128]{2,0,1:T(8,128)(2,1)S(1)}, u32[]{:S(2)}, u32[]{:S(2)}) %all-to-all-start) | async-done | bytes 2097184 | tf_op jit(solution)/shard_map/all_to_all | solution.py:11
  103.3 2.9 %copy.10 = bf16[8192,128]{0,1:T(8,128)(2,1)} copy(bf16[8192,128]{1,0:T(8,128)(2,1)S(1)} %bitcast.26) | data formatting | bytes 4194304 | tf_op jit(solution)/shard_map/all_to_all | solution.py:11
  106.2 3.4 %fusion = bf16[128,8192]{1,0:T(8,128)(2,1)S(1)} fusion(bf16[8192,128]{0,1:T(8,128)(2,1)} %copy.10, bf16[128,8192]{1,0:T(8,128)(2,1)} %param.2, s32[128]{0:T(128)S(1)} %iota_add_fusion, pred[8192]{0:T(1024)(128)(4,1)S(1)} %get-tuple-element.5, pred[8192]{0:T(1024)(128)(4,1)S(1)} %get-tuple-element.6), kind=kLoop, calls=%fused_computation.1 | loop fusion | flops 4194304 | bytes 6308352 | tf_op jit(solution)/shard_map/jit(_where)/select_n | solution.py:24
  109.6 0.6 copy.12
  110.2 1.7 copy.11
  111.9 4.3 %all-to-all-start.1 = ((bf16[128,8,8,128]{3,1,0,2:T(8,128)(2,1)}), bf16[128,8,8,128]{3,1,0,2:T(8,128)(2,1)}, u32[]{:S(2)}, u32[]{:S(2)}) async-start(bf16[128,8,8,128]{3,1,0,2:T(8,128)(2,1)} %copy.11), calls=%async_computation.1 | async-start | bytes 4194304 | tf_op jit(solution)/shard_map/all_to_all | solution.py:30
  116.2 0.0 all-gather.2.cloned.1.call-start
  116.2 0.7 constant_dynamic-slice_fusion
  116.9 0.0 all-gather.2.cloned.1.call-update
  116.9 0.0 reduce-scatter.2.cloned.1.call-start
  117.0 40.0 %all-gather.2.cloned.1.call-done = bf16[1024,512]{1,0:T(8,128)(2,1)} async-done(((bf16[128,512]{1,0:T(8,128)(2,1)}), bf16[1024,512]{1,0:T(8,128)(2,1)}) %all-gather.2.cloned.1.call-update) | async-done | bytes 1048592 | tf_op jit(solution)/shard_map/all_gather | solution.py:34
  157.0 4.7 %all-to-all-done.1 = bf16[128,8,8,128]{3,1,0,2:T(8,128)(2,1)} async-done(((bf16[128,8,8,128]{3,1,0,2:T(8,128)(2,1)}), bf16[128,8,8,128]{3,1,0,2:T(8,128)(2,1)}, u32[]{:S(2)}, u32[]{:S(2)}) %all-to-all-start.1) | async-done | bytes 2097184 | tf_op jit(solution)/shard_map/all_to_all | solution.py:30
  161.7 4.5 %fusion.1 = f32[1024,512]{1,0:T(8,128)} fusion(bf16[1024,512]{1,0:T(8,128)(2,1)} %all-gather.2.cloned.1.call-done, bf16[128,8,8,128]{3,2,1,0:T(8,128)(2,1)} %bitcast.16), kind=kOutput, calls=%fused_computation.2 | convolution fusion | flops 1073741824 | bytes 5242880 | tf_op jit(solution)/shard_map/dot_general | solution.py:32
  166.2 0.0 reduce-scatter.2.cloned.1.call-update
  166.2 48.1 %reduce-scatter.2.cloned.1.call-done = f32[128,512]{1,0:T(8,128)} async-done(((f32[1024,512]{1,0:T(8,128)}), f32[128,512]{1,0:T(8,128)}) %reduce-scatter.2.cloned.1.call-update) | async-done | bytes 262160 | tf_op jit(solution)/shard_map/reduce_scatter | solution.py:38
  214.3 1.6 convert_element_type.3
  (2 shorter events, 0.0 us)
Async XLA Ops:
  12.7 23.8 %copy-start = (s32[64,64]{1,0:T(8,128)S(1)}, s32[64,64]{1,0:T(8,128)}, u32[]{:S(2)}) copy-start(s32[64,64]{1,0:T(8,128)} %param.3) | copy-start | bytes 49156
  12.7 90.6 %all-to-all-start = ((bf16[128,64,128]{2,0,1:T(8,128)(2,1)}), bf16[128,64,128]{2,0,1:T(8,128)(2,1)S(1)}, u32[]{:S(2)}, u32[]{:S(2)}) async-start(bf16[128,64,128]{2,0,1:T(8,128)(2,1)} %copy.9), calls=%async_computation | async-start | bytes 4194304 | tf_op jit(solution)/shard_map/all_to_all | solution.py:11
  111.9 49.9 %all-to-all-start.1 = ((bf16[128,8,8,128]{3,1,0,2:T(8,128)(2,1)}), bf16[128,8,8,128]{3,1,0,2:T(8,128)(2,1)}, u32[]{:S(2)}, u32[]{:S(2)}) async-start(bf16[128,8,8,128]{3,1,0,2:T(8,128)(2,1)} %copy.11), calls=%async_computation.1 | async-start | bytes 4194304 | tf_op jit(solution)/shard_map/all_to_all | solution.py:30
  116.2 40.8 %all-gather.2.cloned.1.call-start = ((), (), s32[]{:S(2)}) async-start(), calls=%async_computation.3 | async-start | bytes 1179648 | tf_op jit(solution)/shard_map/all_gather | solution.py:34
  116.9 97.4 %reduce-scatter.2.cloned.1.call-start = ((), (), s32[]{:S(2)}) async-start(), calls=%async_computation.4 | async-start | bytes 2359296 | tf_op jit(solution)/shard_map/reduce_scatter | solution.py:38
Sparse Core Ops, SparseCore 0:
  119.8 37.2 all-gather.1
  166.3 47.9 reduce-scatter.1
where the time goes:
time: 227 us; the launch traced here: 223 us
  waiting for transfers between devices  159 us (70%)
  starting transfers between devices  28.2 us (12%)
  between operations  13.5 us (6%)
  local copies, waits for them, and re-layouts  12.1 us (5%)
  other arithmetic  5.21 us (2%)
  matrix products  4.45 us (2%)
    all_to_all x1, waiting for transfers between devices, body(): lax.all_to_all(stored, ('row', 'layer'), split_axis=1, concat_axis=0, til...  66.5 us
    reduce_scatter x1, waiting for transfers between devices, body(): summed = lax.psum_scatter(running, 'row', scatter_dimension=0, tiled=True)  48.1 us
    all_gather x1, waiting for transfers between devices, body(): lax.all_gather(column_panel, 'layer', axis=0, tiled=True)  40 us
    all_to_all x1, starting transfers between devices, body(): lax.all_to_all(stored, ('row', 'layer'), split_axis=1, concat_axis=0, til...  23.8 us
    all_to_all x2, local copies, waits for them, and re-layouts, body(): lax.all_to_all(stored, ('row', 'layer'), split_axis=1, concat_axis=0, til...  5.85 us
    all_to_all x1, waiting for transfers between devices, body(): lax.all_to_all(grid, 'layer', split_axis=2, concat_axis=0, tiled=True)  4.7 us
  transfers between devices with their start and end apart: 4, of which 4 were waited for; matrix products, arithmetic and copies ran while one was open for 0% of the time, Pallas kernels for 0%

commit v1 on v0

v1 whole, which is shorter than its diff:
```python
import jax
import jax.numpy as jnp
from jax import lax
from jax.sharding import PartitionSpec as P

B = 128


def body(stored, pattern):
    rows, width = stored.shape
    nz = lax.axis_size("row")
    nl = lax.axis_size("layer")
    nc = lax.axis_size("col")
    z = lax.axis_index("row")
    l = lax.axis_index("layer")
    c = lax.axis_index("col")
    g = z * nl + l
    plane = width // nz
    panel = width // nc
    per = panel // B
    half = nl // per

    row_pattern = lax.dynamic_index_in_dim(pattern, g, 0, keepdims=False)
    row_position = g * B + jnp.arange(B, dtype=jnp.int32)[:, None]
    column_position = jnp.arange(width, dtype=jnp.int32)[None, :]
    present = jnp.repeat(row_pattern, B)[None, :] > 0
    zero = jnp.zeros((), stored.dtype)
    upper = jnp.where(present & (column_position >= row_position), stored, zero)
    strict = jnp.where(present & (column_position > row_position), stored, zero)

    def flat(zz, cc, ll):
        return (zz * nc + cc) * nl + ll

    received = []
    for s in range(per):
        pairs = []
        for zz in range(nz):
            for cc in range(nc):
                for ll in range(nl):
                    a = zz * nl + ll
                    t = cc * per + (ll % per + s) % per
                    if a <= t:
                        pairs.append((flat(zz, cc, ll), flat(t // nl, a // per, t % nl)))
        j = (l % per + s) % per
        block = lax.dynamic_slice(upper, (0, (c * per + j) * B), (B, B))
        received.append(lax.ppermute(block, ("row", "col", "layer"), pairs))
    ordered = jnp.concatenate(received[::-1] + received[::-1][:-1], axis=0)
    ordered = lax.dynamic_slice(ordered, (((per - 1 - l) % per) * B, 0), (panel, B))
    tile_column = c * panel + jnp.arange(panel, dtype=jnp.int32)[None, :]
    tile = lax.dynamic_slice(upper, (0, c * panel), (B, panel))
    tile = jnp.where(tile_column >= row_position, tile, ordered.T)

    lower = []
    right = []
    for s in range(nz):
        shift = (nz - s) % nz
        target = lax.rem(z + shift, nz)
        piece = lax.dynamic_slice(upper, (0, target * plane), (B, plane))
        if shift:
            piece = lax.ppermute(piece, "row", [(k, k + shift) for k in range(nz - shift)])
        lower.append(piece)
        right.append(tile if not shift else lax.ppermute(tile, "row", [(k, (k + shift) % nz) for k in range(nz)]))
    lower = jnp.concatenate(lower, axis=0)
    right = jnp.concatenate(right, axis=0)

    rolled = lax.dynamic_slice(jnp.concatenate([strict, strict], axis=1), (0, z * plane), (B, width))
    rolled = rolled.reshape(B, nz, nl, B).transpose(2, 0, 1, 3)
    high = lax.all_to_all(rolled, "layer", split_axis=0, concat_axis=0, tiled=True)
    high = high.reshape(nl * B, nz * B)

    partial = lax.dot_general(
        lower, right, (((0,), (0,)), ((), ())), preferred_element_type=jnp.float32
    ) + jnp.dot(high, right, preferred_element_type=jnp.float32)
    parts = lax.all_to_all(partial.reshape(nl, B, panel), "layer", split_axis=0, concat_axis=0, tiled=True)
    return jnp.sum(parts, axis=0).astype(jnp.bfloat16)


def solution(mesh):
    return jax.shard_map(
        body,
        mesh=mesh,
        in_specs=(P(("row", "layer"), None), P()),
        out_specs=P(("row", "layer"), "col"),
        check_vma=False,
    )
```

time: 227 us -> 255 us (1.12)
  the two profiles are of different devices: /device:TPU:1 before, /device:TPU:48 now
where the time goes in v1:
time: 255 us; the launch traced here: 254 us
  starting transfers between devices  88.4 us (35%)
  waiting for transfers between devices  72.3 us (28%)
  blocking collectives  57.8 us (23%)
  local copies, waits for them, and re-layouts  15.4 us (6%)
  other arithmetic  15.3 us (6%)
  matrix products  4.1 us (2%)
    all_to_all x1, blocking collectives, body(): lax.all_to_all(partial.reshape(nl, B, panel), 'layer', split_axis=0, conc...  57.8 us
    ppermute x7, starting transfers between devices, body(): lax.ppermute(tile, 'row', [(k, (k + shift) % nz) for k in range(nz)])  47.5 us
    ppermute x4, waiting for transfers between devices, body(): received.append(lax.ppermute(block, ('row', 'col', 'layer'), pairs))  27 us
    ppermute x7, waiting for transfers between devices, body(): lax.ppermute(piece, 'row', [(k, k + shift) for k in range(nz - shift)])  24.6 us
    ppermute x7, waiting for transfers between devices, body(): lax.ppermute(tile, 'row', [(k, (k + shift) % nz) for k in range(nz)])  20.7 us
    ppermute x7, starting transfers between devices, body(): lax.ppermute(piece, 'row', [(k, k + shift) for k in range(nz - shift)])  18 us
    ppermute x4, starting transfers between devices, body(): received.append(lax.ppermute(block, ('row', 'col', 'layer'), pairs))  16.2 us
    unnamed x20, local copies, waits for them, and re-layouts  8.93 us
  transfers between devices with their start and end apart: 19, of which 7 were waited for; matrix products, arithmetic and copies ran while one was open for 3% of the time, Pallas kernels for 0%

profile of v1, /device:TPU:48, one launch (start us, length us, event | category | flops | bytes accessed | tf_op | source)
XLA Modules:
  0.0 253.7 jit_solution(9014131425708661174)
XLA Ops:
  0.0 0.7 compare_bitcast_fusion
  0.7 0.1 broadcast_bitcast_fusion
  0.8 4.1 %copy.9 = bf16[128,8192]{0,1:T(8,128)(2,1)} copy(bf16[128,8192]{1,0:T(8,128)(2,1)} %param.2) | data formatting | bytes 4194304 | tf_op args[0]
  4.9 6.4 %fusion.3 = (bf16[128,8192]{0,1:T(8,128)(2,1)S(1)}, bf16[128,8192]{0,1:T(8,128)(2,1)S(1)}) fusion(bf16[128,8192]{0,1:T(8,128)(2,1)} %copy.9, s32[128]{0:T(128)S(1)} %iota_add_fusion.1, pred[8192]{0:T(1024)(128)(4,1)S(1)} %broadcast_bitcast_fusion), kind=kLoop, calls=%fused_computation.7 | loop fusion | flops 6291456 | bytes 6300160 | tf_op jit(solution)/shard_map/jit(_where)/select_n | solution.py:29
  11.2 7.3 %fusion.4 = bf16[128,8192]{0,1:T(8,128)(2,1)S(1)} fusion(s32[]{:T(128)S(6)} %select_n.117, bf16[128,8192]{0,1:T(8,128)(2,1)S(1)} %get-tuple-element.7), kind=kLoop, calls=%fused_computation.8 | loop fusion | flops 4194304 | bytes 4194308 | tf_op jit(solution)/shard_map/concatenate | solution.py:66
  18.5 1.4 copy.12
  20.0 6.8 %all-to-all-start = ((bf16[8,128,8,128]{1,3,2,0:T(8,128)(2,1)}), bf16[8,128,8,128]{1,3,2,0:T(8,128)(2,1)}, u32[]{:S(2)}, u32[]{:S(2)}) async-start(bf16[8,128,8,128]{1,3,2,0:T(8,128)(2,1)} %copy.12), calls=%async_computation | async-start | bytes 4194304 | tf_op jit(solution)/shard_map/all_to_all | solution.py:68
  26.7 9.9 %collective-permute-start.10 = (bf16[128,128]{0,1:T(8,128)(2,1)S(1)}, bf16[128,128]{0,1:T(8,128)(2,1)S(1)}, u32[]{:S(2)}, u32[]{:S(2)}) collective-permute-start(bf16[128,128]{0,1:T(8,128)(2,1)S(1)} %get-tuple-element.17), channel_id=1, source_target_pairs={{0,0},{1,1},{2,2},{3,3},{8,4},{9,5},{10,6},{11,7},{12,12},{13,13},... | collective-permute-start | bytes 98312 | tf_op jit(solution)/shard_map/ppermute | solution.py:46
  36.7 1.4 collective-permute-start.9
  38.1 3.5 %collective-permute-start.8 = (bf16[128,128]{0,1:T(8,128)(2,1)S(1)}, bf16[128,128]{0,1:T(8,128)(2,1)S(1)}, u32[]{:S(2)}, u32[]{:S(2)}) collective-permute-start(bf16[128,128]{0,1:T(8,128)(2,1)S(1)} %get-tuple-element.19), channel_id=1, source_target_pairs={{0,2},{1,3},{8,6},{9,7},{10,4},{11,5},{12,14},{13,15},{16,130},{17... | collective-permute-start | bytes 98312 | tf_op jit(solution)/shard_map/ppermute | solution.py:46
  41.6 1.3 collective-permute-start.7
  43.1 0.1 copy.14
  43.2 27.0 %collective-permute-done.7 = bf16[128,128]{0,1:T(8,128)(2,1)S(1)} collective-permute-done((bf16[128,128]{0,1:T(8,128)(2,1)S(1)}, bf16[128,128]{0,1:T(8,128)(2,1)S(1)}, u32[]{:S(2)}, u32[]{:S(2)}) %collective-permute-start.7) | collective-permute-done | bytes 32800 | tf_op jit(solution)/shard_map/ppermute | solution.py:46
  70.2 0.0 collective-permute-done.8
  70.4 0.1 constant_dynamic-update-slice_fusion.21
  70.5 24.7 %collective-permute-start.12 = (bf16[128,512]{1,0:T(8,128)(2,1)S(1)}, bf16[128,512]{1,0:T(8,128)(2,1)S(1)}, u32[]{:S(2)}, u32[]{:S(2)}) collective-permute-start(bf16[128,512]{1,0:T(8,128)(2,1)S(1)} %get-tuple-element.6), channel_id=1, source_target_pairs={{0,768},{128,896},{256,0},{384,128},{512,256},{640,384},{768,512},... | collective-permute-start | bytes 393224 | tf_op jit(solution)/shard_map/ppermute | solution.py:62
  95.2 2.5 collective-permute-start.11
  97.7 0.9 constant_dynamic-slice_fusion.5
  98.6 3.4 %collective-permute-start.6 = (bf16[128,1024]{0,1:T(8,128)(2,1)S(1)}, bf16[128,1024]{0,1:T(8,128)(2,1)S(1)}, u32[]{:S(2)}, u32[]{:S(2)}) collective-permute-start(bf16[128,1024]{0,1:T(8,128)(2,1)S(1)} %get-tuple-element.9), channel_id=1, source_target_pairs={{0,128},{128,256},{256,384},{384,512},{512,640},{640,768},{768,896... | collective-permute-start | bytes 786440 | tf_op jit(solution)/shard_map/ppermute | solution.py:60
  102.0 3.4 %collective-permute-start.5 = (bf16[128,1024]{0,1:T(8,128)(2,1)S(1)}, bf16[128,1024]{0,1:T(8,128)(2,1)S(1)}, u32[]{:S(2)}, u32[]{:S(2)}) collective-permute-start(bf16[128,1024]{0,1:T(8,128)(2,1)S(1)} %get-tuple-element.10), channel_id=1, source_target_pairs={{0,256},{128,384},{256,512},{384,640},{512,768},{640,896},{1,257},... | collective-permute-start | bytes 786440 | tf_op jit(solution)/shard_map/ppermute | solution.py:60
  105.4 1.3 collective-permute-start
  106.7 1.9 collective-permute-start.13
  108.7 5.7 %collective-permute-start.14 = (bf16[128,512]{1,0:T(8,128)(2,1)S(1)}, bf16[128,512]{1,0:T(8,128)(2,1)S(1)}, u32[]{:S(2)}, u32[]{:S(2)}) collective-permute-start(bf16[128,512]{1,0:T(8,128)(2,1)S(1)} %get-tuple-element.6), channel_id=1, source_target_pairs={{0,512},{128,640},{256,768},{384,896},{512,0},{640,128},{768,256},... | collective-permute-start | bytes 393224 | tf_op jit(solution)/shard_map/ppermute | solution.py:62
  114.4 12.3 %collective-permute-done.13 = bf16[128,512]{1,0:T(8,128)(2,1)S(1)} collective-permute-done((bf16[128,512]{1,0:T(8,128)(2,1)S(1)}, bf16[128,512]{1,0:T(8,128)(2,1)S(1)}, u32[]{:S(2)}, u32[]{:S(2)}) %collective-permute-start.13) | collective-permute-done | bytes 131104 | tf_op jit(solution)/shard_map/ppermute | solution.py:62
  126.6 1.9 collective-permute-start.15
  128.6 8.8 %collective-permute-start.16 = (bf16[128,512]{1,0:T(8,128)(2,1)S(1)}, bf16[128,512]{1,0:T(8,128)(2,1)S(1)}, u32[]{:S(2)}, u32[]{:S(2)}) collective-permute-start(bf16[128,512]{1,0:T(8,128)(2,1)S(1)} %get-tuple-element.6), channel_id=1, source_target_pairs={{0,256},{128,384},{256,512},{384,640},{512,768},{640,896},{768,0},... | collective-permute-start | bytes 393224 | tf_op jit(solution)/shard_map/ppermute | solution.py:62
  137.5 3.5 %collective-permute-done.15 = bf16[128,512]{1,0:T(8,128)(2,1)S(1)} collective-permute-done((bf16[128,512]{1,0:T(8,128)(2,1)S(1)}, bf16[128,512]{1,0:T(8,128)(2,1)S(1)}, u32[]{:S(2)}, u32[]{:S(2)}) %collective-permute-start.15) | collective-permute-done | bytes 131104 | tf_op jit(solution)/shard_map/ppermute | solution.py:62
  140.9 1.9 collective-permute-start.17
  142.9 2.1 collective-permute-done.16
  144.9 1.5 collective-permute-start.1
  146.4 2.9 %collective-permute-done.17 = bf16[128,512]{1,0:T(8,128)(2,1)S(1)} collective-permute-done((bf16[128,512]{1,0:T(8,128)(2,1)S(1)}, bf16[128,512]{1,0:T(8,128)(2,1)S(1)}, u32[]{:S(2)}, u32[]{:S(2)}) %collective-permute-start.17) | collective-permute-done | bytes 131104 | tf_op jit(solution)/shard_map/ppermute | solution.py:62
  149.3 5.7 %collective-permute-start.2 = (bf16[128,1024]{0,1:T(8,128)(2,1)S(1)}, bf16[128,1024]{0,1:T(8,128)(2,1)S(1)}, u32[]{:S(2)}, u32[]{:S(2)}) collective-permute-start(bf16[128,1024]{0,1:T(8,128)(2,1)S(1)} %get-tuple-element.13), channel_id=1, source_target_pairs={{0,640},{128,768},{256,896},{1,641},{129,769},{257,897},{2,642},{1... | collective-permute-start | bytes 786440 | tf_op jit(solution)/shard_map/ppermute | solution.py:60
  155.0 1.3 collective-permute-start.3
  156.3 0.8 constant_dynamic-update-slice_fusion.6
  157.1 22.7 %collective-permute-done.1 = bf16[128,1024]{0,1:T(8,128)(2,1)S(1)} collective-permute-done((bf16[128,1024]{0,1:T(8,128)(2,1)S(1)}, bf16[128,1024]{0,1:T(8,128)(2,1)S(1)}, u32[]{:S(2)}, u32[]{:S(2)}) %collective-permute-start.1) | collective-permute-done | bytes 262176 | tf_op jit(solution)/shard_map/ppermute | solution.py:60
  179.8 1.5 collective-permute-start.4
  181.3 0.8 constant_dynamic-update-slice_fusion.5
  182.0 1.9 collective-permute-done.2
  183.9 0.8 constant_dynamic-update-slice_fusion.4
  184.7 0.7 constant_dynamic-update-slice_fusion.3
  185.5 0.8 constant_dynamic-update-slice_fusion.2
  186.2 0.8 constant_dynamic-update-slice_fusion.1
  187.0 0.7 constant_dynamic-update-slice_fusion
  187.7 3.2 %copy.13 = bf16[8,128,8,128]{3,2,1,0:T(8,128)(2,1)S(1)} copy(bf16[8,128,8,128]{1,3,2,0:T(8,128)(2,1)} %all-to-all-done) | data formatting | bytes 4194304 | tf_op jit(solution)/shard_map/all_to_all | solution.py:68
  190.9 1.2 fusion.5
  192.2 2.9 %convolution_add_fusion = f32[1024,512]{1,0:T(8,128)S(1)} fusion(f32[1024,512]{1,0:T(8,128)S(1)} %fusion.5, bf16[1024,1024]{0,1:T(8,128)(2,1)} %constant_dynamic-update-slice_fusion, bf16[1024,512]{1,0:T(8,128)(2,1)S(1)} %constant_dynamic-update-slice_fusion.14), kind=kOutput, calls=%fused_computation.12 | convolution fusion | flops 1074266112 | bytes 7340032 | tf_op jit(solution)/shard_map/dot_general | solution.py:71
  195.1 57.8 %all_to_all.10 = f32[8,128,512]{2,1,0:T(8,128)S(1)} all-to-all(f32[8,128,512]{2,1,0:T(8,128)S(1)} %bitcast.20), channel_id=1, replica_groups=mesh['row'=8,'col'=16,'layer'=8] {'layer'}, dimensions={0} | all-to-all | bytes 4194304 | tf_op jit(solution)/shard_map/all_to_all | solution.py:74
  252.8 0.9 reduce_sum.9
  (29 shorter events, 0.2 us)
Async XLA Ops:
  20.0 167.8 %all-to-all-start = ((bf16[8,128,8,128]{1,3,2,0:T(8,128)(2,1)}), bf16[8,128,8,128]{1,3,2,0:T(8,128)(2,1)}, u32[]{:S(2)}, u32[]{:S(2)}) async-start(bf16[8,128,8,128]{1,3,2,0:T(8,128)(2,1)} %copy.12), calls=%async_computation | async-start | bytes 4194304 | tf_op jit(solution)/shard_map/all_to_all | solution.py:68
  26.7 43.6 %collective-permute-start.10 = (bf16[128,128]{0,1:T(8,128)(2,1)S(1)}, bf16[128,128]{0,1:T(8,128)(2,1)S(1)}, u32[]{:S(2)}, u32[]{:S(2)}) collective-permute-start(bf16[128,128]{0,1:T(8,128)(2,1)S(1)} %get-tuple-element.17), channel_id=1, source_target_pairs={{0,0},{1,1},{2,2},{3,3},{8,4},{9,5},{10,6},{11,7},{12,12},{13,13},... | collective-permute-start | bytes 98312 | tf_op jit(solution)/shard_map/ppermute | solution.py:46
  36.7 33.6 %collective-permute-start.9 = (bf16[128,128]{0,1:T(8,128)(2,1)S(1)}, bf16[128,128]{0,1:T(8,128)(2,1)S(1)}, u32[]{:S(2)}, u32[]{:S(2)}) collective-permute-start(bf16[128,128]{0,1:T(8,128)(2,1)S(1)} %get-tuple-element.18), channel_id=1, source_target_pairs={{0,1},{1,2},{2,3},{8,5},{9,6},{10,7},{11,4},{12,13},{13,14},{14,15... | collective-permute-start | bytes 98312 | tf_op jit(solution)/shard_map/ppermute | solution.py:46
  38.1 32.1 %collective-permute-start.8 = (bf16[128,128]{0,1:T(8,128)(2,1)S(1)}, bf16[128,128]{0,1:T(8,128)(2,1)S(1)}, u32[]{:S(2)}, u32[]{:S(2)}) collective-permute-start(bf16[128,128]{0,1:T(8,128)(2,1)S(1)} %get-tuple-element.19), channel_id=1, source_target_pairs={{0,2},{1,3},{8,6},{9,7},{10,4},{11,5},{12,14},{13,15},{16,130},{17... | collective-permute-start | bytes 98312 | tf_op jit(solution)/shard_map/ppermute | solution.py:46
  41.6 28.6 %collective-permute-start.7 = (bf16[128,128]{0,1:T(8,128)(2,1)S(1)}, bf16[128,128]{0,1:T(8,128)(2,1)S(1)}, u32[]{:S(2)}, u32[]{:S(2)}) collective-permute-start(bf16[128,128]{0,1:T(8,128)(2,1)S(1)} %get-tuple-element.20), channel_id=1, source_target_pairs={{0,3},{8,7},{9,4},{10,5},{11,6},{12,15},{16,131},{17,128},{18,129}... | collective-permute-start | bytes 98312 | tf_op jit(solution)/shard_map/ppermute | solution.py:46
  70.5 38.2 %collective-permute-start.12 = (bf16[128,512]{1,0:T(8,128)(2,1)S(1)}, bf16[128,512]{1,0:T(8,128)(2,1)S(1)}, u32[]{:S(2)}, u32[]{:S(2)}) collective-permute-start(bf16[128,512]{1,0:T(8,128)(2,1)S(1)} %get-tuple-element.6), channel_id=1, source_target_pairs={{0,768},{128,896},{256,0},{384,128},{512,256},{640,384},{768,512},... | collective-permute-start | bytes 393224 | tf_op jit(solution)/shard_map/ppermute | solution.py:62
  95.2 11.5 %collective-permute-start.11 = (bf16[128,512]{1,0:T(8,128)(2,1)S(1)}, bf16[128,512]{1,0:T(8,128)(2,1)S(1)}, u32[]{:S(2)}, u32[]{:S(2)}) collective-permute-start(bf16[128,512]{1,0:T(8,128)(2,1)S(1)} %get-tuple-element.6), channel_id=1, source_target_pairs={{0,896},{128,0},{256,128},{384,256},{512,384},{640,512},{768,640},... | collective-permute-start | bytes 393224 | tf_op jit(solution)/shard_map/ppermute | solution.py:62
  98.6 88.4 %collective-permute-start.6 = (bf16[128,1024]{0,1:T(8,128)(2,1)S(1)}, bf16[128,1024]{0,1:T(8,128)(2,1)S(1)}, u32[]{:S(2)}, u32[]{:S(2)}) collective-permute-start(bf16[128,1024]{0,1:T(8,128)(2,1)S(1)} %get-tuple-element.9), channel_id=1, source_target_pairs={{0,128},{128,256},{256,384},{384,512},{512,640},{640,768},{768,896... | collective-permute-start | bytes 786440 | tf_op jit(solution)/shard_map/ppermute | solution.py:60
  102.0 84.2 %collective-permute-start.5 = (bf16[128,1024]{0,1:T(8,128)(2,1)S(1)}, bf16[128,1024]{0,1:T(8,128)(2,1)S(1)}, u32[]{:S(2)}, u32[]{:S(2)}) collective-permute-start(bf16[128,1024]{0,1:T(8,128)(2,1)S(1)} %get-tuple-element.10), channel_id=1, source_target_pairs={{0,256},{128,384},{256,512},{384,640},{512,768},{640,896},{1,257},... | collective-permute-start | bytes 786440 | tf_op jit(solution)/shard_map/ppermute | solution.py:60
  105.4 49.6 %collective-permute-start = (bf16[128,1024]{0,1:T(8,128)(2,1)S(1)}, bf16[128,1024]{0,1:T(8,128)(2,1)S(1)}, u32[]{:S(2)}, u32[]{:S(2)}) collective-permute-start(bf16[128,1024]{0,1:T(8,128)(2,1)S(1)} %get-tuple-element.15), channel_id=1, source_target_pairs={{0,896},{1,897},{2,898},{3,899},{4,900},{5,901},{6,902},{7,903},{8... | collective-permute-start | bytes 786440 | tf_op jit(solution)/shard_map/ppermute | solution.py:60
  106.7 19.9 %collective-permute-start.13 = (bf16[128,512]{1,0:T(8,128)(2,1)S(1)}, bf16[128,512]{1,0:T(8,128)(2,1)S(1)}, u32[]{:S(2)}, u32[]{:S(2)}) collective-permute-start(bf16[128,512]{1,0:T(8,128)(2,1)S(1)} %get-tuple-element.6), channel_id=1, source_target_pairs={{0,640},{128,768},{256,896},{384,0},{512,128},{640,256},{768,384},... | collective-permute-start | bytes 393224 | tf_op jit(solution)/shard_map/ppermute | solution.py:62
  108.7 19.9 %collective-permute-start.14 = (bf16[128,512]{1,0:T(8,128)(2,1)S(1)}, bf16[128,512]{1,0:T(8,128)(2,1)S(1)}, u32[]{:S(2)}, u32[]{:S(2)}) collective-permute-start(bf16[128,512]{1,0:T(8,128)(2,1)S(1)} %get-tuple-element.6), channel_id=1, source_target_pairs={{0,512},{128,640},{256,768},{384,896},{512,0},{640,128},{768,256},... | collective-permute-start | bytes 393224 | tf_op jit(solution)/shard_map/ppermute | solution.py:62
  126.6 14.3 %collective-permute-start.15 = (bf16[128,512]{1,0:T(8,128)(2,1)S(1)}, bf16[128,512]{1,0:T(8,128)(2,1)S(1)}, u32[]{:S(2)}, u32[]{:S(2)}) collective-permute-start(bf16[128,512]{1,0:T(8,128)(2,1)S(1)} %get-tuple-element.6), channel_id=1, source_target_pairs={{0,384},{128,512},{256,640},{384,768},{512,896},{640,0},{768,128},... | collective-permute-start | bytes 393224 | tf_op jit(solution)/shard_map/ppermute | solution.py:62
  128.6 16.3 %collective-permute-start.16 = (bf16[128,512]{1,0:T(8,128)(2,1)S(1)}, bf16[128,512]{1,0:T(8,128)(2,1)S(1)}, u32[]{:S(2)}, u32[]{:S(2)}) collective-permute-start(bf16[128,512]{1,0:T(8,128)(2,1)S(1)} %get-tuple-element.6), channel_id=1, source_target_pairs={{0,256},{128,384},{256,512},{384,640},{512,768},{640,896},{768,0},... | collective-permute-start | bytes 393224 | tf_op jit(solution)/shard_map/ppermute | solution.py:62
  140.9 8.4 %collective-permute-start.17 = (bf16[128,512]{1,0:T(8,128)(2,1)S(1)}, bf16[128,512]{1,0:T(8,128)(2,1)S(1)}, u32[]{:S(2)}, u32[]{:S(2)}) collective-permute-start(bf16[128,512]{1,0:T(8,128)(2,1)S(1)} %get-tuple-element.6), channel_id=1, source_target_pairs={{0,128},{128,256},{256,384},{384,512},{512,640},{640,768},{768,896... | collective-permute-start | bytes 393224 | tf_op jit(solution)/shard_map/ppermute | solution.py:62
  144.9 34.9 %collective-permute-start.1 = (bf16[128,1024]{0,1:T(8,128)(2,1)S(1)}, bf16[128,1024]{0,1:T(8,128)(2,1)S(1)}, u32[]{:S(2)}, u32[]{:S(2)}) collective-permute-start(bf16[128,1024]{0,1:T(8,128)(2,1)S(1)} %get-tuple-element.14), channel_id=1, source_target_pairs={{0,768},{128,896},{1,769},{129,897},{2,770},{130,898},{3,771},{131... | collective-permute-start | bytes 786440 | tf_op jit(solution)/shard_map/ppermute | solution.py:60
  149.3 34.7 %collective-permute-start.2 = (bf16[128,1024]{0,1:T(8,128)(2,1)S(1)}, bf16[128,1024]{0,1:T(8,128)(2,1)S(1)}, u32[]{:S(2)}, u32[]{:S(2)}) collective-permute-start(bf16[128,1024]{0,1:T(8,128)(2,1)S(1)} %get-tuple-element.13), channel_id=1, source_target_pairs={{0,640},{128,768},{256,896},{1,641},{129,769},{257,897},{2,642},{1... | collective-permute-start | bytes 786440 | tf_op jit(solution)/shard_map/ppermute | solution.py:60
  155.0 29.7 %collective-permute-start.3 = (bf16[128,1024]{0,1:T(8,128)(2,1)S(1)}, bf16[128,1024]{0,1:T(8,128)(2,1)S(1)}, u32[]{:S(2)}, u32[]{:S(2)}) collective-permute-start(bf16[128,1024]{0,1:T(8,128)(2,1)S(1)} %get-tuple-element.12), channel_id=1, source_target_pairs={{0,512},{128,640},{256,768},{384,896},{1,513},{129,641},{257,769},... | collective-permute-start | bytes 786440 | tf_op jit(solution)/shard_map/ppermute | solution.py:60
  179.8 5.7 %collective-permute-start.4 = (bf16[128,1024]{0,1:T(8,128)(2,1)S(1)}, bf16[128,1024]{0,1:T(8,128)(2,1)S(1)}, u32[]{:S(2)}, u32[]{:S(2)}) collective-permute-start(bf16[128,1024]{0,1:T(8,128)(2,1)S(1)} %get-tuple-element.11), channel_id=1, source_target_pairs={{0,384},{128,512},{256,640},{384,768},{512,896},{1,385},{129,513},... | collective-permute-start | bytes 786440 | tf_op jit(solution)/shard_map/ppermute | solution.py:60

commit v2 on v0

v2 whole, which is shorter than its diff:
```python
import jax
import jax.numpy as jnp
from jax import lax
from jax.sharding import Mesh, PartitionSpec as P

B = 128
AXES = ("z", "y", "w", "u", "v", "core")


def body(stored, pattern):
    nz, ny, nw, nu, nv, ncore = (lax.axis_size(a) for a in AXES)
    z, y, w, u, v, core = (lax.axis_index(a) for a in AXES)
    four = nv * ncore
    wide = four * B
    i = v * ncore + core
    ra = z * nu + u
    c = y * nw + w
    g = ra * four + i

    band = nw * wide
    raw = lax.dynamic_slice(stored, (0, y * band), (B, band))
    present = lax.dynamic_slice(pattern, (g, y * nw * four), (1, nw * four))
    present = jnp.repeat(present, B, axis=1) > 0
    row = g * B + jnp.arange(B, dtype=jnp.int32)[:, None]
    column = y * band + jnp.arange(band, dtype=jnp.int32)[None, :]
    upper = jnp.where(present & (column >= row), raw, jnp.zeros((), raw.dtype))
    tile = lax.dynamic_slice(upper, (0, w * wide), (B, wide))

    def flat(zz, uu, yy, ww, ii):
        return (((zz * ny + yy) * nw + ww) * nu + uu) * four + ii

    everywhere = [
        (zz, uu, yy, ww, ii)
        for zz in range(nz)
        for uu in range(nu)
        for yy in range(ny)
        for ww in range(nw)
        for ii in range(four)
    ]

    blocks = tile.reshape(B, four, B).transpose(1, 0, 2)
    crossed = lax.all_to_all(blocks, ("v", "core"), split_axis=0, concat_axis=0, tiled=True)
    crossed = crossed.reshape(wide, B).T
    mirrored = lax.ppermute(
        tile,
        AXES,
        [(flat(*d), flat(d[2], d[3], d[0], d[1], d[4])) for d in everywhere if d[0] * nu + d[1] <= d[2] * nw + d[3]],
    )
    k_row = (c * four + i) * B + jnp.arange(B, dtype=jnp.int32)[:, None]
    i_column = ra * wide + jnp.arange(wide, dtype=jnp.int32)[None, :]
    left = jnp.where(k_row <= i_column, mirrored, crossed)

    received = []
    for s in range(four):
        j = (i + s) % four
        pair = jnp.concatenate(
            [lax.dynamic_slice(upper, (0, (h * four + j) * B), (B, B)) for h in range(nw)], axis=1
        )
        received.append(
            lax.ppermute(
                pair,
                AXES,
                [
                    (flat(*d), flat(d[2], d[3], d[0], d[1], (d[4] + s) % four))
                    for d in everywhere
                    if d[0] * nu + d[1] <= d[2] * nw + nw - 1
                ],
            )
        )
    backward = received[::-1]
    ring = jnp.stack(backward + backward[:-1])
    ring = lax.dynamic_slice(ring, ((four - 1 - i) % four, 0, 0), (four, B, nu * B))
    turned = ring.reshape(wide, nu * B).T
    other = lax.ppermute(tile, "u", [(a, nu - 1 - a) for a in range(nu)])
    first = u == 0
    direct = jnp.concatenate([jnp.where(first, tile, other), jnp.where(first, other, tile)], axis=0)
    half = jnp.arange(nu, dtype=jnp.int32)[:, None]
    r_row = ((z * nu + half) * four + i) * B + jnp.arange(B, dtype=jnp.int32)[None, :]
    r_row = r_row.reshape(nu * B, 1)
    j_column = c * wide + jnp.arange(wide, dtype=jnp.int32)[None, :]
    right = jnp.where(r_row <= j_column, direct, turned)

    right = lax.all_gather(right, "z", axis=0, tiled=True)
    left = jnp.broadcast_to(left[None], (ny * nw, B, wide))
    left = lax.all_to_all(left, ("y", "w"), split_axis=0, concat_axis=0, tiled=True)
    left = left.reshape(ny * nw * B, wide)

    partial = lax.dot_general(left, right, (((0,), (0,)), ((), ())), preferred_element_type=jnp.float32)
    partial = partial.reshape(nv, ncore, B, wide)
    partial = jnp.sum(lax.all_to_all(partial, "core", split_axis=1, concat_axis=1, tiled=True), axis=1)
    partial = jnp.sum(lax.all_to_all(partial, "v", split_axis=0, concat_axis=0, tiled=True), axis=0)
    return partial.astype(jnp.bfloat16)


def solution(mesh):
    finer = Mesh(mesh.devices.reshape(8, 8, 2, 2, 2, 2), AXES)
    return jax.shard_map(
        body,
        mesh=finer,
        in_specs=(P(("z", "u", "v", "core"), None), P()),
        out_specs=P(("z", "u", "v", "core"), ("y", "w")),
        check_vma=False,
    )
```

time: 227 us -> 174 us (0.77); the launches traced: 223 us -> 173 us
  waiting for transfers between devices: 159 us -> 51.6 us
  starting transfers between devices: 28.2 us -> 67.8 us
  blocking collectives: 0 us -> 24.6 us
  local copies, waits for them, and re-layouts: 12.1 us -> 8.49 us
    reduce_scatter x1 -> x0, waiting for transfers between devices: 48.1 us -> none  [body(): summed = lax.psum_scatter(running, 'row', scatter_dimension=0, tiled=True)]
    all_gather x1, waiting for transfers between devices: 40 us -> 0.02 us  [body(): right = lax.all_gather(right, 'z', axis=0, tiled=True)]
    all_to_all x0 -> x2, blocking collectives: none -> 24.6 us  [the longest x1 17.1 us: body(): lax.all_to_all(partial, 'v', split_axis=0, concat_axis=0, tiled=True)]
    all_to_all x2, waiting for transfers between devices: 71.2 us -> 47.6 us  [the longest x1 47.6 us: body(): lax.all_to_all(left, ('y', 'w'), split_axis=0, concat_axis=0, tiled=True)]
    all_to_all x2, starting transfers between devices: 28.1 us -> 49 us  [the longest x1 38.2 us: body(): lax.all_to_all(left, ('y', 'w'), split_axis=0, concat_axis=0, tiled=True)]
    ppermute x0 -> x6, starting transfers between devices: none -> 18.7 us  [the longest x4 9.45 us: body(): lax.ppermute(pair, AXES, [(flat(*d), flat(d[2], d[3], d[0], d[1], (d[4] +...]
    ppermute x0 -> x6, waiting for transfers between devices: none -> 3.97 us  [the longest x4 3.97 us: body(): lax.ppermute(pair, AXES, [(flat(*d), flat(d[2], d[3], d[0], d[1], (d[4] +...]
    unnamed x4 -> x6, local copies, waits for them, and re-layouts: 3.82 us -> 0.04 us
  transfers between devices with their start and end apart: 4 -> 9, of which waited for: 4 -> 2; matrix products, arithmetic and copies ran while one was open for 0% -> 6% of each run, Pallas kernels for 0% -> 0%
where the time goes in v2:
time: 174 us; the launch traced here: 173 us
  starting transfers between devices  67.8 us (39%)
  waiting for transfers between devices  51.6 us (30%)
  blocking collectives  24.6 us (14%)
  between operations  13.7 us (8%)
  local copies, waits for them, and re-layouts  8.49 us (5%)
  other arithmetic  3.85 us (2%)
  matrix products  2.83 us (2%)
    all_to_all x1, waiting for transfers between devices, body(): lax.all_to_all(left, ('y', 'w'), split_axis=0, concat_axis=0, tiled=True)  47.6 us
    all_to_all x1, starting transfers between devices, body(): lax.all_to_all(left, ('y', 'w'), split_axis=0, concat_axis=0, tiled=True)  38.2 us
    all_to_all x1, blocking collectives, body(): lax.all_to_all(partial, 'v', split_axis=0, concat_axis=0, tiled=True)  17.1 us
    all_to_all x1, starting transfers between devices, body(): lax.all_to_all(blocks, ('v', 'core'), split_axis=0, concat_axis=0, tiled=...  10.8 us
    ppermute x4, starting transfers between devices, body(): lax.ppermute(pair, AXES, [(flat(*d), flat(d[2], d[3], d[0], d[1], (d[4] +...  9.45 us
    ppermute x1, starting transfers between devices, body(): other = lax.ppermute(tile, 'u', [(a, nu - 1 - a) for a in range(nu)])  8.56 us
    all_to_all x1, blocking collectives, body(): lax.all_to_all(partial, 'core', split_axis=1, concat_axis=1, tiled=True)  7.55 us
    ppermute x4, waiting for transfers between devices, body(): lax.ppermute(pair, AXES, [(flat(*d), flat(d[2], d[3], d[0], d[1], (d[4] +...  3.97 us
  transfers between devices with their start and end apart: 9, of which 2 were waited for; matrix products, arithmetic and copies ran while one was open for 6% of the time, Pallas kernels for 0%

profile of v2, /device:TPU:1, one launch (start us, length us, event | category | flops | bytes accessed | tf_op | source)
XLA Modules:
  0.0 172.9 jit_solution(13014851624428149513)
XLA Ops:
  6.5 0.8 compare_bitcast_fusion
  7.3 0.1 broadcast_bitcast_fusion
  7.4 1.1 and_select_fusion
  8.5 0.7 collective-permute-start
  9.2 8.6 %collective-permute-start.1 = (bf16[128,512]{1,0:T(8,128)(2,1)S(1)}, bf16[128,512]{1,0:T(8,128)(2,1)S(1)}, u32[]{:S(2)}, u32[]{:S(2)}) collective-permute-start(bf16[128,512]{1,0:T(8,128)(2,1)S(1)} %constant_dynamic-slice_fusion.9), channel_id=1, source_target_pairs={{0,4},{4,0},{1,5},{5,1},{2,6},{6,2},{3,7},{7,3},{8,12},{12,8},{9,1... | collective-permute-start | bytes 393224 | tf_op jit(solution)/shard_map/ppermute | solution.py:74
  17.8 0.8 copy.21
  18.6 10.8 %all-to-all-start = ((bf16[4,128,128]{1,2,0:T(8,128)(2,1)}), bf16[4,128,128]{1,2,0:T(8,128)(2,1)S(1)}, u32[]{:S(2)}, u32[]{:S(2)}) async-start(bf16[4,128,128]{1,2,0:T(8,128)(2,1)} %bitcast.3), calls=%async_computation | async-start | bytes 262144 | tf_op jit(solution)/shard_map/all_to_all | solution.py:42
  29.4 0.1 constant_dynamic-slice_fusion.2
  29.4 4.4 %collective-permute-start.4 = (bf16[128,256]{1,0:T(8,128)(2,1)S(1)}, bf16[128,256]{1,0:T(8,128)(2,1)S(1)}, u32[]{:S(2)}, u32[]{:S(2)}) collective-permute-start(bf16[128,256]{1,0:T(8,128)(2,1)S(1)} %pad_maximum_fusion.2), channel_id=1, source_target_pairs={{0,1},{1,2},{2,3},{3,0},{8,5},{9,6},{10,7},{11,4},{16,129},{17,130... | collective-permute-start | bytes 196616 | tf_op jit(solution)/shard_map/ppermute | solution.py:60
  33.9 1.9 %collective-permute-start.3 = (bf16[128,256]{1,0:T(8,128)(2,1)S(1)}, bf16[128,256]{1,0:T(8,128)(2,1)S(1)}, u32[]{:S(2)}, u32[]{:S(2)}) collective-permute-start(bf16[128,256]{1,0:T(8,128)(2,1)S(1)} %pad_maximum_fusion.1), channel_id=1, source_target_pairs={{0,2},{1,3},{2,0},{3,1},{8,6},{9,7},{10,4},{11,5},{16,130},{17,131... | collective-permute-start | bytes 196616 | tf_op jit(solution)/shard_map/ppermute | solution.py:60
  35.9 2.4 %collective-permute-start.2 = (bf16[128,256]{1,0:T(8,128)(2,1)S(1)}, bf16[128,256]{1,0:T(8,128)(2,1)S(1)}, u32[]{:S(2)}, u32[]{:S(2)}) collective-permute-start(bf16[128,256]{1,0:T(8,128)(2,1)S(1)} %pad_maximum_fusion), channel_id=1, source_target_pairs={{0,3},{1,0},{2,1},{3,2},{8,7},{9,4},{10,5},{11,6},{16,131},{17,128... | collective-permute-start | bytes 196616 | tf_op jit(solution)/shard_map/ppermute | solution.py:60
  38.4 0.1 add_bitcast_fusion
  38.5 4.0 %collective-permute-done.2 = bf16[128,256]{1,0:T(8,128)(2,1)S(1)} collective-permute-done((bf16[128,256]{1,0:T(8,128)(2,1)S(1)}, bf16[128,256]{1,0:T(8,128)(2,1)S(1)}, u32[]{:S(2)}, u32[]{:S(2)}) %collective-permute-start.2) | collective-permute-done | bytes 65568 | tf_op jit(solution)/shard_map/ppermute | solution.py:60
  42.4 0.7 collective-permute-start.5
  43.1 0.0 collective-permute-done.3
  43.1 0.0 collective-permute-done.4
  43.2 0.0 collective-permute-done.5
  43.3 0.1 copy.30
  43.4 0.0 collective-permute-done
  43.4 0.0 all-to-all-done
  43.4 0.1 compare_select_fusion.1
  43.6 0.1 copy.23
  43.7 1.7 broadcast_in_dim.10
  45.4 38.2 %all-to-all-start.1 = ((bf16[16,128,512]{1,2,0:T(8,128)(2,1)}), bf16[16,128,512]{1,2,0:T(8,128)(2,1)S(1)}, u32[]{:S(2)}, u32[]{:S(2)}) async-start(bf16[16,128,512]{1,2,0:T(8,128)(2,1)} %broadcast_in_dim.10), calls=%async_computation.1 | async-start | bytes 4194304 | tf_op jit(solution)/shard_map/all_to_all | solution.py:85
  83.7 0.0 all-gather.2.cloned.1.call-start
  83.7 0.0 collective-permute-done.1
  83.7 0.1 broadcast_select_fusion.1
  83.8 0.8 compare_select_fusion
  84.6 0.0 all-gather.2.cloned.1.call-update
  84.7 47.6 %all-to-all-done.1 = bf16[16,128,512]{1,2,0:T(8,128)(2,1)S(1)} async-done(((bf16[16,128,512]{1,2,0:T(8,128)(2,1)}), bf16[16,128,512]{1,2,0:T(8,128)(2,1)S(1)}, u32[]{:S(2)}, u32[]{:S(2)}) %all-to-all-start.1) | async-done | bytes 2097184 | tf_op jit(solution)/shard_map/all_to_all | solution.py:85
  132.3 2.6 %copy.24 = bf16[16,128,512]{2,1,0:T(8,128)(2,1)} copy(bf16[16,128,512]{1,2,0:T(8,128)(2,1)S(1)} %all-to-all-done.1) | data formatting | bytes 4194304 | tf_op jit(solution)/shard_map/all_to_all | solution.py:85
  134.8 2.9 %copy.25 = bf16[512,2048]{1,0:T(8,128)(2,1)S(1)} copy(bf16[512,2048]{0,1:T(8,128)(2,1)} %bitcast.41) | data formatting | bytes 4194304 | tf_op jit(solution)/shard_map/dot_general | solution.py:88
  137.8 0.0 all-gather.2.cloned.1.call-done
  137.8 2.8 %fusion = f32[2,2,128,512]{3,2,0,1:T(8,128)S(1)} fusion(bf16[2048,512]{1,0:T(8,128)(2,1)} %all-gather.2.cloned.1.call-done, bf16[2,2,128,2048]{3,2,1,0:T(8,128)(2,1)S(1)} %bitcast.42), kind=kOutput, calls=%fused_computation | convolution fusion | flops 1073741824 | bytes 5242880 | tf_op jit(solution)/shard_map/dot_general | solution.py:88
  140.6 7.6 %all_to_all.20 = f32[2,2,128,512]{3,2,0,1:T(8,128)S(1)} all-to-all(f32[2,2,128,512]{3,2,0,1:T(8,128)S(1)} %fusion), channel_id=1, replica_groups=mesh['z'=8,'y'=8,'w'=2,'u'=2,'v'=2,'core'=2] {'core'}, dimensions={1} | all-to-all | bytes 2097152 | tf_op jit(solution)/shard_map/all_to_all | solution.py:90
  148.2 0.1 reduce_sum.18
  148.3 17.1 %all_to_all.21 = f32[2,128,512]{2,1,0:T(8,128)S(1)} all-to-all(f32[2,128,512]{2,1,0:T(8,128)S(1)} %reduce_sum.18), channel_id=1, replica_groups=mesh['z'=8,'y'=8,'w'=2,'u'=2,'v'=2,'core'=2] {'v'}, dimensions={0} | all-to-all | bytes 1048576 | tf_op jit(solution)/shard_map/all_to_all | solution.py:91
  165.3 0.7 reduce_sum.19
  (19 shorter events, 0.2 us)
Async XLA Ops:
  8.5 34.9 %collective-permute-start = (bf16[128,512]{1,0:T(8,128)(2,1)S(1)}, bf16[128,512]{1,0:T(8,128)(2,1)S(1)}, u32[]{:S(2)}, u32[]{:S(2)}) collective-permute-start(bf16[128,512]{1,0:T(8,128)(2,1)S(1)} %constant_dynamic-slice_fusion.9), channel_id=1, source_target_pairs={{0,0},{1,1},{2,2},{3,3},{8,4},{9,5},{10,6},{11,7},{16,128},{17,129... | collective-permute-start | bytes 393224 | tf_op jit(solution)/shard_map/ppermute | solution.py:44
  9.2 74.5 %collective-permute-start.1 = (bf16[128,512]{1,0:T(8,128)(2,1)S(1)}, bf16[128,512]{1,0:T(8,128)(2,1)S(1)}, u32[]{:S(2)}, u32[]{:S(2)}) collective-permute-start(bf16[128,512]{1,0:T(8,128)(2,1)S(1)} %constant_dynamic-slice_fusion.9), channel_id=1, source_target_pairs={{0,4},{4,0},{1,5},{5,1},{2,6},{6,2},{3,7},{7,3},{8,12},{12,8},{9,1... | collective-permute-start | bytes 393224 | tf_op jit(solution)/shard_map/ppermute | solution.py:74
  18.6 24.9 %all-to-all-start = ((bf16[4,128,128]{1,2,0:T(8,128)(2,1)}), bf16[4,128,128]{1,2,0:T(8,128)(2,1)S(1)}, u32[]{:S(2)}, u32[]{:S(2)}) async-start(bf16[4,128,128]{1,2,0:T(8,128)(2,1)} %bitcast.3), calls=%async_computation | async-start | bytes 262144 | tf_op jit(solution)/shard_map/all_to_all | solution.py:42
  29.4 13.7 %collective-permute-start.4 = (bf16[128,256]{1,0:T(8,128)(2,1)S(1)}, bf16[128,256]{1,0:T(8,128)(2,1)S(1)}, u32[]{:S(2)}, u32[]{:S(2)}) collective-permute-start(bf16[128,256]{1,0:T(8,128)(2,1)S(1)} %pad_maximum_fusion.2), channel_id=1, source_target_pairs={{0,1},{1,2},{2,3},{3,0},{8,5},{9,6},{10,7},{11,4},{16,129},{17,130... | collective-permute-start | bytes 196616 | tf_op jit(solution)/shard_map/ppermute | solution.py:60
  33.9 9.2 %collective-permute-start.3 = (bf16[128,256]{1,0:T(8,128)(2,1)S(1)}, bf16[128,256]{1,0:T(8,128)(2,1)S(1)}, u32[]{:S(2)}, u32[]{:S(2)}) collective-permute-start(bf16[128,256]{1,0:T(8,128)(2,1)S(1)} %pad_maximum_fusion.1), channel_id=1, source_target_pairs={{0,2},{1,3},{2,0},{3,1},{8,6},{9,7},{10,4},{11,5},{16,130},{17,131... | collective-permute-start | bytes 196616 | tf_op jit(solution)/shard_map/ppermute | solution.py:60
  35.9 6.6 %collective-permute-start.2 = (bf16[128,256]{1,0:T(8,128)(2,1)S(1)}, bf16[128,256]{1,0:T(8,128)(2,1)S(1)}, u32[]{:S(2)}, u32[]{:S(2)}) collective-permute-start(bf16[128,256]{1,0:T(8,128)(2,1)S(1)} %pad_maximum_fusion), channel_id=1, source_target_pairs={{0,3},{1,0},{2,1},{3,2},{8,7},{9,4},{10,5},{11,6},{16,131},{17,128... | collective-permute-start | bytes 196616 | tf_op jit(solution)/shard_map/ppermute | solution.py:60
  42.4 0.7 collective-permute-start.5
  45.4 86.8 %all-to-all-start.1 = ((bf16[16,128,512]{1,2,0:T(8,128)(2,1)}), bf16[16,128,512]{1,2,0:T(8,128)(2,1)S(1)}, u32[]{:S(2)}, u32[]{:S(2)}) async-start(bf16[16,128,512]{1,2,0:T(8,128)(2,1)} %broadcast_in_dim.10), calls=%async_computation.1 | async-start | bytes 4194304 | tf_op jit(solution)/shard_map/all_to_all | solution.py:85
  83.7 54.1 %all-gather.2.cloned.1.call-start = ((), (), s32[]{:S(2)}) async-start(), calls=%async_computation.4 | async-start | bytes 2359296 | tf_op jit(solution)/shard_map/all_gather | solution.py:83
Sparse Core Ops, SparseCore 0:
  87.2 47.4 all-gather.1

commit v3 on v2

v3 whole, which is shorter than its diff:
```python
import jax
import jax.numpy as jnp
from jax import lax
from jax.experimental import pallas as pl
from jax.experimental.pallas import tpu as pltpu
from jax.sharding import Mesh, PartitionSpec as P

B = 128
AXES = ("z", "y", "w", "u", "v", "core")


def product_kernel(left_ref, right_ref, out_ref):
    pieces = [left_ref[k] for k in range(left_ref.shape[0])]
    out_ref[...] = jnp.dot(jnp.concatenate(pieces, axis=1), right_ref[...], preferred_element_type=jnp.float32)


def product(left, right, swap):
    count, rows, depth = left.shape
    columns = right.shape[1]
    step = B
    return pl.pallas_call(
        product_kernel,
        grid=(rows // step,),
        in_specs=[
            pl.BlockSpec((count, step, depth), lambda m: (0, m, 0)),
            pl.BlockSpec((count * depth, columns), lambda m: (0, 0)),
        ],
        out_specs=pl.BlockSpec((step, columns), lambda m: ((m % swap) * (rows // step // swap) + m // swap, 0)),
        out_shape=jax.ShapeDtypeStruct((rows, columns), jnp.float32),
        compiler_params=pltpu.CompilerParams(vmem_limit_bytes=24 * 1024 * 1024),
        cost_estimate=pl.CostEstimate(
            flops=2 * rows * columns * count * depth,
            bytes_accessed=2 * (left.size + right.size) + 4 * rows * columns,
            transcendentals=0,
        ),
        name="product",
    )(left, right)


def body(stored, pattern):
    nz, ny, nw, nu, nv, ncore = (lax.axis_size(a) for a in AXES)
    z, y, w, u, v, core = (lax.axis_index(a) for a in AXES)
    four = nv * ncore
    wide = four * B
    i = v * ncore + core
    ra = z * nu + u
    c = y * nw + w
    g = ra * four + i

    raw = lax.dynamic_slice(stored, (0, c * wide), (B, wide))
    present = lax.dynamic_slice(pattern, (g, c * four), (1, four))
    present = jnp.repeat(present, B, axis=1) > 0
    row = g * B + jnp.arange(B, dtype=jnp.int32)[:, None]
    column = c * wide + jnp.arange(wide, dtype=jnp.int32)[None, :]
    tile = jnp.where(present & (column >= row), raw, jnp.zeros((), raw.dtype))

    def flat(zz, uu, yy, ww, ii):
        return (((zz * ny + yy) * nw + ww) * nu + uu) * four + ii

    everywhere = [
        (zz, uu, yy, ww, ii)
        for zz in range(nz)
        for uu in range(nu)
        for yy in range(ny)
        for ww in range(nw)
        for ii in range(four)
    ]

    mirrored = lax.ppermute(
        tile,
        AXES,
        [(flat(*d), flat(d[2], d[3], d[0], d[1], d[4])) for d in everywhere if d[0] * nu + d[1] < d[2] * nw + d[3]],
    )
    other = lax.ppermute(tile, "u", [(a, nu - 1 - a) for a in range(nu)])
    own = jnp.where(ra <= c, tile, mirrored)
    blocks = own.reshape(B, four, B).transpose(1, 0, 2)
    blocks = jnp.concatenate([blocks] * nu, axis=0)
    crossed = lax.all_to_all(blocks, ("u", "v", "core"), split_axis=0, concat_axis=0, tiled=True)
    crossed = crossed.reshape(nu, wide, B)

    first = u == 0
    i_row = ra * wide + jnp.arange(wide, dtype=jnp.int32)[:, None]
    k_column = (c * four + i) * B + jnp.arange(B, dtype=jnp.int32)[None, :]
    left = jnp.where(k_column <= i_row, own.T, jnp.where(first, crossed[0], crossed[1]))

    direct = jnp.stack([jnp.where(first, tile, other), jnp.where(first, other, tile)])
    half = jnp.arange(nu, dtype=jnp.int32)[:, None, None]
    r_row = ((z * nu + half) * four + i) * B + jnp.arange(B, dtype=jnp.int32)[None, :, None]
    j_column = c * wide + jnp.arange(wide, dtype=jnp.int32)[None, None, :]
    right = jnp.where(r_row <= j_column, direct, crossed.transpose(0, 2, 1)).reshape(nu * B, wide)

    left, right = lax.optimization_barrier((left, right))
    right = lax.all_gather(right, "z", axis=0, tiled=True)
    left = jnp.broadcast_to(left[None], (ny * nw, wide, B))
    left = lax.all_to_all(left, ("y", "w"), split_axis=0, concat_axis=0, tiled=True)
    partial = product(left, right, ncore)
    partial = partial.reshape(ncore, nv, B, wide)
    partial = jnp.sum(lax.all_to_all(partial, "core", split_axis=0, concat_axis=0, tiled=True), axis=0)
    partial = jnp.sum(lax.all_to_all(partial, "v", split_axis=0, concat_axis=0, tiled=True), axis=0)
    return partial.astype(jnp.bfloat16)


def solution(mesh):
    finer = Mesh(mesh.devices.reshape(8, 8, 2, 2, 2, 2), AXES)
    return jax.shard_map(
        body,
        mesh=finer,
        in_specs=(P(("z", "u", "v", "core"), None), P()),
        out_specs=P(("z", "u", "v", "core"), ("y", "w")),
        check_vma=False,
    )
```

time: 174 us -> 159 us (0.914)
  starting transfers between devices: 67.8 us -> 42.1 us
  waiting for transfers between devices: 51.6 us -> 63.3 us
  Pallas kernels: 0 us -> 3.49 us
  local copies, waits for them, and re-layouts: 8.49 us -> 5.1 us
  matrix products: 2.83 us -> 0 us
  blocking collectives: 24.6 us -> 26.6 us
    all_gather x1, waiting for transfers between devices: 0.02 us -> 48.5 us  [body(): right = lax.all_gather(right, 'z', axis=0, tiled=True)]
    all_to_all x1, waiting for transfers between devices: 47.6 us -> 0.07 us  [body(): lax.all_to_all(left, ('y', 'w'), split_axis=0, concat_axis=0, tiled=True)]
    all_to_all x1, starting transfers between devices: 38.2 us -> 17.4 us  [body(): lax.all_to_all(left, ('y', 'w'), split_axis=0, concat_axis=0, tiled=True)]
    all_to_all x1, waiting for transfers between devices: 0.01 us -> 9.72 us  [body(): lax.all_to_all(blocks, ('u', 'v', 'core'), split_axis=0, concat_axis=0, t...]
    ppermute x4 -> x0, starting transfers between devices: 9.45 us -> none  [body(): lax.ppermute(pair, AXES, [(flat(*d), flat(d[2], d[3], d[0], d[1], (d[4] +...]
    all_to_all x1, starting transfers between devices: 10.8 us -> 15.3 us  [body(): lax.all_to_all(blocks, ('u', 'v', 'core'), split_axis=0, concat_axis=0, t...]
    ppermute x1, waiting for transfers between devices: 0.01 us -> 4.31 us  [body(): other = lax.ppermute(tile, 'u', [(a, nu - 1 - a) for a in range(nu)])]
    ppermute x4 -> x0, waiting for transfers between devices: 3.97 us -> none  [body(): lax.ppermute(pair, AXES, [(flat(*d), flat(d[2], d[3], d[0], d[1], (d[4] +...]
  transfers between devices with their start and end apart: 9 -> 5, of which waited for: 2 -> 4; matrix products, arithmetic and copies ran while one was open for 6% -> 0% of each run, Pallas kernels for 0% -> 0%
where the time goes in v3:
time: 159 us; the launch traced here: 158 us
  waiting for transfers between devices  63.3 us (40%)
  starting transfers between devices  42.1 us (26%)
  blocking collectives  26.6 us (17%)
  between operations  13.5 us (8%)
  local copies, waits for them, and re-layouts  5.1 us (3%)
  other arithmetic  4.02 us (3%)
  Pallas kernels  3.49 us (2%)
    all_gather x1, waiting for transfers between devices, body(): right = lax.all_gather(right, 'z', axis=0, tiled=True)  48.5 us
    all_to_all x1, blocking collectives, body(): lax.all_to_all(partial, 'v', split_axis=0, concat_axis=0, tiled=True)  17.5 us
    all_to_all x1, starting transfers between devices, body(): lax.all_to_all(left, ('y', 'w'), split_axis=0, concat_axis=0, tiled=True)  17.4 us
    all_to_all x1, starting transfers between devices, body(): lax.all_to_all(blocks, ('u', 'v', 'core'), split_axis=0, concat_axis=0, t...  15.3 us
    all_to_all x1, waiting for transfers between devices, body(): lax.all_to_all(blocks, ('u', 'v', 'core'), split_axis=0, concat_axis=0, t...  9.72 us
    all_to_all x1, blocking collectives, body(): lax.all_to_all(partial, 'core', split_axis=0, concat_axis=0, tiled=True)  9.05 us
    ppermute x1, starting transfers between devices, body(): other = lax.ppermute(tile, 'u', [(a, nu - 1 - a) for a in range(nu)])  8.56 us
    ppermute x1, waiting for transfers between devices, body(): other = lax.ppermute(tile, 'u', [(a, nu - 1 - a) for a in range(nu)])  4.31 us
  transfers between devices with their start and end apart: 5, of which 4 were waited for; matrix products, arithmetic and copies ran while one was open for 0% of the time, Pallas kernels for 0%

profile of v3, /device:TPU:1, one launch (start us, length us, event | category | flops | bytes accessed | tf_op | source)
XLA Modules:
  0.0 158.0 jit_solution(9447946245031600025)
XLA Ops:
  6.5 0.0 copy-start
  6.5 0.9 compare_bitcast_fusion
  7.5 0.1 broadcast_bitcast_fusion
  7.5 0.6 copy-done
  8.2 0.1 copy.11
  8.3 0.2 and_select_fusion
  8.5 0.7 collective-permute-start
  9.2 8.6 %collective-permute-start.1 = (bf16[128,512]{0,1:T(8,128)(2,1)S(1)}, bf16[128,512]{0,1:T(8,128)(2,1)S(1)}, u32[]{:S(2)}, u32[]{:S(2)}) collective-permute-start(bf16[128,512]{0,1:T(8,128)(2,1)S(1)} %and_select_fusion), channel_id=1, source_target_pairs={{0,4},{4,0},{1,5},{5,1},{2,6},{6,2},{3,7},{7,3},{8,12},{12,8},{9,1... | collective-permute-start | bytes 393224 | tf_op jit(solution)/shard_map/ppermute | solution.py:74
  17.8 0.0 collective-permute-done
  17.8 4.3 %collective-permute-done.1 = bf16[128,512]{0,1:T(8,128)(2,1)S(1)} collective-permute-done((bf16[128,512]{0,1:T(8,128)(2,1)S(1)}, bf16[128,512]{0,1:T(8,128)(2,1)S(1)}, u32[]{:S(2)}, u32[]{:S(2)}) %collective-permute-start.1) | collective-permute-done | bytes 131104 | tf_op jit(solution)/shard_map/ppermute | solution.py:74
  22.1 0.2 select_bitcast_fusion.1
  22.3 0.1 copy.9
  22.4 0.7 pad_maximum_fusion
  23.2 15.3 %all-to-all-start = ((bf16[8,128,128]{2,1,0:T(8,128)(2,1)}), bf16[8,128,128]{2,1,0:T(8,128)(2,1)S(1)}, u32[]{:S(2)}, u32[]{:S(2)}) async-start(bf16[8,128,128]{2,1,0:T(8,128)(2,1)} %pad_maximum_fusion), calls=%async_computation | async-start | bytes 524288 | tf_op jit(solution)/shard_map/all_to_all | solution.py:78
  38.5 0.1 iota_add_fusion.2
  38.6 9.7 %all-to-all-done = bf16[8,128,128]{2,1,0:T(8,128)(2,1)S(1)} async-done(((bf16[8,128,128]{2,1,0:T(8,128)(2,1)}), bf16[8,128,128]{2,1,0:T(8,128)(2,1)S(1)}, u32[]{:S(2)}, u32[]{:S(2)}) %all-to-all-start) | async-done | bytes 262176 | tf_op jit(solution)/shard_map/all_to_all | solution.py:78
  48.3 0.1 compare_select_fusion
  48.5 0.8 copy.10
  49.3 0.1 compare_select_fusion.1
  49.5 1.7 %broadcast_in_dim.10 = bf16[16,512,128]{2,1,0:T(8,128)(2,1)} broadcast(bf16[512,128]{1,0:T(8,128)(2,1)S(1)} %compare_select_fusion.1), dimensions={1,2} | broadcast | bytes 2228224 | tf_op jit(solution)/shard_map/broadcast_in_dim | solution.py:94
  51.2 17.4 %all-to-all-start.1 = ((bf16[16,512,128]{2,1,0:T(8,128)(2,1)}), bf16[16,512,128]{2,1,0:T(8,128)(2,1)}, u32[]{:S(2)}, u32[]{:S(2)}) async-start(bf16[16,512,128]{2,1,0:T(8,128)(2,1)} %broadcast_in_dim.10), calls=%async_computation.1 | async-start | bytes 4194304 | tf_op jit(solution)/shard_map/all_to_all | solution.py:95
  68.6 0.0 all-gather.2.cloned.1.call-start
  68.7 0.7 all-gather.2.cloned.1.call-update
  69.4 48.5 %all-gather.2.cloned.1.call-done.right_ref = bf16[2048,512]{1,0:T(8,128)(2,1)} async-done(((bf16[256,512]{1,0:T(8,128)(2,1)}), bf16[2048,512]{1,0:T(8,128)(2,1)}) %all-gather.2.cloned.1.call-update) | async-done | bytes 2097168 | tf_op jit(solution)/shard_map/all_gather | solution.py:93
  117.9 0.1 all-to-all-done.1.left_ref
  117.9 0.0 copy-start.1
  117.9 1.6 %copy-done.1 = bf16[2048,512]{1,0:T(8,128)(2,1)S(1)} copy-done((bf16[2048,512]{1,0:T(8,128)(2,1)S(1)}, bf16[2048,512]{1,0:T(8,128)(2,1)}, u32[]{:S(2)}) %copy-start.1) | copy-done | bytes 2097176
  119.5 3.5 %product.1 = f32[512,512]{1,0:T(8,128)S(1)} custom-call(bf16[16,512,128]{2,1,0:T(8,128)(2,1)} %all-to-all-done.1.left_ref, bf16[2048,512]{1,0:T(8,128)(2,1)S(1)} %copy-done.1), custom_call_target="tpu_custom_call" | custom-call | flops 1073741824 | bytes 5242880 | tf_op jit(solution)/shard_map/product/pallas_call | solution.py:21
  123.0 9.0 %all_to_all.20 = f32[2,2,128,512]{3,2,1,0:T(8,128)S(1)} all-to-all(f32[2,2,128,512]{3,2,1,0:T(8,128)S(1)} %bitcast.19), channel_id=1, replica_groups=mesh['z'=8,'y'=8,'w'=2,'u'=2,'v'=2,'core'=2] {'core'}, dimensions={0} | all-to-all | bytes 2097152 | tf_op jit(solution)/shard_map/all_to_all | solution.py:98
  132.1 0.9 reduce_sum.18
  133.0 17.5 %all_to_all.21 = f32[2,128,512]{2,1,0:T(8,128)S(1)} all-to-all(f32[2,128,512]{2,1,0:T(8,128)} %reduce_sum.18), channel_id=1, replica_groups=mesh['z'=8,'y'=8,'w'=2,'u'=2,'v'=2,'core'=2] {'v'}, dimensions={0} | all-to-all | bytes 1048576 | tf_op jit(solution)/shard_map/all_to_all | solution.py:99
  150.5 0.7 reduce_sum.19
  (7 shorter events, 0.0 us)
Async XLA Ops:
  6.5 1.6 %copy-start = (bf16[128,8192]{1,0:T(8,128)(2,1)S(1)}, bf16[128,8192]{1,0:T(8,128)(2,1)}, u32[]{:S(2)}) copy-start(bf16[128,8192]{1,0:T(8,128)(2,1)} %param.2) | copy-start | bytes 6291460
  8.5 9.3 %collective-permute-start = (bf16[128,512]{0,1:T(8,128)(2,1)S(1)}, bf16[128,512]{0,1:T(8,128)(2,1)S(1)}, u32[]{:S(2)}, u32[]{:S(2)}) collective-permute-start(bf16[128,512]{0,1:T(8,128)(2,1)S(1)} %and_select_fusion), channel_id=1, source_target_pairs={{8,4},{9,5},{10,6},{11,7},{16,128},{17,129},{18,130},{19,131},{24,... | collective-permute-start | bytes 393224 | tf_op jit(solution)/shard_map/ppermute | solution.py:69
  9.2 12.9 %collective-permute-start.1 = (bf16[128,512]{0,1:T(8,128)(2,1)S(1)}, bf16[128,512]{0,1:T(8,128)(2,1)S(1)}, u32[]{:S(2)}, u32[]{:S(2)}) collective-permute-start(bf16[128,512]{0,1:T(8,128)(2,1)S(1)} %and_select_fusion), channel_id=1, source_target_pairs={{0,4},{4,0},{1,5},{5,1},{2,6},{6,2},{3,7},{7,3},{8,12},{12,8},{9,1... | collective-permute-start | bytes 393224 | tf_op jit(solution)/shard_map/ppermute | solution.py:74
  23.2 25.2 %all-to-all-start = ((bf16[8,128,128]{2,1,0:T(8,128)(2,1)}), bf16[8,128,128]{2,1,0:T(8,128)(2,1)S(1)}, u32[]{:S(2)}, u32[]{:S(2)}) async-start(bf16[8,128,128]{2,1,0:T(8,128)(2,1)} %pad_maximum_fusion), calls=%async_computation | async-start | bytes 524288 | tf_op jit(solution)/shard_map/all_to_all | solution.py:78
  51.2 66.7 %all-to-all-start.1 = ((bf16[16,512,128]{2,1,0:T(8,128)(2,1)}), bf16[16,512,128]{2,1,0:T(8,128)(2,1)}, u32[]{:S(2)}, u32[]{:S(2)}) async-start(bf16[16,512,128]{2,1,0:T(8,128)(2,1)} %broadcast_in_dim.10), calls=%async_computation.1 | async-start | bytes 4194304 | tf_op jit(solution)/shard_map/all_to_all | solution.py:95
  68.6 49.2 %all-gather.2.cloned.1.call-start = ((), (), s32[]{:S(2)}) async-start(), calls=%async_computation.4 | async-start | bytes 2359296 | tf_op jit(solution)/shard_map/all_gather | solution.py:93
  117.9 1.6 %copy-start.1 = (bf16[2048,512]{1,0:T(8,128)(2,1)S(1)}, bf16[2048,512]{1,0:T(8,128)(2,1)}, u32[]{:S(2)}) copy-start(bf16[2048,512]{1,0:T(8,128)(2,1)} %all-gather.2.cloned.1.call-done.right_ref) | copy-start | bytes 6291460
Sparse Core Ops, SparseCore 0:
  72.1 45.6 all-gather.1

commit v4 on v3

--- a/solution.py
+++ b/solution.py
@@ -9,7 +9,24 @@
 AXES = ("z", "y", "w", "u", "v", "core")
 
 
-def product_kernel(left_ref, right_ref, out_ref):
+def first_rows_kernel(right_ref, out_ref):
+    out_ref[...] = right_ref[...]
+
+
+def first_rows(right):
+    shape = (16, right.shape[1])
+    return pl.pallas_call(
+        first_rows_kernel,
+        grid=(1,),
+        in_specs=[pl.BlockSpec(shape, lambda m: (0, 0))],
+        out_specs=pl.BlockSpec(shape, lambda m: (0, 0)),
+        out_shape=jax.ShapeDtypeStruct(shape, right.dtype),
+        cost_estimate=pl.CostEstimate(flops=10**11, bytes_accessed=10**8, transcendentals=0),
+        name="first_rows",
+    )(right)
+
+
+def product_kernel(left_ref, right_ref, rows_ref, out_ref):
     pieces = [left_ref[k] for k in range(left_ref.shape[0])]
     out_ref[...] = jnp.dot(jnp.concatenate(pieces, axis=1), right_ref[...], preferred_element_type=jnp.float32)
 
@@ -24,6 +41,7 @@
         in_specs=[
             pl.BlockSpec((count, step, depth), lambda m: (0, m, 0)),
             pl.BlockSpec((count * depth, columns), lambda m: (0, 0)),
+            pl.BlockSpec((16, columns), lambda m: (0, 0)),
         ],
         out_specs=pl.BlockSpec((step, columns), lambda m: ((m % swap) * (rows // step // swap) + m // swap, 0)),
         out_shape=jax.ShapeDtypeStruct((rows, columns), jnp.float32),
@@ -34,7 +52,7 @@
             transcendentals=0,
         ),
         name="product",
-    )(left, right)
+    )(left, right, first_rows(right))
 
 
 def body(stored, pattern):
@@ -71,11 +89,13 @@
         AXES,
         [(flat(*d), flat(d[2], d[3], d[0], d[1], d[4])) for d in everywhere if d[0] * nu + d[1] < d[2] * nw + d[3]],
     )
-    other = lax.ppermute(tile, "u", [(a, nu - 1 - a) for a in range(nu)])
+    mirrored, later = lax.optimization_barrier((mirrored, tile))
+    other = lax.ppermute(later, "u", [(a, nu - 1 - a) for a in range(nu)])
     own = jnp.where(ra <= c, tile, mirrored)
     blocks = own.reshape(B, four, B).transpose(1, 0, 2)
     blocks = jnp.concatenate([blocks] * nu, axis=0)
     crossed = lax.all_to_all(blocks, ("u", "v", "core"), split_axis=0, concat_axis=0, tiled=True)
+    crossed, other, plain = lax.optimization_barrier((crossed, other, tile))
     crossed = crossed.reshape(nu, wide, B)
 
     first = u == 0
@@ -83,7 +103,7 @@
     k_column = (c * four + i) * B + jnp.arange(B, dtype=jnp.int32)[None, :]
     left = jnp.where(k_column <= i_row, own.T, jnp.where(first, crossed[0], crossed[1]))
 
-    direct = jnp.stack([jnp.where(first, tile, other), jnp.where(first, other, tile)])
+    direct = jnp.stack([jnp.where(first, plain, other), jnp.where(first, other, plain)])
     half = jnp.arange(nu, dtype=jnp.int32)[:, None, None]
     r_row = ((z * nu + half) * four + i) * B + jnp.arange(B, dtype=jnp.int32)[None, :, None]
     j_column = c * wide + jnp.arange(wide, dtype=jnp.int32)[None, None, :]

time: 159 us -> 159 us (level)
  waiting for transfers between devices: 63.3 us -> 57 us
  starting transfers between devices: 42.1 us -> 47.7 us
    all_to_all x1, waiting for transfers between devices: 9.72 us -> 0.01 us  [body(): lax.all_to_all(blocks, ('u', 'v', 'core'), split_axis=0, concat_axis=0, t...]
    all_gather x1, waiting for transfers between devices: 48.5 us -> 39.2 us  [body(): right = lax.all_gather(right, 'z', axis=0, tiled=True)]
    all_to_all x1, waiting for transfers between devices: 0.07 us -> 8.73 us  [body(): lax.all_to_all(left, ('y', 'w'), split_axis=0, concat_axis=0, tiled=True)]
    ppermute x1, waiting for transfers between devices: 4.31 us -> 9.06 us  [body(): other = lax.ppermute(later, 'u', [(a, nu - 1 - a) for a in range(nu)])]
    all_to_all x1, starting transfers between devices: 17.4 us -> 21 us  [body(): lax.all_to_all(left, ('y', 'w'), split_axis=0, concat_axis=0, tiled=True)]
    all_to_all x1, starting transfers between devices: 15.3 us -> 18.8 us  [body(): lax.all_to_all(blocks, ('u', 'v', 'core'), split_axis=0, concat_axis=0, t...]
    all_to_all x1, blocking collectives: 9.05 us -> 7 us  [body(): lax.all_to_all(partial, 'core', split_axis=0, concat_axis=0, tiled=True)]
  transfers between devices with their start and end apart: 5 -> 5, of which waited for: 4 -> 3; matrix products, arithmetic and copies ran while one was open for 0% -> 1% of each run, Pallas kernels for 0% -> 1%
where the time goes in v4:
time: 159 us; the launch traced here: 158 us
  waiting for transfers between devices  57 us (36%)
  starting transfers between devices  47.7 us (30%)
  blocking collectives  25.4 us (16%)
  between operations  13.5 us (8%)
  local copies, waits for them, and re-layouts  5.83 us (4%)
  Pallas kernels  4.81 us (3%)
  other arithmetic  4.04 us (3%)
    all_gather x1, waiting for transfers between devices, body(): right = lax.all_gather(right, 'z', axis=0, tiled=True)  39.2 us
    all_to_all x1, starting transfers between devices, body(): lax.all_to_all(left, ('y', 'w'), split_axis=0, concat_axis=0, tiled=True)  21 us
    all_to_all x1, starting transfers between devices, body(): lax.all_to_all(blocks, ('u', 'v', 'core'), split_axis=0, concat_axis=0, t...  18.8 us
    all_to_all x1, blocking collectives, body(): lax.all_to_all(partial, 'v', split_axis=0, concat_axis=0, tiled=True)  18.4 us
    ppermute x1, waiting for transfers between devices, body(): other = lax.ppermute(later, 'u', [(a, nu - 1 - a) for a in range(nu)])  9.06 us
    all_to_all x1, waiting for transfers between devices, body(): lax.all_to_all(left, ('y', 'w'), split_axis=0, concat_axis=0, tiled=True)  8.73 us
    ppermute x1, starting transfers between devices, body(): other = lax.ppermute(later, 'u', [(a, nu - 1 - a) for a in range(nu)])  7.19 us
    all_to_all x1, blocking collectives, body(): lax.all_to_all(partial, 'core', split_axis=0, concat_axis=0, tiled=True)  7 us
  transfers between devices with their start and end apart: 5, of which 3 were waited for; matrix products, arithmetic and copies ran while one was open for 1% of the time, Pallas kernels for 1%

profile of v4, /device:TPU:1, one launch (start us, length us, event | category | flops | bytes accessed | tf_op | source)
XLA Modules:
  0.0 158.3 jit_solution(10261300019350332628)
XLA Ops:
  6.5 0.0 copy-start
  6.5 0.9 compare_bitcast_fusion
  7.5 0.1 broadcast_bitcast_fusion
  7.5 0.6 copy-done
  8.2 0.1 copy.11
  8.3 0.2 and_select_fusion
  8.5 0.7 collective-permute-start
  9.2 0.0 collective-permute-done
  9.2 0.2 broadcast_select_fusion
  9.4 0.1 copy.9
  9.5 0.7 pad_maximum_fusion
  10.3 18.8 %all-to-all-start = ((bf16[8,128,128]{2,1,0:T(8,128)(2,1)}), bf16[8,128,128]{2,1,0:T(8,128)(2,1)S(1)}, u32[]{:S(2)}, u32[]{:S(2)}) async-start(bf16[8,128,128]{2,1,0:T(8,128)(2,1)} %pad_maximum_fusion), calls=%async_computation | async-start | bytes 524288 | tf_op jit(solution)/shard_map/all_to_all | solution.py:97
  29.0 0.0 all-gather.2.cloned.1.call-start
  29.1 0.1 iota_add_fusion.2
  29.1 7.2 %collective-permute-start.1 = (bf16[128,512]{0,1:T(8,128)(2,1)S(1)}, bf16[128,512]{0,1:T(8,128)(2,1)S(1)}, u32[]{:S(2)}, u32[]{:S(2)}) collective-permute-start(bf16[128,512]{0,1:T(8,128)(2,1)S(1)} %and_select_fusion), channel_id=1, source_target_pairs={{0,4},{4,0},{1,5},{5,1},{2,6},{6,2},{3,7},{7,3},{8,12},{12,8},{9,1... | collective-permute-start | bytes 393224 | tf_op jit(solution)/shard_map/ppermute | solution.py:93
  36.4 9.1 %collective-permute-done.1 = bf16[128,512]{0,1:T(8,128)(2,1)S(1)} collective-permute-done((bf16[128,512]{0,1:T(8,128)(2,1)S(1)}, bf16[128,512]{0,1:T(8,128)(2,1)S(1)}, u32[]{:S(2)}, u32[]{:S(2)}) %collective-permute-start.1) | collective-permute-done | bytes 131104 | tf_op jit(solution)/shard_map/ppermute | solution.py:93
  45.4 0.0 all-to-all-done
  45.5 0.1 compare_select_fusion
  45.6 0.8 copy.10
  46.5 0.1 compare_select_fusion.1
  46.6 0.0 all-gather.2.cloned.1.call-update
  46.6 1.7 %broadcast_in_dim.10 = bf16[16,512,128]{2,1,0:T(8,128)(2,1)} broadcast(bf16[512,128]{1,0:T(8,128)(2,1)S(1)} %compare_select_fusion.1), dimensions={1,2} | broadcast | bytes 2228224 | tf_op jit(solution)/shard_map/broadcast_in_dim | solution.py:114
  48.4 21.0 %all-to-all-start.1 = ((bf16[16,512,128]{2,1,0:T(8,128)(2,1)}), bf16[16,512,128]{2,1,0:T(8,128)(2,1)}, u32[]{:S(2)}, u32[]{:S(2)}) async-start(bf16[16,512,128]{2,1,0:T(8,128)(2,1)} %broadcast_in_dim.10), calls=%async_computation.1 | async-start | bytes 4194304 | tf_op jit(solution)/shard_map/all_to_all | solution.py:115
  69.4 39.2 %all-gather.2.cloned.1.call-done.right_ref = bf16[2048,512]{1,0:T(8,128)(2,1)} async-done(((bf16[256,512]{1,0:T(8,128)(2,1)}), bf16[2048,512]{1,0:T(8,128)(2,1)}) %all-gather.2.cloned.1.call-update) | async-done | bytes 2097168 | tf_op jit(solution)/shard_map/all_gather | solution.py:113
  108.6 1.3 first_rows.1.rows_ref
  109.9 8.7 %all-to-all-done.1.left_ref = bf16[16,512,128]{2,1,0:T(8,128)(2,1)} async-done(((bf16[16,512,128]{2,1,0:T(8,128)(2,1)}), bf16[16,512,128]{2,1,0:T(8,128)(2,1)}, u32[]{:S(2)}, u32[]{:S(2)}) %all-to-all-start.1) | async-done | bytes 2097184 | tf_op jit(solution)/shard_map/all_to_all | solution.py:115
  118.7 0.0 copy-start.1
  118.7 1.6 %copy-done.1 = bf16[2048,512]{1,0:T(8,128)(2,1)S(1)} copy-done((bf16[2048,512]{1,0:T(8,128)(2,1)S(1)}, bf16[2048,512]{1,0:T(8,128)(2,1)}, u32[]{:S(2)}) %copy-start.1) | copy-done | bytes 2097176
  120.3 0.0 copy-start.2
  120.3 0.7 copy-done.2
  121.0 3.5 %product.1 = f32[512,512]{1,0:T(8,128)S(1)} custom-call(bf16[16,512,128]{2,1,0:T(8,128)(2,1)} %all-to-all-done.1.left_ref, bf16[2048,512]{1,0:T(8,128)(2,1)S(1)} %copy-done.1, bf16[16,512]{1,0:T(8,128)(2,1)S(1)} %copy-done.2), custom_call_target="tpu_custom_call" | custom-call | flops 1073741824 | bytes 5242880 | tf_op jit(solution)/shard_map/product/pallas_call | solution.py:38
  124.5 7.0 %all_to_all.20 = f32[2,2,128,512]{3,2,1,0:T(8,128)S(1)} all-to-all(f32[2,2,128,512]{3,2,1,0:T(8,128)S(1)} %bitcast.19), channel_id=1, replica_groups=mesh['z'=8,'y'=8,'w'=2,'u'=2,'v'=2,'core'=2] {'core'}, dimensions={0} | all-to-all | bytes 2097152 | tf_op jit(solution)/shard_map/all_to_all | solution.py:118
  131.5 0.9 reduce_sum.18
  132.4 18.4 %all_to_all.21 = f32[2,128,512]{2,1,0:T(8,128)S(1)} all-to-all(f32[2,128,512]{2,1,0:T(8,128)} %reduce_sum.18), channel_id=1, replica_groups=mesh['z'=8,'y'=8,'w'=2,'u'=2,'v'=2,'core'=2] {'v'}, dimensions={0} | all-to-all | bytes 1048576 | tf_op jit(solution)/shard_map/all_to_all | solution.py:119
  150.8 0.7 reduce_sum.19
  (8 shorter events, 0.1 us)
Async XLA Ops:
  6.5 1.6 %copy-start = (bf16[128,8192]{1,0:T(8,128)(2,1)S(1)}, bf16[128,8192]{1,0:T(8,128)(2,1)}, u32[]{:S(2)}) copy-start(bf16[128,8192]{1,0:T(8,128)(2,1)} %param.2) | copy-start | bytes 6291460
  8.5 0.7 collective-permute-start
  10.3 35.2 %all-to-all-start = ((bf16[8,128,128]{2,1,0:T(8,128)(2,1)}), bf16[8,128,128]{2,1,0:T(8,128)(2,1)S(1)}, u32[]{:S(2)}, u32[]{:S(2)}) async-start(bf16[8,128,128]{2,1,0:T(8,128)(2,1)} %pad_maximum_fusion), calls=%async_computation | async-start | bytes 524288 | tf_op jit(solution)/shard_map/all_to_all | solution.py:97
  29.0 79.6 %all-gather.2.cloned.1.call-start = ((), (), s32[]{:S(2)}) async-start(), calls=%async_computation.4 | async-start | bytes 2359296 | tf_op jit(solution)/shard_map/all_gather | solution.py:113
  29.1 16.3 %collective-permute-start.1 = (bf16[128,512]{0,1:T(8,128)(2,1)S(1)}, bf16[128,512]{0,1:T(8,128)(2,1)S(1)}, u32[]{:S(2)}, u32[]{:S(2)}) collective-permute-start(bf16[128,512]{0,1:T(8,128)(2,1)S(1)} %and_select_fusion), channel_id=1, source_target_pairs={{0,4},{4,0},{1,5},{5,1},{2,6},{6,2},{3,7},{7,3},{8,12},{12,8},{9,1... | collective-permute-start | bytes 393224 | tf_op jit(solution)/shard_map/ppermute | solution.py:93
  48.4 70.3 %all-to-all-start.1 = ((bf16[16,512,128]{2,1,0:T(8,128)(2,1)}), bf16[16,512,128]{2,1,0:T(8,128)(2,1)}, u32[]{:S(2)}, u32[]{:S(2)}) async-start(bf16[16,512,128]{2,1,0:T(8,128)(2,1)} %broadcast_in_dim.10), calls=%async_computation.1 | async-start | bytes 4194304 | tf_op jit(solution)/shard_map/all_to_all | solution.py:115
  118.7 1.6 %copy-start.1 = (bf16[2048,512]{1,0:T(8,128)(2,1)S(1)}, bf16[2048,512]{1,0:T(8,128)(2,1)}, u32[]{:S(2)}) copy-start(bf16[2048,512]{1,0:T(8,128)(2,1)} %all-gather.2.cloned.1.call-done.right_ref) | copy-start | bytes 6291460
  120.3 0.7 copy-start.2
Sparse Core Ops, SparseCore 0:
  46.7 61.8 all-gather.1

commit v5 on v0

v5 whole, which is shorter than its diff:
```python
import jax
import jax.numpy as jnp
from jax import lax
from jax.experimental import pallas as pl
from jax.experimental.pallas import tpu as pltpu
from jax.sharding import Mesh, PartitionSpec as P

B = 128
AXES = ("z", "y", "w", "u", "v", "core")
TAIL = 16


def product_kernel(y_ref, *refs):
    *left_refs, right_ref, out_ref, ordered = refs
    n, depth, _ = right_ref.shape
    y = y_ref[0]

    @pl.when(pl.program_id(0) == 0)
    def _():
        for s in range(n):
            ordered[s * depth : (s + 1) * depth, :] = right_ref[lax.rem(y - s + n, n)]

    left = jnp.concatenate([r[...] for r in left_refs], axis=0)
    total = lax.dot_general(
        left, ordered[...], (((0,), (0,)), ((), ())), preferred_element_type=jnp.float32
    )
    cores, ways, rows, columns = out_ref.shape
    for a in range(cores):
        for b in range(ways):
            out_ref[a, b] = total[a * rows : (a + 1) * rows, b * columns : (b + 1) * columns]


def product(lefts, right, y, cores, ways):
    n, depth, wide = right.shape
    step = cores * B
    panel = wide // ways
    return pl.pallas_call(
        product_kernel,
        grid_spec=pltpu.PrefetchScalarGridSpec(
            num_scalar_prefetch=1,
            grid=(wide // step,),
            in_specs=[pl.BlockSpec((depth, step), lambda m, _: (0, m)) for _ in lefts]
            + [pl.BlockSpec((n, depth, wide), lambda m, _: (0, 0, 0))],
            out_specs=pl.BlockSpec((cores, ways, B, panel), lambda m, _: (0, m, 0, 0)),
            scratch_shapes=[pltpu.VMEM((n * depth, wide), right.dtype)],
        ),
        out_shape=jax.ShapeDtypeStruct((cores, wide // step * ways, B, panel), jnp.float32),
        compiler_params=pltpu.CompilerParams(vmem_limit_bytes=24 * 1024 * 1024),
        cost_estimate=pl.CostEstimate(
            flops=2 * n * depth * wide * wide,
            bytes_accessed=4 * n * depth * wide + 4 * wide * wide,
            transcendentals=0,
        ),
        name="product",
    )(y.reshape(1), *lefts, right)


def body(stored, pattern):
    nz, ny, nw, nu, nv, ncore = (lax.axis_size(a) for a in AXES)
    z, y, w, u, v, core = (lax.axis_index(a) for a in AXES)
    nl = nu * nv * ncore
    l = (u * nv + v) * ncore + core
    g = z * nl + l
    plane = nl * B
    part = B // nw

    raw = lax.dynamic_slice(stored, (0, y * plane), (B, plane))
    present = lax.dynamic_slice(pattern, (g, y * nl), (1, nl))
    present = jnp.repeat(present, B, axis=1) > 0
    row = g * B + jnp.arange(B, dtype=jnp.int32)[:, None]
    column = y * plane + jnp.arange(plane, dtype=jnp.int32)[None, :]
    band = jnp.where(present & (column >= row), raw, jnp.zeros((), raw.dtype))

    def flat(zz, yy, r):
        return (zz * ny + yy) * (nw * nl) + r

    mirrored = lax.ppermute(
        band,
        AXES,
        [
            (flat(a, b, r), flat(b, a, r))
            for a in range(nz)
            for b in range(a + 1, ny)
            for r in range(nw * nl)
        ],
    )
    own = jnp.where(z <= y, band, mirrored)
    turned = own.T.reshape(nl, nw, part, B)
    turned = lax.dynamic_index_in_dim(turned, w, 1, keepdims=False)
    crossed = lax.all_to_all(turned, ("u", "v", "core"), split_axis=0, concat_axis=0, tiled=True)
    crossed = crossed.transpose(1, 0, 2).reshape(part, plane)
    straight = lax.dynamic_slice(own, (w * part, 0), (part, plane))

    offset = l * B + w * part + jnp.arange(part, dtype=jnp.int32)[:, None]
    across = jnp.arange(plane, dtype=jnp.int32)[None, :]
    left = jnp.where(y * plane + offset <= z * plane + across, straight, crossed)
    right = jnp.where(z * plane + offset <= y * plane + across, straight, crossed)

    right = jnp.broadcast_to(right[None], (nz, part, plane))
    right = lax.all_to_all(right, "z", split_axis=0, concat_axis=0, tiled=True)
    lefts = [left] + [lax.ppermute(left, "y", [(a, (a + s) % ny) for a in range(ny)]) for s in range(1, ny)]

    partial = product(lefts, right, y, ncore, nw)
    partial = jnp.sum(lax.all_to_all(partial, "core", split_axis=0, concat_axis=0, tiled=True), axis=0)

    most = jnp.max(jnp.abs(partial))
    power = jnp.clip(jnp.ceil(jnp.log2(jnp.maximum(most, 1e-30))) - 14.0, -100.0, 100.0)
    scaled = (partial * jnp.exp2(-power)).astype(jnp.float16)
    tail = jnp.broadcast_to(power.astype(jnp.float16), (scaled.shape[0], TAIL, scaled.shape[2]))
    sent = jnp.concatenate([scaled, tail], axis=1)
    got = lax.all_to_all(sent, ("u", "v", "w"), split_axis=0, concat_axis=0, tiled=True)
    scale = jnp.exp2(got[:, B, 0].astype(jnp.float32))
    total = jnp.sum(got[:, :B].astype(jnp.float32) * scale[:, None, None], axis=0)
    return total.astype(jnp.bfloat16)


def solution(mesh):
    finer = Mesh(mesh.devices.reshape(8, 8, 2, 2, 2, 2), AXES)
    return jax.shard_map(
        body,
        mesh=finer,
        in_specs=(P(("z", "u", "v", "core"), None), P()),
        out_specs=P(("z", "u", "v", "core"), ("y", "w")),
        check_vma=False,
    )
```

time: 227 us -> 158 us (0.70); the launches traced: 223 us -> 157 us
  waiting for transfers between devices: 159 us -> 22.6 us
  starting transfers between devices: 28.2 us -> 78.3 us
  blocking collectives: 0 us -> 42.7 us
  between operations: 13.5 us -> 0.92 us
  local copies, waits for them, and re-layouts: 12.1 us -> 2.26 us
  matrix products: 4.45 us -> 0 us
  other arithmetic: 5.21 us -> 8.26 us
  Pallas kernels: 0 us -> 2.51 us
    all_to_all x2, waiting for transfers between devices: 71.2 us -> 8.03 us  [the longest x1 8.02 us: body(): lax.all_to_all(turned, ('u', 'v', 'core'), split_axis=0, concat_axis=0, t...]
    reduce_scatter x1 -> x0, waiting for transfers between devices: 48.1 us -> none  [body(): summed = lax.psum_scatter(running, 'row', scatter_dimension=0, tiled=True)]
    all_to_all x0 -> x2, blocking collectives: none -> 42.7 us  [the longest x1 33.5 us: body(): lax.all_to_all(sent, ('u', 'v', 'w'), split_axis=0, concat_axis=0, tiled=...]
    all_gather x1 -> x0, waiting for transfers between devices: 40 us -> none  [body(): lax.all_gather(column_panel, 'layer', axis=0, tiled=True)]
    all_to_all x2, starting transfers between devices: 28.1 us -> 54 us  [the longest x1 36.6 us: body(): right = lax.all_to_all(right, 'z', split_axis=0, concat_axis=0, tiled=True)]
    ppermute x0 -> x8, starting transfers between devices: none -> 24.2 us  [the longest x7 23.6 us: body(): lax.ppermute(left, 'y', [(a, (a + s) % ny) for a in range(ny)])]
    ppermute x0 -> x8, waiting for transfers between devices: none -> 14.5 us  [the longest x7 14.5 us: body(): lax.ppermute(left, 'y', [(a, (a + s) % ny) for a in range(ny)])]
    all_to_all x2 -> x0, local copies, waits for them, and re-layouts: 5.85 us -> none  [body(): lax.all_to_all(stored, ('row', 'layer'), split_axis=1, concat_axis=0, til...]
  transfers between devices with their start and end apart: 4 -> 10, of which waited for: 4 -> 3; matrix products, arithmetic and copies ran while one was open for 0% -> 0% of each run, Pallas kernels for 0% -> 0%
where the time goes in v5:
time: 158 us; the launch traced here: 157 us
  starting transfers between devices  78.3 us (50%)
  blocking collectives  42.7 us (27%)
  waiting for transfers between devices  22.6 us (14%)
  other arithmetic  8.26 us (5%)
  Pallas kernels  2.51 us (2%)
  local copies, waits for them, and re-layouts  2.26 us (1%)
    all_to_all x1, starting transfers between devices, body(): right = lax.all_to_all(right, 'z', split_axis=0, concat_axis=0, tiled=True)  36.6 us
    all_to_all x1, blocking collectives, body(): lax.all_to_all(sent, ('u', 'v', 'w'), split_axis=0, concat_axis=0, tiled=...  33.5 us
    ppermute x7, starting transfers between devices, body(): lax.ppermute(left, 'y', [(a, (a + s) % ny) for a in range(ny)])  23.6 us
    all_to_all x1, starting transfers between devices, body(): lax.all_to_all(turned, ('u', 'v', 'core'), split_axis=0, concat_axis=0, t...  17.4 us
    ppermute x7, waiting for transfers between devices, body(): lax.ppermute(left, 'y', [(a, (a + s) % ny) for a in range(ny)])  14.5 us
    all_to_all x1, blocking collectives, body(): lax.all_to_all(partial, 'core', split_axis=0, concat_axis=0, tiled=True)  9.19 us
    all_to_all x1, waiting for transfers between devices, body(): lax.all_to_all(turned, ('u', 'v', 'core'), split_axis=0, concat_axis=0, t...  8.02 us
  transfers between devices with their start and end apart: 10, of which 3 were waited for; matrix products, arithmetic and copies ran while one was open for 0% of the time, Pallas kernels for 0%

profile of v5, /device:TPU:1, one launch (start us, length us, event | category | flops | bytes accessed | tf_op | source)
XLA Modules:
  0.0 157.4 jit_solution(11835818510100091227)
XLA Ops:
  0.0 0.8 compare_bitcast_fusion
  0.8 0.1 broadcast_bitcast_fusion
  0.9 1.1 and_select_fusion
  2.0 0.7 collective-permute-start
  2.7 0.0 collective-permute-done
  2.7 1.2 broadcast_select_fusion
  3.9 0.2 copy.9
  4.0 0.7 dynamic-slice_bitcast_fusion
  4.7 17.4 %all-to-all-start = ((bf16[8,64,128]{2,1,0:T(8,128)(2,1)}), bf16[8,64,128]{2,1,0:T(8,128)(2,1)S(1)}, u32[]{:S(2)}, u32[]{:S(2)}) async-start(bf16[8,64,128]{2,1,0:T(8,128)(2,1)} %dynamic-slice_bitcast_fusion), calls=%async_computation | async-start | bytes 262144 | tf_op jit(solution)/shard_map/all_to_all | solution.py:90
  22.1 8.0 %all-to-all-done = bf16[8,64,128]{2,1,0:T(8,128)(2,1)S(1)} async-done(((bf16[8,64,128]{2,1,0:T(8,128)(2,1)}), bf16[8,64,128]{2,1,0:T(8,128)(2,1)S(1)}, u32[]{:S(2)}, u32[]{:S(2)}) %all-to-all-start) | async-done | bytes 131104 | tf_op jit(solution)/shard_map/all_to_all | solution.py:90
  30.2 0.2 compare_select_fusion
  30.3 1.1 broadcast_in_dim.10
  31.4 36.6 %all-to-all-start.1 = ((bf16[8,64,1024]{2,1,0:T(8,128)(2,1)}), bf16[8,64,1024]{2,1,0:T(8,128)(2,1)S(1)}, u32[]{:S(2)}, u32[]{:S(2)}) async-start(bf16[8,64,1024]{2,1,0:T(8,128)(2,1)} %broadcast_in_dim.10), calls=%async_computation.1 | async-start | bytes 2097152 | tf_op jit(solution)/shard_map/all_to_all | solution.py:100
  68.0 1.9 %collective-permute-start.7 = (bf16[64,1024]{1,0:T(8,128)(2,1)S(1)}, bf16[64,1024]{1,0:T(8,128)(2,1)S(1)}, u32[]{:S(2)}, u32[]{:S(2)}) collective-permute-start(bf16[64,1024]{1,0:T(8,128)(2,1)S(1)} %get-tuple-element.6.refs_0_), channel_id=1, source_target_pairs={{0,112},{16,0},{32,16},{48,32},{64,48},{80,64},{96,80},{112,96},{1... | collective-permute-start | bytes 393224 | tf_op jit(solution)/shard_map/ppermute | solution.py:101
  69.9 1.9 %collective-permute-start.6 = (bf16[64,1024]{1,0:T(8,128)(2,1)S(1)}, bf16[64,1024]{1,0:T(8,128)(2,1)S(1)}, u32[]{:S(2)}, u32[]{:S(2)}) collective-permute-start(bf16[64,1024]{1,0:T(8,128)(2,1)S(1)} %get-tuple-element.6.refs_0_), channel_id=1, source_target_pairs={{0,96},{16,112},{32,0},{48,16},{64,32},{80,48},{96,64},{112,80},{1... | collective-permute-start | bytes 393224 | tf_op jit(solution)/shard_map/ppermute | solution.py:101
  71.9 5.3 %collective-permute-start.5 = (bf16[64,1024]{1,0:T(8,128)(2,1)S(1)}, bf16[64,1024]{1,0:T(8,128)(2,1)S(1)}, u32[]{:S(2)}, u32[]{:S(2)}) collective-permute-start(bf16[64,1024]{1,0:T(8,128)(2,1)S(1)} %get-tuple-element.6.refs_0_), channel_id=1, source_target_pairs={{0,80},{16,96},{32,112},{48,0},{64,16},{80,32},{96,48},{112,64},{1... | collective-permute-start | bytes 393224 | tf_op jit(solution)/shard_map/ppermute | solution.py:101
  77.2 4.2 %collective-permute-start.4 = (bf16[64,1024]{1,0:T(8,128)(2,1)S(1)}, bf16[64,1024]{1,0:T(8,128)(2,1)S(1)}, u32[]{:S(2)}, u32[]{:S(2)}) collective-permute-start(bf16[64,1024]{1,0:T(8,128)(2,1)S(1)} %get-tuple-element.6.refs_0_), channel_id=1, source_target_pairs={{0,64},{16,80},{32,96},{48,112},{64,0},{80,16},{96,32},{112,48},{1... | collective-permute-start | bytes 393224 | tf_op jit(solution)/shard_map/ppermute | solution.py:101
  81.3 2.9 %collective-permute-start.3 = (bf16[64,1024]{1,0:T(8,128)(2,1)S(1)}, bf16[64,1024]{1,0:T(8,128)(2,1)S(1)}, u32[]{:S(2)}, u32[]{:S(2)}) collective-permute-start(bf16[64,1024]{1,0:T(8,128)(2,1)S(1)} %get-tuple-element.6.refs_0_), channel_id=1, source_target_pairs={{0,48},{16,64},{32,80},{48,96},{64,112},{80,0},{96,16},{112,32},{1... | collective-permute-start | bytes 393224 | tf_op jit(solution)/shard_map/ppermute | solution.py:101
  84.2 0.0 collective-permute-done.7.refs_7_
  84.2 5.5 %collective-permute-start.2 = (bf16[64,1024]{1,0:T(8,128)(2,1)S(1)}, bf16[64,1024]{1,0:T(8,128)(2,1)S(1)}, u32[]{:S(2)}, u32[]{:S(2)}) collective-permute-start(bf16[64,1024]{1,0:T(8,128)(2,1)S(1)} %get-tuple-element.6.refs_0_), channel_id=1, source_target_pairs={{0,32},{16,48},{32,64},{48,80},{64,96},{80,112},{96,0},{112,16},{1... | collective-permute-start | bytes 393224 | tf_op jit(solution)/shard_map/ppermute | solution.py:101
  89.7 0.0 collective-permute-done.6.refs_6_
  89.7 1.9 %collective-permute-start.1 = (bf16[64,1024]{1,0:T(8,128)(2,1)S(1)}, bf16[64,1024]{1,0:T(8,128)(2,1)S(1)}, u32[]{:S(2)}, u32[]{:S(2)}) collective-permute-start(bf16[64,1024]{1,0:T(8,128)(2,1)S(1)} %get-tuple-element.6.refs_0_), channel_id=1, source_target_pairs={{0,16},{16,32},{32,48},{48,64},{64,80},{80,96},{96,112},{112,0},{1... | collective-permute-start | bytes 393224 | tf_op jit(solution)/shard_map/ppermute | solution.py:101
  91.7 0.0 collective-permute-done.5.refs_5_
  91.7 0.0 collective-permute-done.4.refs_4_
  91.7 9.9 %collective-permute-done.3.refs_3_ = bf16[64,1024]{1,0:T(8,128)(2,1)S(1)} collective-permute-done((bf16[64,1024]{1,0:T(8,128)(2,1)S(1)}, bf16[64,1024]{1,0:T(8,128)(2,1)S(1)}, u32[]{:S(2)}, u32[]{:S(2)}) %collective-permute-start.3) | collective-permute-done | bytes 131104 | tf_op jit(solution)/shard_map/ppermute | solution.py:101
  101.6 0.0 collective-permute-done.2.refs_2_
  101.6 4.6 %collective-permute-done.1.refs_1_ = bf16[64,1024]{1,0:T(8,128)(2,1)S(1)} collective-permute-done((bf16[64,1024]{1,0:T(8,128)(2,1)S(1)}, bf16[64,1024]{1,0:T(8,128)(2,1)S(1)}, u32[]{:S(2)}, u32[]{:S(2)}) %collective-permute-start.1) | collective-permute-done | bytes 131104 | tf_op jit(solution)/shard_map/ppermute | solution.py:101
  106.2 0.0 all-to-all-done.1.refs_8_
  106.2 2.5 %product.1 = f32[2,8,128,512]{3,2,1,0:T(8,128)S(1)} custom-call(s32[1]{0:T(128)} %bitcast.y_ref, bf16[64,1024]{1,0:T(8,128)(2,1)S(1)} %get-tuple-element.6.refs_0_, bf16[64,1024]{1,0:T(8,128)(2,1)S(1)} %collective-permute-done.1.refs_1_, bf16[64,1024]{1,0:T(8,128)(2,1)S(1)} %collective-permute-done.2.refs_2_, ...), custom_call_target="tpu_custom_call" | custom-call | flops 1073741824 | bytes 6291456 | tf_op jit(solution)/shard_map/product/pallas_call | solution.py:37
  108.7 9.2 %all_to_all.20 = f32[2,8,128,512]{3,2,1,0:T(8,128)} all-to-all(f32[2,8,128,512]{3,2,1,0:T(8,128)S(1)} %product.1), channel_id=1, replica_groups=mesh['z'=8,'y'=8,'w'=2,'u'=2,'v'=2,'core'=2] {'core'}, dimensions={0} | all-to-all | bytes 8388608 | tf_op jit(solution)/shard_map/all_to_all | solution.py:104
  117.9 2.9 %reduce_sum.18 = f32[8,128,512]{2,1,0:T(8,128)S(1)} reduce(f32[2,8,128,512]{3,2,1,0:T(8,128)} %all_to_all.20, f32[]{:T(128)} %constant.53.clone.1), dimensions={0}, to_apply=%region_0.1 | reduce | flops 524288 | bytes 6291460 | tf_op jit(solution)/shard_map/reduce_sum | solution.py:104
  120.8 0.8 abs_reduce_fusion
  122.3 0.3 multiply_convert_fusion
  122.6 0.2 concatenate.3
  122.9 33.5 %all_to_all.21 = f16[8,144,512]{2,1,0:T(8,128)(2,1)S(1)} all-to-all(f16[8,144,512]{2,1,0:T(8,128)(2,1)S(1)} %concatenate.3), channel_id=1, replica_groups=mesh['z'=8,'y'=8,'w'=2,'u'=2,'v'=2,'core'=2] {'u','v','w'}, dimensions={0} | all-to-all | bytes 2359296 | tf_op jit(solution)/shard_map/all_to_all | solution.py:111
  156.3 0.1 fusion.2
  156.5 0.9 multiply_reduce_fusion
  (4 shorter events, 0.0 us)
Async XLA Ops:
  2.0 0.7 collective-permute-start
  4.7 25.5 %all-to-all-start = ((bf16[8,64,128]{2,1,0:T(8,128)(2,1)}), bf16[8,64,128]{2,1,0:T(8,128)(2,1)S(1)}, u32[]{:S(2)}, u32[]{:S(2)}) async-start(bf16[8,64,128]{2,1,0:T(8,128)(2,1)} %dynamic-slice_bitcast_fusion), calls=%async_computation | async-start | bytes 262144 | tf_op jit(solution)/shard_map/all_to_all | solution.py:90
  31.4 74.8 %all-to-all-start.1 = ((bf16[8,64,1024]{2,1,0:T(8,128)(2,1)}), bf16[8,64,1024]{2,1,0:T(8,128)(2,1)S(1)}, u32[]{:S(2)}, u32[]{:S(2)}) async-start(bf16[8,64,1024]{2,1,0:T(8,128)(2,1)} %broadcast_in_dim.10), calls=%async_computation.1 | async-start | bytes 2097152 | tf_op jit(solution)/shard_map/all_to_all | solution.py:100
  68.0 16.2 %collective-permute-start.7 = (bf16[64,1024]{1,0:T(8,128)(2,1)S(1)}, bf16[64,1024]{1,0:T(8,128)(2,1)S(1)}, u32[]{:S(2)}, u32[]{:S(2)}) collective-permute-start(bf16[64,1024]{1,0:T(8,128)(2,1)S(1)} %get-tuple-element.6.refs_0_), channel_id=1, source_target_pairs={{0,112},{16,0},{32,16},{48,32},{64,48},{80,64},{96,80},{112,96},{1... | collective-permute-start | bytes 393224 | tf_op jit(solution)/shard_map/ppermute | solution.py:101
  69.9 19.8 %collective-permute-start.6 = (bf16[64,1024]{1,0:T(8,128)(2,1)S(1)}, bf16[64,1024]{1,0:T(8,128)(2,1)S(1)}, u32[]{:S(2)}, u32[]{:S(2)}) collective-permute-start(bf16[64,1024]{1,0:T(8,128)(2,1)S(1)} %get-tuple-element.6.refs_0_), channel_id=1, source_target_pairs={{0,96},{16,112},{32,0},{48,16},{64,32},{80,48},{96,64},{112,80},{1... | collective-permute-start | bytes 393224 | tf_op jit(solution)/shard_map/ppermute | solution.py:101
  71.9 19.8 %collective-permute-start.5 = (bf16[64,1024]{1,0:T(8,128)(2,1)S(1)}, bf16[64,1024]{1,0:T(8,128)(2,1)S(1)}, u32[]{:S(2)}, u32[]{:S(2)}) collective-permute-start(bf16[64,1024]{1,0:T(8,128)(2,1)S(1)} %get-tuple-element.6.refs_0_), channel_id=1, source_target_pairs={{0,80},{16,96},{32,112},{48,0},{64,16},{80,32},{96,48},{112,64},{1... | collective-permute-start | bytes 393224 | tf_op jit(solution)/shard_map/ppermute | solution.py:101
  77.2 14.5 %collective-permute-start.4 = (bf16[64,1024]{1,0:T(8,128)(2,1)S(1)}, bf16[64,1024]{1,0:T(8,128)(2,1)S(1)}, u32[]{:S(2)}, u32[]{:S(2)}) collective-permute-start(bf16[64,1024]{1,0:T(8,128)(2,1)S(1)} %get-tuple-element.6.refs_0_), channel_id=1, source_target_pairs={{0,64},{16,80},{32,96},{48,112},{64,0},{80,16},{96,32},{112,48},{1... | collective-permute-start | bytes 393224 | tf_op jit(solution)/shard_map/ppermute | solution.py:101
  81.3 20.3 %collective-permute-start.3 = (bf16[64,1024]{1,0:T(8,128)(2,1)S(1)}, bf16[64,1024]{1,0:T(8,128)(2,1)S(1)}, u32[]{:S(2)}, u32[]{:S(2)}) collective-permute-start(bf16[64,1024]{1,0:T(8,128)(2,1)S(1)} %get-tuple-element.6.refs_0_), channel_id=1, source_target_pairs={{0,48},{16,64},{32,80},{48,96},{64,112},{80,0},{96,16},{112,32},{1... | collective-permute-start | bytes 393224 | tf_op jit(solution)/shard_map/ppermute | solution.py:101
  84.2 17.4 %collective-permute-start.2 = (bf16[64,1024]{1,0:T(8,128)(2,1)S(1)}, bf16[64,1024]{1,0:T(8,128)(2,1)S(1)}, u32[]{:S(2)}, u32[]{:S(2)}) collective-permute-start(bf16[64,1024]{1,0:T(8,128)(2,1)S(1)} %get-tuple-element.6.refs_0_), channel_id=1, source_target_pairs={{0,32},{16,48},{32,64},{48,80},{64,96},{80,112},{96,0},{112,16},{1... | collective-permute-start | bytes 393224 | tf_op jit(solution)/shard_map/ppermute | solution.py:101
  89.7 16.5 %collective-permute-start.1 = (bf16[64,1024]{1,0:T(8,128)(2,1)S(1)}, bf16[64,1024]{1,0:T(8,128)(2,1)S(1)}, u32[]{:S(2)}, u32[]{:S(2)}) collective-permute-start(bf16[64,1024]{1,0:T(8,128)(2,1)S(1)} %get-tuple-element.6.refs_0_), channel_id=1, source_target_pairs={{0,16},{16,32},{32,48},{48,64},{64,80},{80,96},{96,112},{112,0},{1... | collective-permute-start | bytes 393224 | tf_op jit(solution)/shard_map/ppermute | solution.py:101

commit v6 on v5

v6 whole, which is shorter than its diff:
```python
import jax
import jax.numpy as jnp
from jax import lax
from jax.experimental import pallas as pl
from jax.experimental.pallas import tpu as pltpu
from jax.sharding import Mesh, PartitionSpec as P

B = 128
AXES = ("z", "y", "w", "u", "v", "core")


def product_kernel(z_ref, left_ref, *refs):
    *right_refs, out_ref, ordered = refs
    n, depth, step = left_ref.shape
    z = z_ref[0]

    @pl.when(pl.program_id(0) == 0)
    def _():
        for s, piece in enumerate(right_refs):
            ordered[lax.rem(z - s + n, n)] = piece[...]

    total = lax.dot_general(
        left_ref[...].reshape(n * depth, step),
        ordered[...].reshape(n * depth, ordered.shape[2]),
        (((0,), (0,)), ((), ())),
        preferred_element_type=jnp.float32,
    )
    for a in range(out_ref.shape[0]):
        out_ref[a, 0] = total[a * B : (a + 1) * B]


def product(left, rights, z, cores):
    n, depth, wide = left.shape
    panel = rights[0].shape[1]
    step = cores * B
    return pl.pallas_call(
        product_kernel,
        grid_spec=pltpu.PrefetchScalarGridSpec(
            num_scalar_prefetch=1,
            grid=(wide // step,),
            in_specs=[pl.BlockSpec((n, depth, step), lambda m, _: (0, 0, m))]
            + [pl.BlockSpec((depth, panel), lambda m, _: (0, 0)) for _ in rights],
            out_specs=pl.BlockSpec((cores, 1, B, panel), lambda m, _: (0, m, 0, 0)),
            scratch_shapes=[pltpu.VMEM((n, depth, panel), left.dtype)],
        ),
        out_shape=jax.ShapeDtypeStruct((cores, wide // step, B, panel), jnp.float32),
        compiler_params=pltpu.CompilerParams(vmem_limit_bytes=24 * 1024 * 1024),
        cost_estimate=pl.CostEstimate(
            flops=2 * n * depth * wide * panel,
            bytes_accessed=2 * n * depth * (wide + panel) + 4 * wide * panel,
            transcendentals=0,
        ),
        name="product",
    )(z.reshape(1), left, *rights)


def body(stored, pattern):
    nz, ny, nw, nu, nv, ncore = (lax.axis_size(a) for a in AXES)
    z, y, w, u, v, core = (lax.axis_index(a) for a in AXES)
    nl = nu * nv * ncore
    l = (u * nv + v) * ncore + core
    g = z * nl + l
    plane = nl * B
    panel = plane // nw

    raw = lax.dynamic_slice(stored, (0, y * plane), (B, plane))
    present = lax.dynamic_slice(pattern, (g, y * nl), (1, nl))
    present = jnp.repeat(present, B, axis=1) > 0
    row = g * B + jnp.arange(B, dtype=jnp.int32)[:, None]
    column = y * plane + jnp.arange(plane, dtype=jnp.int32)[None, :]
    band = jnp.where(present & (column >= row), raw, jnp.zeros((), raw.dtype))

    def flat(zz, yy, r):
        return (zz * ny + yy) * (nw * nl) + r

    mirror = [
        (flat(a, b, r), flat(b, a, r))
        for a in range(nz)
        for b in range(a + 1, ny)
        for r in range(nw * nl)
    ]

    turned = band.T.reshape(nl, B, B)
    crossed = lax.all_to_all(turned, ("u", "v", "core"), split_axis=0, concat_axis=0, tiled=True)
    crossed = crossed.transpose(1, 0, 2).reshape(B, plane)
    mirrored = lax.ppermute(band, AXES, mirror)
    half = lax.dynamic_slice(crossed, (0, w * panel), (B, panel))
    mirrored_half = lax.ppermute(half, AXES, mirror)

    diagonal = z == y
    offset = l * B + jnp.arange(B, dtype=jnp.int32)[:, None]
    across = jnp.arange(plane, dtype=jnp.int32)[None, :]
    left = jnp.where(
        y * plane + offset <= z * plane + across, jnp.where(diagonal, band, mirrored), crossed
    )
    own = y * plane + w * panel + jnp.arange(panel, dtype=jnp.int32)[None, :]
    right = jnp.where(
        z * plane + offset <= own,
        lax.dynamic_slice(band, (0, w * panel), (B, panel)),
        jnp.where(diagonal, half, mirrored_half),
    )

    left = jnp.broadcast_to(left[None], (ny, B, plane))
    left = lax.all_to_all(left, "y", split_axis=0, concat_axis=0, tiled=True)
    rights = [right] + [lax.ppermute(right, "z", [(a, (a + s) % nz) for a in range(nz)]) for s in range(1, nz)]

    partial = product(left, rights, z, ncore)
    partial = jnp.sum(lax.all_to_all(partial, "core", split_axis=0, concat_axis=0, tiled=True), axis=0)
    partial = jnp.sum(lax.all_to_all(partial, ("u", "v"), split_axis=0, concat_axis=0, tiled=True), axis=0)
    return partial.astype(jnp.bfloat16)


def solution(mesh):
    finer = Mesh(mesh.devices.reshape(8, 8, 2, 2, 2, 2), AXES)
    return jax.shard_map(
        body,
        mesh=finer,
        in_specs=(P(("z", "u", "v", "core"), None), P()),
        out_specs=P(("z", "u", "v", "core"), ("y", "w")),
        check_vma=False,
    )
```

time: 158 us -> 199 us (1.26)
  starting transfers between devices: 78.3 us -> 128 us
  blocking collectives: 42.7 us -> 38.9 us
  other arithmetic: 8.26 us -> 5.39 us
  waiting for transfers between devices: 22.6 us -> 20.6 us
    ppermute x8 -> x9, starting transfers between devices: 24.2 us -> 85 us  [the longest x7 83.7 us: body(): lax.ppermute(right, 'z', [(a, (a + s) % nz) for a in range(nz)])]
    all_to_all x1, starting transfers between devices: 36.6 us -> 25.8 us  [body(): left = lax.all_to_all(left, 'y', split_axis=0, concat_axis=0, tiled=True)]
    all_to_all x1, blocking collectives: 9.19 us -> 6.09 us  [body(): lax.all_to_all(partial, 'core', split_axis=0, concat_axis=0, tiled=True)]
    reduce_sum x1, other arithmetic: 2.87 us -> 0.27 us  [body(): jnp.sum(lax.all_to_all(partial, 'core', split_axis=0, concat_axis=0, tile...]
    ppermute x8 -> x9, waiting for transfers between devices: 14.5 us -> 12.8 us  [the longest x7 12.8 us: body(): lax.ppermute(right, 'z', [(a, (a + s) % nz) for a in range(nz)])]
  transfers between devices with their start and end apart: 10 -> 11, of which waited for: 3 -> 4; matrix products, arithmetic and copies ran while one was open for 0% -> 1% of each run, Pallas kernels for 0% -> 0%
where the time goes in v6:
time: 199 us; the launch traced here: 198 us
  starting transfers between devices  128 us (64%)
  blocking collectives  38.9 us (20%)
  waiting for transfers between devices  20.6 us (10%)
  other arithmetic  5.39 us (3%)
  local copies, waits for them, and re-layouts  2.57 us (1%)
  Pallas kernels  2.45 us (1%)
    ppermute x7, starting transfers between devices, body(): lax.ppermute(right, 'z', [(a, (a + s) % nz) for a in range(nz)])  83.7 us
    all_to_all x1, blocking collectives, body(): lax.all_to_all(partial, ('u', 'v'), split_axis=0, concat_axis=0, tiled=True)  32.8 us
    all_to_all x1, starting transfers between devices, body(): left = lax.all_to_all(left, 'y', split_axis=0, concat_axis=0, tiled=True)  25.8 us
    all_to_all x1, starting transfers between devices, body(): lax.all_to_all(turned, ('u', 'v', 'core'), split_axis=0, concat_axis=0, t...  17.5 us
    ppermute x7, waiting for transfers between devices, body(): lax.ppermute(right, 'z', [(a, (a + s) % nz) for a in range(nz)])  12.8 us
    all_to_all x1, waiting for transfers between devices, body(): lax.all_to_all(turned, ('u', 'v', 'core'), split_axis=0, concat_axis=0, t...  7.84 us
    all_to_all x1, blocking collectives, body(): lax.all_to_all(partial, 'core', split_axis=0, concat_axis=0, tiled=True)  6.09 us
  transfers between devices with their start and end apart: 11, of which 4 were waited for; matrix products, arithmetic and copies ran while one was open for 1% of the time, Pallas kernels for 0%

profile of v6, /device:TPU:1, one launch (start us, length us, event | category | flops | bytes accessed | tf_op | source)
XLA Modules:
  0.0 198.5 jit_solution(18340563206634669771)
XLA Ops:
  0.0 0.8 compare_bitcast_fusion
  0.8 0.1 broadcast_bitcast_fusion
  0.8 1.1 fusion.2
  2.0 0.8 copy.8
  2.8 17.5 %all-to-all-start = ((bf16[8,128,128]{2,1,0:T(8,128)(2,1)}), bf16[8,128,128]{2,1,0:T(8,128)(2,1)S(1)}, u32[]{:S(2)}, u32[]{:S(2)}) async-start(bf16[8,128,128]{2,1,0:T(8,128)(2,1)} %bitcast.4), calls=%async_computation | async-start | bytes 524288 | tf_op jit(solution)/shard_map/all_to_all | solution.py:84
  20.3 1.1 and_select_fusion
  21.4 0.7 collective-permute-start
  22.1 0.0 collective-permute-done
  22.1 7.8 %all-to-all-done = bf16[8,128,128]{2,1,0:T(8,128)(2,1)S(1)} async-done(((bf16[8,128,128]{2,1,0:T(8,128)(2,1)}), bf16[8,128,128]{2,1,0:T(8,128)(2,1)S(1)}, u32[]{:S(2)}, u32[]{:S(2)}) %all-to-all-start) | async-done | bytes 262176 | tf_op jit(solution)/shard_map/all_to_all | solution.py:84
  30.0 1.2 compare_select_fusion
  31.2 1.6 broadcast_in_dim.10
  32.8 25.8 %all-to-all-start.1 = ((bf16[8,128,1024]{2,1,0:T(8,128)(2,1)}), bf16[8,128,1024]{2,1,0:T(8,128)(2,1)S(1)}, u32[]{:S(2)}, u32[]{:S(2)}) async-start(bf16[8,128,1024]{2,1,0:T(8,128)(2,1)} %broadcast_in_dim.10), calls=%async_computation.1 | async-start | bytes 4194304 | tf_op jit(solution)/shard_map/all_to_all | solution.py:104
  58.7 0.7 collective-permute-start.1
  59.4 0.0 collective-permute-done.1
  59.4 0.1 compare_select_fusion.1.refs_0_
  59.5 59.6 %collective-permute-start.2 = (bf16[128,512]{1,0:T(8,128)(2,1)S(1)}, bf16[128,512]{1,0:T(8,128)(2,1)S(1)}, u32[]{:S(2)}, u32[]{:S(2)}) collective-permute-start(bf16[128,512]{1,0:T(8,128)(2,1)S(1)} %compare_select_fusion.1.refs_0_), channel_id=1, source_target_pairs={{0,128},{128,256},{256,384},{384,512},{512,640},{640,768},{768,896... | collective-permute-start | bytes 393224 | tf_op jit(solution)/shard_map/ppermute | solution.py:105
  119.1 1.9 collective-permute-start.3
  121.0 7.0 %collective-permute-start.4 = (bf16[128,512]{1,0:T(8,128)(2,1)S(1)}, bf16[128,512]{1,0:T(8,128)(2,1)S(1)}, u32[]{:S(2)}, u32[]{:S(2)}) collective-permute-start(bf16[128,512]{1,0:T(8,128)(2,1)S(1)} %compare_select_fusion.1.refs_0_), channel_id=1, source_target_pairs={{0,384},{128,512},{256,640},{384,768},{512,896},{640,0},{768,128},... | collective-permute-start | bytes 393224 | tf_op jit(solution)/shard_map/ppermute | solution.py:105
  128.1 3.2 %collective-permute-start.5 = (bf16[128,512]{1,0:T(8,128)(2,1)S(1)}, bf16[128,512]{1,0:T(8,128)(2,1)S(1)}, u32[]{:S(2)}, u32[]{:S(2)}) collective-permute-start(bf16[128,512]{1,0:T(8,128)(2,1)S(1)} %compare_select_fusion.1.refs_0_), channel_id=1, source_target_pairs={{0,512},{128,640},{256,768},{384,896},{512,0},{640,128},{768,256},... | collective-permute-start | bytes 393224 | tf_op jit(solution)/shard_map/ppermute | solution.py:105
  131.3 6.4 %collective-permute-start.6 = (bf16[128,512]{1,0:T(8,128)(2,1)S(1)}, bf16[128,512]{1,0:T(8,128)(2,1)S(1)}, u32[]{:S(2)}, u32[]{:S(2)}) collective-permute-start(bf16[128,512]{1,0:T(8,128)(2,1)S(1)} %compare_select_fusion.1.refs_0_), channel_id=1, source_target_pairs={{0,640},{128,768},{256,896},{384,0},{512,128},{640,256},{768,384},... | collective-permute-start | bytes 393224 | tf_op jit(solution)/shard_map/ppermute | solution.py:105
  137.7 0.0 collective-permute-done.2.refs_1_
  137.7 2.2 %collective-permute-start.7 = (bf16[128,512]{1,0:T(8,128)(2,1)S(1)}, bf16[128,512]{1,0:T(8,128)(2,1)S(1)}, u32[]{:S(2)}, u32[]{:S(2)}) collective-permute-start(bf16[128,512]{1,0:T(8,128)(2,1)S(1)} %compare_select_fusion.1.refs_0_), channel_id=1, source_target_pairs={{0,768},{128,896},{256,0},{384,128},{512,256},{640,384},{768,512},... | collective-permute-start | bytes 393224 | tf_op jit(solution)/shard_map/ppermute | solution.py:105
  139.9 0.0 collective-permute-done.3.refs_2_
  139.9 3.4 %collective-permute-start.8 = (bf16[128,512]{1,0:T(8,128)(2,1)S(1)}, bf16[128,512]{1,0:T(8,128)(2,1)S(1)}, u32[]{:S(2)}, u32[]{:S(2)}) collective-permute-start(bf16[128,512]{1,0:T(8,128)(2,1)S(1)} %compare_select_fusion.1.refs_0_), channel_id=1, source_target_pairs={{0,896},{128,0},{256,128},{384,256},{512,384},{640,512},{768,640},... | collective-permute-start | bytes 393224 | tf_op jit(solution)/shard_map/ppermute | solution.py:105
  143.3 0.0 collective-permute-done.4.refs_3_
  143.3 0.8 collective-permute-done.5.refs_4_
  144.1 0.0 collective-permute-done.6.refs_5_
  144.1 11.4 %collective-permute-done.7.refs_6_ = bf16[128,512]{1,0:T(8,128)(2,1)S(1)} collective-permute-done((bf16[128,512]{1,0:T(8,128)(2,1)S(1)}, bf16[128,512]{1,0:T(8,128)(2,1)S(1)}, u32[]{:S(2)}, u32[]{:S(2)}) %collective-permute-start.7) | collective-permute-done | bytes 131104 | tf_op jit(solution)/shard_map/ppermute | solution.py:105
  155.4 0.6 collective-permute-done.8.refs_7_
  156.1 0.0 all-to-all-done.1.left_ref
  156.1 2.4 %product.1 = f32[2,4,128,512]{3,2,1,0:T(8,128)S(1)} custom-call(s32[1]{0:T(128)} %bitcast.z_ref, bf16[8,128,1024]{2,1,0:T(8,128)(2,1)S(1)} %all-to-all-done.1.left_ref, bf16[128,512]{1,0:T(8,128)(2,1)S(1)} %compare_select_fusion.1.refs_0_, bf16[128,512]{1,0:T(8,128)(2,1)S(1)} %collective-permute-done.2.refs_1_, ...), custom_call_target="tpu_custom_call" | custom-call | flops 1073741824 | bytes 5242880 | tf_op jit(solution)/shard_map/product/pallas_call | solution.py:36
  158.5 6.1 %all_to_all.20 = f32[2,4,128,512]{3,2,1,0:T(8,128)S(1)} all-to-all(f32[2,4,128,512]{3,2,1,0:T(8,128)S(1)} %product.1), channel_id=1, replica_groups=mesh['z'=8,'y'=8,'w'=2,'u'=2,'v'=2,'core'=2] {'core'}, dimensions={0} | all-to-all | bytes 4194304 | tf_op jit(solution)/shard_map/all_to_all | solution.py:108
  164.6 0.3 reduce_sum.18
  164.9 32.8 %all_to_all.21 = f32[4,128,512]{2,1,0:T(8,128)S(1)} all-to-all(f32[4,128,512]{2,1,0:T(8,128)S(1)} %reduce_sum.18), channel_id=1, replica_groups=mesh['z'=8,'y'=8,'w'=2,'u'=2,'v'=2,'core'=2] {'u','v'}, dimensions={0} | all-to-all | bytes 2097152 | tf_op jit(solution)/shard_map/all_to_all | solution.py:109
  197.7 0.8 reduce_sum.19
  (8 shorter events, 0.1 us)
Async XLA Ops:
  2.8 27.2 %all-to-all-start = ((bf16[8,128,128]{2,1,0:T(8,128)(2,1)}), bf16[8,128,128]{2,1,0:T(8,128)(2,1)S(1)}, u32[]{:S(2)}, u32[]{:S(2)}) async-start(bf16[8,128,128]{2,1,0:T(8,128)(2,1)} %bitcast.4), calls=%async_computation | async-start | bytes 524288 | tf_op jit(solution)/shard_map/all_to_all | solution.py:84
  21.4 0.7 collective-permute-start
  32.8 123.2 %all-to-all-start.1 = ((bf16[8,128,1024]{2,1,0:T(8,128)(2,1)}), bf16[8,128,1024]{2,1,0:T(8,128)(2,1)S(1)}, u32[]{:S(2)}, u32[]{:S(2)}) async-start(bf16[8,128,1024]{2,1,0:T(8,128)(2,1)} %broadcast_in_dim.10), calls=%async_computation.1 | async-start | bytes 4194304 | tf_op jit(solution)/shard_map/all_to_all | solution.py:104
  58.7 0.7 collective-permute-start.1
  59.5 78.2 %collective-permute-start.2 = (bf16[128,512]{1,0:T(8,128)(2,1)S(1)}, bf16[128,512]{1,0:T(8,128)(2,1)S(1)}, u32[]{:S(2)}, u32[]{:S(2)}) collective-permute-start(bf16[128,512]{1,0:T(8,128)(2,1)S(1)} %compare_select_fusion.1.refs_0_), channel_id=1, source_target_pairs={{0,128},{128,256},{256,384},{384,512},{512,640},{640,768},{768,896... | collective-permute-start | bytes 393224 | tf_op jit(solution)/shard_map/ppermute | solution.py:105
  119.1 20.8 %collective-permute-start.3 = (bf16[128,512]{1,0:T(8,128)(2,1)S(1)}, bf16[128,512]{1,0:T(8,128)(2,1)S(1)}, u32[]{:S(2)}, u32[]{:S(2)}) collective-permute-start(bf16[128,512]{1,0:T(8,128)(2,1)S(1)} %compare_select_fusion.1.refs_0_), channel_id=1, source_target_pairs={{0,256},{128,384},{256,512},{384,640},{512,768},{640,896},{768,0},... | collective-permute-start | bytes 393224 | tf_op jit(solution)/shard_map/ppermute | solution.py:105
  121.0 22.3 %collective-permute-start.4 = (bf16[128,512]{1,0:T(8,128)(2,1)S(1)}, bf16[128,512]{1,0:T(8,128)(2,1)S(1)}, u32[]{:S(2)}, u32[]{:S(2)}) collective-permute-start(bf16[128,512]{1,0:T(8,128)(2,1)S(1)} %compare_select_fusion.1.refs_0_), channel_id=1, source_target_pairs={{0,384},{128,512},{256,640},{384,768},{512,896},{640,0},{768,128},... | collective-permute-start | bytes 393224 | tf_op jit(solution)/shard_map/ppermute | solution.py:105
  128.1 16.0 %collective-permute-start.5 = (bf16[128,512]{1,0:T(8,128)(2,1)S(1)}, bf16[128,512]{1,0:T(8,128)(2,1)S(1)}, u32[]{:S(2)}, u32[]{:S(2)}) collective-permute-start(bf16[128,512]{1,0:T(8,128)(2,1)S(1)} %compare_select_fusion.1.refs_0_), channel_id=1, source_target_pairs={{0,512},{128,640},{256,768},{384,896},{512,0},{640,128},{768,256},... | collective-permute-start | bytes 393224 | tf_op jit(solution)/shard_map/ppermute | solution.py:105
  131.3 12.7 %collective-permute-start.6 = (bf16[128,512]{1,0:T(8,128)(2,1)S(1)}, bf16[128,512]{1,0:T(8,128)(2,1)S(1)}, u32[]{:S(2)}, u32[]{:S(2)}) collective-permute-start(bf16[128,512]{1,0:T(8,128)(2,1)S(1)} %compare_select_fusion.1.refs_0_), channel_id=1, source_target_pairs={{0,640},{128,768},{256,896},{384,0},{512,128},{640,256},{768,384},... | collective-permute-start | bytes 393224 | tf_op jit(solution)/shard_map/ppermute | solution.py:105
  137.7 17.7 %collective-permute-start.7 = (bf16[128,512]{1,0:T(8,128)(2,1)S(1)}, bf16[128,512]{1,0:T(8,128)(2,1)S(1)}, u32[]{:S(2)}, u32[]{:S(2)}) collective-permute-start(bf16[128,512]{1,0:T(8,128)(2,1)S(1)} %compare_select_fusion.1.refs_0_), channel_id=1, source_target_pairs={{0,768},{128,896},{256,0},{384,128},{512,256},{640,384},{768,512},... | collective-permute-start | bytes 393224 | tf_op jit(solution)/shard_map/ppermute | solution.py:105
  139.9 16.2 %collective-permute-start.8 = (bf16[128,512]{1,0:T(8,128)(2,1)S(1)}, bf16[128,512]{1,0:T(8,128)(2,1)S(1)}, u32[]{:S(2)}, u32[]{:S(2)}) collective-permute-start(bf16[128,512]{1,0:T(8,128)(2,1)S(1)} %compare_select_fusion.1.refs_0_), channel_id=1, source_target_pairs={{0,896},{128,0},{256,128},{384,256},{512,384},{640,512},{768,640},... | collective-permute-start | bytes 393224 | tf_op jit(solution)/shard_map/ppermute | solution.py:105

commit v7 on v5

--- a/solution.py
+++ b/solution.py
@@ -74,28 +74,30 @@
     def flat(zz, yy, r):
         return (zz * ny + yy) * (nw * nl) + r
 
-    mirrored = lax.ppermute(
-        band,
-        AXES,
-        [
-            (flat(a, b, r), flat(b, a, r))
-            for a in range(nz)
-            for b in range(a + 1, ny)
-            for r in range(nw * nl)
-        ],
-    )
-    own = jnp.where(z <= y, band, mirrored)
-    turned = own.T.reshape(nl, nw, part, B)
+    mirror = [
+        (flat(a, b, r), flat(b, a, r))
+        for a in range(nz)
+        for b in range(a + 1, ny)
+        for r in range(nw * nl)
+    ]
+
+    turned = band.T.reshape(nl, nw, part, B)
     turned = lax.dynamic_index_in_dim(turned, w, 1, keepdims=False)
     crossed = lax.all_to_all(turned, ("u", "v", "core"), split_axis=0, concat_axis=0, tiled=True)
+    straight = lax.dynamic_slice(band, (w * part, 0), (part, plane))
+    straight_mirrored = lax.ppermute(straight, AXES, mirror)
+    crossed, straight_mirrored = lax.optimization_barrier((crossed, straight_mirrored))
     crossed = crossed.transpose(1, 0, 2).reshape(part, plane)
-    straight = lax.dynamic_slice(own, (w * part, 0), (part, plane))
+    crossed_mirrored = lax.ppermute(crossed, AXES, mirror)
+    straight = jnp.where(z <= y, straight, straight_mirrored)
+    crossed = jnp.where(z <= y, crossed, crossed_mirrored)
 
     offset = l * B + w * part + jnp.arange(part, dtype=jnp.int32)[:, None]
     across = jnp.arange(plane, dtype=jnp.int32)[None, :]
     left = jnp.where(y * plane + offset <= z * plane + across, straight, crossed)
     right = jnp.where(z * plane + offset <= y * plane + across, straight, crossed)
 
+    left, right = lax.optimization_barrier((left, right))
     right = jnp.broadcast_to(right[None], (nz, part, plane))
     right = lax.all_to_all(right, "z", split_axis=0, concat_axis=0, tiled=True)
     lefts = [left] + [lax.ppermute(left, "y", [(a, (a + s) % ny) for a in range(ny)]) for s in range(1, ny)]

time: 158 us -> 159 us (level)
  blocking collectives: 42.7 us -> 45.1 us
    all_to_all x1, blocking collectives: 33.5 us -> 36.4 us  [body(): lax.all_to_all(sent, ('u', 'v', 'w'), split_axis=0, concat_axis=0, tiled=...]
    all_to_all x1, waiting for transfers between devices: 8.02 us -> 6.17 us  [body(): lax.all_to_all(turned, ('u', 'v', 'core'), split_axis=0, concat_axis=0, t...]
  transfers between devices with their start and end apart: 10 -> 11, of which waited for: 3 -> 3; matrix products, arithmetic and copies ran while one was open for 0% -> 1% of each run, Pallas kernels for 0% -> 0%
where the time goes in v7:
time: 159 us
  starting transfers between devices  77.8 us (49%)
  blocking collectives  45.1 us (28%)
  waiting for transfers between devices  21.8 us (14%)
  other arithmetic  8.19 us (5%)
  Pallas kernels  2.51 us (2%)
  local copies, waits for them, and re-layouts  2.3 us (1%)
    all_to_all x1, blocking collectives, body(): lax.all_to_all(sent, ('u', 'v', 'w'), split_axis=0, concat_axis=0, tiled=...  36.4 us
    all_to_all x1, starting transfers between devices, body(): right = lax.all_to_all(right, 'z', split_axis=0, concat_axis=0, tiled=True)  36.1 us
    ppermute x7, starting transfers between devices, body(): lax.ppermute(left, 'y', [(a, (a + s) % ny) for a in range(ny)])  22.9 us
    all_to_all x1, starting transfers between devices, body(): lax.all_to_all(turned, ('u', 'v', 'core'), split_axis=0, concat_axis=0, t...  17.4 us
    ppermute x7, waiting for transfers between devices, body(): lax.ppermute(left, 'y', [(a, (a + s) % ny) for a in range(ny)])  15.6 us
    all_to_all x1, blocking collectives, body(): lax.all_to_all(partial, 'core', split_axis=0, concat_axis=0, tiled=True)  8.68 us
    all_to_all x1, waiting for transfers between devices, body(): lax.all_to_all(turned, ('u', 'v', 'core'), split_axis=0, concat_axis=0, t...  6.17 us
  transfers between devices with their start and end apart: 11, of which 3 were waited for; matrix products, arithmetic and copies ran while one was open for 1% of the time, Pallas kernels for 0%

profile of v7, /device:TPU:1, one launch (start us, length us, event | category | flops | bytes accessed | tf_op | source)
XLA Modules:
  0.0 158.7 jit_solution(12061166576511750961)
XLA Ops:
  0.0 0.8 compare_bitcast_fusion
  0.8 0.1 broadcast_bitcast_fusion
  0.9 1.1 fusion.5
  2.0 0.2 copy.7
  2.2 0.7 dynamic-slice_bitcast_fusion
  2.8 17.4 %all-to-all-start = ((bf16[8,64,128]{2,1,0:T(8,128)(2,1)}), bf16[8,64,128]{2,1,0:T(8,128)(2,1)S(1)}, u32[]{:S(2)}, u32[]{:S(2)}) async-start(bf16[8,64,128]{2,1,0:T(8,128)(2,1)} %dynamic-slice_bitcast_fusion), calls=%async_computation | async-start | bytes 262144 | tf_op jit(solution)/shard_map/all_to_all | solution.py:86
  20.3 1.1 and_select_fusion
  21.4 0.7 collective-permute-start
  22.1 0.0 collective-permute-done
  22.1 6.2 %all-to-all-done = bf16[8,64,128]{2,1,0:T(8,128)(2,1)S(1)} async-done(((bf16[8,64,128]{2,1,0:T(8,128)(2,1)}), bf16[8,64,128]{2,1,0:T(8,128)(2,1)S(1)}, u32[]{:S(2)}, u32[]{:S(2)}) %all-to-all-start) | async-done | bytes 131104 | tf_op jit(solution)/shard_map/all_to_all | solution.py:86
  28.3 0.7 collective-permute-start.1
  29.0 0.0 collective-permute-done.1
  29.0 0.1 compare_select_fusion
  29.2 1.1 broadcast_in_dim.10
  30.3 36.1 %all-to-all-start.1 = ((bf16[8,64,1024]{2,1,0:T(8,128)(2,1)}), bf16[8,64,1024]{2,1,0:T(8,128)(2,1)S(1)}, u32[]{:S(2)}, u32[]{:S(2)}) async-start(bf16[8,64,1024]{2,1,0:T(8,128)(2,1)} %broadcast_in_dim.10), calls=%async_computation.1 | async-start | bytes 2097152 | tf_op jit(solution)/shard_map/all_to_all | solution.py:102
  66.4 1.9 %collective-permute-start.8 = (bf16[64,1024]{1,0:T(8,128)(2,1)S(1)}, bf16[64,1024]{1,0:T(8,128)(2,1)S(1)}, u32[]{:S(2)}, u32[]{:S(2)}) collective-permute-start(bf16[64,1024]{1,0:T(8,128)(2,1)S(1)} %get-tuple-element.11.refs_0_), channel_id=1, source_target_pairs={{0,112},{16,0},{32,16},{48,32},{64,48},{80,64},{96,80},{112,96},{1... | collective-permute-start | bytes 393224 | tf_op jit(solution)/shard_map/ppermute | solution.py:103
  68.3 1.9 %collective-permute-start.7 = (bf16[64,1024]{1,0:T(8,128)(2,1)S(1)}, bf16[64,1024]{1,0:T(8,128)(2,1)S(1)}, u32[]{:S(2)}, u32[]{:S(2)}) collective-permute-start(bf16[64,1024]{1,0:T(8,128)(2,1)S(1)} %get-tuple-element.11.refs_0_), channel_id=1, source_target_pairs={{0,96},{16,112},{32,0},{48,16},{64,32},{80,48},{96,64},{112,80},{1... | collective-permute-start | bytes 393224 | tf_op jit(solution)/shard_map/ppermute | solution.py:103
  70.2 5.8 %collective-permute-start.6 = (bf16[64,1024]{1,0:T(8,128)(2,1)S(1)}, bf16[64,1024]{1,0:T(8,128)(2,1)S(1)}, u32[]{:S(2)}, u32[]{:S(2)}) collective-permute-start(bf16[64,1024]{1,0:T(8,128)(2,1)S(1)} %get-tuple-element.11.refs_0_), channel_id=1, source_target_pairs={{0,80},{16,96},{32,112},{48,0},{64,16},{80,32},{96,48},{112,64},{1... | collective-permute-start | bytes 393224 | tf_op jit(solution)/shard_map/ppermute | solution.py:103
  76.1 3.6 %collective-permute-start.5 = (bf16[64,1024]{1,0:T(8,128)(2,1)S(1)}, bf16[64,1024]{1,0:T(8,128)(2,1)S(1)}, u32[]{:S(2)}, u32[]{:S(2)}) collective-permute-start(bf16[64,1024]{1,0:T(8,128)(2,1)S(1)} %get-tuple-element.11.refs_0_), channel_id=1, source_target_pairs={{0,64},{16,80},{32,96},{48,112},{64,0},{80,16},{96,32},{112,48},{1... | collective-permute-start | bytes 393224 | tf_op jit(solution)/shard_map/ppermute | solution.py:103
  79.7 3.2 %collective-permute-start.4 = (bf16[64,1024]{1,0:T(8,128)(2,1)S(1)}, bf16[64,1024]{1,0:T(8,128)(2,1)S(1)}, u32[]{:S(2)}, u32[]{:S(2)}) collective-permute-start(bf16[64,1024]{1,0:T(8,128)(2,1)S(1)} %get-tuple-element.11.refs_0_), channel_id=1, source_target_pairs={{0,48},{16,64},{32,80},{48,96},{64,112},{80,0},{96,16},{112,32},{1... | collective-permute-start | bytes 393224 | tf_op jit(solution)/shard_map/ppermute | solution.py:103
  82.9 0.0 collective-permute-done.8.refs_7_
  82.9 3.0 %collective-permute-start.3 = (bf16[64,1024]{1,0:T(8,128)(2,1)S(1)}, bf16[64,1024]{1,0:T(8,128)(2,1)S(1)}, u32[]{:S(2)}, u32[]{:S(2)}) collective-permute-start(bf16[64,1024]{1,0:T(8,128)(2,1)S(1)} %get-tuple-element.11.refs_0_), channel_id=1, source_target_pairs={{0,32},{16,48},{32,64},{48,80},{64,96},{80,112},{96,0},{112,16},{1... | collective-permute-start | bytes 393224 | tf_op jit(solution)/shard_map/ppermute | solution.py:103
  85.9 0.0 collective-permute-done.7.refs_6_
  85.9 3.5 %collective-permute-start.2 = (bf16[64,1024]{1,0:T(8,128)(2,1)S(1)}, bf16[64,1024]{1,0:T(8,128)(2,1)S(1)}, u32[]{:S(2)}, u32[]{:S(2)}) collective-permute-start(bf16[64,1024]{1,0:T(8,128)(2,1)S(1)} %get-tuple-element.11.refs_0_), channel_id=1, source_target_pairs={{0,16},{16,32},{32,48},{48,64},{64,80},{80,96},{96,112},{112,0},{1... | collective-permute-start | bytes 393224 | tf_op jit(solution)/shard_map/ppermute | solution.py:103
  89.4 0.0 collective-permute-done.6.refs_5_
  89.4 0.0 collective-permute-done.5.refs_4_
  89.4 10.1 %collective-permute-done.4.refs_3_ = bf16[64,1024]{1,0:T(8,128)(2,1)S(1)} collective-permute-done((bf16[64,1024]{1,0:T(8,128)(2,1)S(1)}, bf16[64,1024]{1,0:T(8,128)(2,1)S(1)}, u32[]{:S(2)}, u32[]{:S(2)}) %collective-permute-start.4) | collective-permute-done | bytes 131104 | tf_op jit(solution)/shard_map/ppermute | solution.py:103
  99.6 0.0 collective-permute-done.3.refs_2_
  99.6 5.5 %collective-permute-done.2.refs_1_ = bf16[64,1024]{1,0:T(8,128)(2,1)S(1)} collective-permute-done((bf16[64,1024]{1,0:T(8,128)(2,1)S(1)}, bf16[64,1024]{1,0:T(8,128)(2,1)S(1)}, u32[]{:S(2)}, u32[]{:S(2)}) %collective-permute-start.2) | collective-permute-done | bytes 131104 | tf_op jit(solution)/shard_map/ppermute | solution.py:103
  105.1 0.0 all-to-all-done.1.refs_8_
  105.1 2.5 %product.1 = f32[2,8,128,512]{3,2,1,0:T(8,128)S(1)} custom-call(s32[1]{0:T(128)} %bitcast.y_ref, bf16[64,1024]{1,0:T(8,128)(2,1)S(1)} %get-tuple-element.11.refs_0_, bf16[64,1024]{1,0:T(8,128)(2,1)S(1)} %collective-permute-done.2.refs_1_, bf16[64,1024]{1,0:T(8,128)(2,1)S(1)} %collective-permute-done.3.refs_2_, ...), custom_call_target="tpu_custom_call" | custom-call | flops 1073741824 | bytes 6291456 | tf_op jit(solution)/shard_map/product/pallas_call | solution.py:37
  107.6 8.7 %all_to_all.20 = f32[2,8,128,512]{3,2,1,0:T(8,128)} all-to-all(f32[2,8,128,512]{3,2,1,0:T(8,128)S(1)} %product.1), channel_id=1, replica_groups=mesh['z'=8,'y'=8,'w'=2,'u'=2,'v'=2,'core'=2] {'core'}, dimensions={0} | all-to-all | bytes 8388608 | tf_op jit(solution)/shard_map/all_to_all | solution.py:106
  116.3 2.9 %reduce_sum.18 = f32[8,128,512]{2,1,0:T(8,128)S(1)} reduce(f32[2,8,128,512]{3,2,1,0:T(8,128)} %all_to_all.20, f32[]{:T(128)} %constant.53.clone.1), dimensions={0}, to_apply=%region_0.1 | reduce | flops 524288 | bytes 6291460 | tf_op jit(solution)/shard_map/reduce_sum | solution.py:106
  119.1 0.8 abs_reduce_fusion
  120.7 0.3 multiply_convert_fusion
  121.0 0.2 concatenate.3
  121.2 36.4 %all_to_all.21 = f16[8,144,512]{2,1,0:T(8,128)(2,1)S(1)} all-to-all(f16[8,144,512]{2,1,0:T(8,128)(2,1)S(1)} %concatenate.3), channel_id=1, replica_groups=mesh['z'=8,'y'=8,'w'=2,'u'=2,'v'=2,'core'=2] {'u','v','w'}, dimensions={0} | all-to-all | bytes 2359296 | tf_op jit(solution)/shard_map/all_to_all | solution.py:113
  157.6 0.1 fusion.2
  157.8 0.9 multiply_reduce_fusion
  (7 shorter events, 0.1 us)
Async XLA Ops:
  2.8 25.5 %all-to-all-start = ((bf16[8,64,128]{2,1,0:T(8,128)(2,1)}), bf16[8,64,128]{2,1,0:T(8,128)(2,1)S(1)}, u32[]{:S(2)}, u32[]{:S(2)}) async-start(bf16[8,64,128]{2,1,0:T(8,128)(2,1)} %dynamic-slice_bitcast_fusion), calls=%async_computation | async-start | bytes 262144 | tf_op jit(solution)/shard_map/all_to_all | solution.py:86
  21.4 0.7 collective-permute-start
  28.3 0.7 collective-permute-start.1
  30.3 74.8 %all-to-all-start.1 = ((bf16[8,64,1024]{2,1,0:T(8,128)(2,1)}), bf16[8,64,1024]{2,1,0:T(8,128)(2,1)S(1)}, u32[]{:S(2)}, u32[]{:S(2)}) async-start(bf16[8,64,1024]{2,1,0:T(8,128)(2,1)} %broadcast_in_dim.10), calls=%async_computation.1 | async-start | bytes 2097152 | tf_op jit(solution)/shard_map/all_to_all | solution.py:102
  66.4 16.5 %collective-permute-start.8 = (bf16[64,1024]{1,0:T(8,128)(2,1)S(1)}, bf16[64,1024]{1,0:T(8,128)(2,1)S(1)}, u32[]{:S(2)}, u32[]{:S(2)}) collective-permute-start(bf16[64,1024]{1,0:T(8,128)(2,1)S(1)} %get-tuple-element.11.refs_0_), channel_id=1, source_target_pairs={{0,112},{16,0},{32,16},{48,32},{64,48},{80,64},{96,80},{112,96},{1... | collective-permute-start | bytes 393224 | tf_op jit(solution)/shard_map/ppermute | solution.py:103
  68.3 17.6 %collective-permute-start.7 = (bf16[64,1024]{1,0:T(8,128)(2,1)S(1)}, bf16[64,1024]{1,0:T(8,128)(2,1)S(1)}, u32[]{:S(2)}, u32[]{:S(2)}) collective-permute-start(bf16[64,1024]{1,0:T(8,128)(2,1)S(1)} %get-tuple-element.11.refs_0_), channel_id=1, source_target_pairs={{0,96},{16,112},{32,0},{48,16},{64,32},{80,48},{96,64},{112,80},{1... | collective-permute-start | bytes 393224 | tf_op jit(solution)/shard_map/ppermute | solution.py:103
  70.2 19.2 %collective-permute-start.6 = (bf16[64,1024]{1,0:T(8,128)(2,1)S(1)}, bf16[64,1024]{1,0:T(8,128)(2,1)S(1)}, u32[]{:S(2)}, u32[]{:S(2)}) collective-permute-start(bf16[64,1024]{1,0:T(8,128)(2,1)S(1)} %get-tuple-element.11.refs_0_), channel_id=1, source_target_pairs={{0,80},{16,96},{32,112},{48,0},{64,16},{80,32},{96,48},{112,64},{1... | collective-permute-start | bytes 393224 | tf_op jit(solution)/shard_map/ppermute | solution.py:103
  76.1 13.4 %collective-permute-start.5 = (bf16[64,1024]{1,0:T(8,128)(2,1)S(1)}, bf16[64,1024]{1,0:T(8,128)(2,1)S(1)}, u32[]{:S(2)}, u32[]{:S(2)}) collective-permute-start(bf16[64,1024]{1,0:T(8,128)(2,1)S(1)} %get-tuple-element.11.refs_0_), channel_id=1, source_target_pairs={{0,64},{16,80},{32,96},{48,112},{64,0},{80,16},{96,32},{112,48},{1... | collective-permute-start | bytes 393224 | tf_op jit(solution)/shard_map/ppermute | solution.py:103
  79.7 19.9 %collective-permute-start.4 = (bf16[64,1024]{1,0:T(8,128)(2,1)S(1)}, bf16[64,1024]{1,0:T(8,128)(2,1)S(1)}, u32[]{:S(2)}, u32[]{:S(2)}) collective-permute-start(bf16[64,1024]{1,0:T(8,128)(2,1)S(1)} %get-tuple-element.11.refs_0_), channel_id=1, source_target_pairs={{0,48},{16,64},{32,80},{48,96},{64,112},{80,0},{96,16},{112,32},{1... | collective-permute-start | bytes 393224 | tf_op jit(solution)/shard_map/ppermute | solution.py:103
  82.9 16.7 %collective-permute-start.3 = (bf16[64,1024]{1,0:T(8,128)(2,1)S(1)}, bf16[64,1024]{1,0:T(8,128)(2,1)S(1)}, u32[]{:S(2)}, u32[]{:S(2)}) collective-permute-start(bf16[64,1024]{1,0:T(8,128)(2,1)S(1)} %get-tuple-element.11.refs_0_), channel_id=1, source_target_pairs={{0,32},{16,48},{32,64},{48,80},{64,96},{80,112},{96,0},{112,16},{1... | collective-permute-start | bytes 393224 | tf_op jit(solution)/shard_map/ppermute | solution.py:103
  85.9 19.1 %collective-permute-start.2 = (bf16[64,1024]{1,0:T(8,128)(2,1)S(1)}, bf16[64,1024]{1,0:T(8,128)(2,1)S(1)}, u32[]{:S(2)}, u32[]{:S(2)}) collective-permute-start(bf16[64,1024]{1,0:T(8,128)(2,1)S(1)} %get-tuple-element.11.refs_0_), channel_id=1, source_target_pairs={{0,16},{16,32},{32,48},{48,64},{64,80},{80,96},{96,112},{112,0},{1... | collective-permute-start | bytes 393224 | tf_op jit(solution)/shard_map/ppermute | solution.py:103

commit v8 on v6

v8 whole, which is shorter than its diff:
```python
import jax
import jax.numpy as jnp
from jax import lax
from jax.experimental import pallas as pl
from jax.experimental.pallas import tpu as pltpu
from jax.sharding import Mesh, PartitionSpec as P

B = 128
AXES = ("z", "y", "w", "u", "v", "core")
TAIL = 16


def product_kernel(z_ref, left_ref, right_ref, out_ref, ordered):
    n, depth, _ = right_ref.shape
    z = z_ref[0]

    @pl.when(pl.program_id(0) == 0)
    def _():
        for p in range(n):
            ordered[p * depth : (p + 1) * depth, :] = right_ref[lax.rem(p - z + n, n)]

    total = lax.dot_general(
        left_ref[...], ordered[...], (((0,), (0,)), ((), ())), preferred_element_type=jnp.float32
    )
    for a in range(out_ref.shape[0]):
        out_ref[a, 0] = total[a * B : (a + 1) * B]


def product(left, right, z, cores):
    n, depth, panel = right.shape
    wide = left.shape[1]
    step = cores * B
    return pl.pallas_call(
        product_kernel,
        grid_spec=pltpu.PrefetchScalarGridSpec(
            num_scalar_prefetch=1,
            grid=(wide // step,),
            in_specs=[
                pl.BlockSpec((n * depth, step), lambda m, _: (0, m)),
                pl.BlockSpec((n, depth, panel), lambda m, _: (0, 0, 0)),
            ],
            out_specs=pl.BlockSpec((cores, 1, B, panel), lambda m, _: (0, m, 0, 0)),
            scratch_shapes=[pltpu.VMEM((n * depth, panel), left.dtype)],
        ),
        out_shape=jax.ShapeDtypeStruct((cores, wide // step, B, panel), jnp.float32),
        compiler_params=pltpu.CompilerParams(vmem_limit_bytes=24 * 1024 * 1024),
        cost_estimate=pl.CostEstimate(
            flops=2 * n * depth * wide * panel,
            bytes_accessed=2 * n * depth * (wide + panel) + 4 * wide * panel,
            transcendentals=0,
        ),
        name="product",
    )(z.reshape(1), left, right)


def body(stored, pattern):
    nz, ny, nw, nu, nv, ncore = (lax.axis_size(a) for a in AXES)
    z, y, w, u, v, core = (lax.axis_index(a) for a in AXES)
    nl = nu * nv * ncore
    l = (u * nv + v) * ncore + core
    g = z * nl + l
    plane = nl * B
    panel = plane // nw

    def upper(first_block, blocks):
        raw = lax.dynamic_slice(stored, (0, first_block * B), (B, blocks * B))
        present = lax.dynamic_slice(pattern, (g, first_block), (1, blocks))
        present = jnp.repeat(present, B, axis=1) > 0
        row = g * B + jnp.arange(B, dtype=jnp.int32)[:, None]
        column = first_block * B + jnp.arange(blocks * B, dtype=jnp.int32)[None, :]
        return jnp.where(present & (column >= row), raw, jnp.zeros((), raw.dtype))

    def flat(zz, yy, r):
        return (zz * ny + yy) * (nw * nl) + r

    def pairs(target, least):
        found = []
        for a in range(nz):
            for b in range(ny):
                c = (b - a) % nz
                if c >= a + least:
                    found += [(flat(a, b, r), flat(*target(a, b, c), r)) for r in range(nw * nl)]
        return found

    k = lax.rem(y - z + nz, nz)
    band = upper(k * nl, nl)
    turned = band.T.reshape(nl, B, B)
    crossed = lax.all_to_all(turned, ("u", "v", "core"), split_axis=0, concat_axis=0, tiled=True)
    straight = lax.ppermute(band, AXES, pairs(lambda a, b, c: (c, b), 1))
    crossed = crossed.transpose(1, 0, 2).reshape(B, plane)
    offset = l * B + jnp.arange(B, dtype=jnp.int32)[:, None]
    across = jnp.arange(plane, dtype=jnp.int32)[None, :]
    left = jnp.where(
        k * plane + offset <= z * plane + across, jnp.where(k == z, band, straight), crossed
    )
    left = lax.all_gather(left, "y", axis=0, tiled=True)

    half = lax.dynamic_slice(crossed, (0, w * panel), (B, panel))
    half = lax.ppermute(half, AXES, pairs(lambda a, b, c: (c, a), 0))
    tile = upper(y * nl + w * (nl // nw), nl // nw)
    own = y * plane + w * panel + jnp.arange(panel, dtype=jnp.int32)[None, :]
    right = jnp.where(z * plane + offset <= own, tile, half)
    right = jnp.broadcast_to(right[None], (nz, B, panel))
    right = lax.all_to_all(right, "z", split_axis=0, concat_axis=0, tiled=True)

    partial = product(left, right, z, ncore)
    partial = jnp.sum(lax.all_to_all(partial, "core", split_axis=0, concat_axis=0, tiled=True), axis=0)

    most = jnp.max(jnp.abs(partial))
    power = jnp.clip(jnp.ceil(jnp.log2(jnp.maximum(most, 1e-30))) - 14.0, -100.0, 100.0)
    grown = jnp.exp2(-power)
    tail = jnp.broadcast_to(power.astype(jnp.float16), (TAIL, panel))
    mine = u * nv + v
    total = lax.dynamic_index_in_dim(partial, mine, 0, keepdims=False)
    for d in range(1, nu * nv):
        chunk = lax.dynamic_index_in_dim(partial, mine ^ d, 0, keepdims=False)
        chunk = jnp.concatenate([(chunk * grown).astype(jnp.float16), tail], axis=0)
        got = lax.ppermute(chunk, ("u", "v"), [(a, a ^ d) for a in range(nu * nv)])
        total = total + got[:B].astype(jnp.float32) * jnp.exp2(got[B:, :1].astype(jnp.float32)[:1])
    return total.astype(jnp.bfloat16)


def solution(mesh):
    finer = Mesh(mesh.devices.reshape(8, 8, 2, 2, 2, 2), AXES)
    return jax.shard_map(
        body,
        mesh=finer,
        in_specs=(P(("z", "u", "v", "core"), None), P()),
        out_specs=P(("z", "u", "v", "core"), ("y", "w")),
        check_vma=False,
    )
```

time: 199 us -> 144 us (0.72)
  starting transfers between devices: 128 us -> 58.7 us
  blocking collectives: 38.9 us -> 5.54 us
  waiting for transfers between devices: 20.6 us -> 46.5 us
  between operations: 0.21 us -> 16.4 us
  other arithmetic: 5.39 us -> 8.61 us
  local copies, waits for them, and re-layouts: 2.57 us -> 5.32 us
    ppermute x9 -> x5, starting transfers between devices: 85 us -> 12.7 us  [the longest x3 11.4 us: body(): got = lax.ppermute(chunk, ('u', 'v'), [(a, a ^ d) for a in range(nu * nv)])]
    all_to_all x1 -> x0, blocking collectives: 32.8 us -> none  [body(): lax.all_to_all(partial, ('u', 'v'), split_axis=0, concat_axis=0, tiled=True)]
    all_to_all x1, waiting for transfers between devices: 0.01 us -> 29.2 us  [body(): right = lax.all_to_all(right, 'z', split_axis=0, concat_axis=0, tiled=True)]
    ppermute x9 -> x5, waiting for transfers between devices: 12.8 us -> 9.45 us  [the longest x3 9.44 us: body(): got = lax.ppermute(chunk, ('u', 'v'), [(a, a ^ d) for a in range(nu * nv)])]
    all_to_all x1, starting transfers between devices: 25.8 us -> 28.5 us  [body(): right = lax.all_to_all(right, 'z', split_axis=0, concat_axis=0, tiled=True)]
  transfers between devices with their start and end apart: 11 -> 8, of which waited for: 4 -> 5; matrix products, arithmetic and copies ran while one was open for 1% -> 4% of each run, Pallas kernels for 0% -> 0%
where the time goes in v8:
time: 144 us
  starting transfers between devices  58.7 us (41%)
  waiting for transfers between devices  46.5 us (32%)
  between operations  16.4 us (11%)
  other arithmetic  8.61 us (6%)
  blocking collectives  5.54 us (4%)
  local copies, waits for them, and re-layouts  5.32 us (4%)
  Pallas kernels  2.42 us (2%)
    all_to_all x1, waiting for transfers between devices, body(): right = lax.all_to_all(right, 'z', split_axis=0, concat_axis=0, tiled=True)  29.2 us
    all_to_all x1, starting transfers between devices, body(): right = lax.all_to_all(right, 'z', split_axis=0, concat_axis=0, tiled=True)  28.5 us
    all_to_all x1, starting transfers between devices, body(): lax.all_to_all(turned, ('u', 'v', 'core'), split_axis=0, concat_axis=0, t...  17.5 us
    ppermute x3, starting transfers between devices, body(): got = lax.ppermute(chunk, ('u', 'v'), [(a, a ^ d) for a in range(nu * nv)])  11.4 us
    ppermute x3, waiting for transfers between devices, body(): got = lax.ppermute(chunk, ('u', 'v'), [(a, a ^ d) for a in range(nu * nv)])  9.44 us
    all_to_all x1, waiting for transfers between devices, body(): lax.all_to_all(turned, ('u', 'v', 'core'), split_axis=0, concat_axis=0, t...  7.83 us
    all_to_all x1, blocking collectives, body(): lax.all_to_all(partial, 'core', split_axis=0, concat_axis=0, tiled=True)  5.54 us
  transfers between devices with their start and end apart: 8, of which 5 were waited for; matrix products, arithmetic and copies ran while one was open for 4% of the time, Pallas kernels for 0%

profile of v8, /device:TPU:1, one launch (start us, length us, event | category | flops | bytes accessed | tf_op | source)
XLA Modules:
  0.0 143.5 jit_solution(1998708773951306855)
XLA Ops:
  6.5 0.8 compare_bitcast_fusion.1
  7.3 0.1 broadcast_bitcast_fusion
  7.4 1.1 fusion.8
  8.5 0.8 copy.6
  9.3 17.5 %all-to-all-start = ((bf16[8,128,128]{2,1,0:T(8,128)(2,1)}), bf16[8,128,128]{2,1,0:T(8,128)(2,1)S(1)}, u32[]{:S(2)}, u32[]{:S(2)}) async-start(bf16[8,128,128]{2,1,0:T(8,128)(2,1)} %bitcast.4), calls=%async_computation | async-start | bytes 524288 | tf_op jit(solution)/shard_map/all_to_all | solution.py:88
  26.8 0.0 all-gather.2.cloned.1.call-start
  26.8 1.1 and_select_fusion
  27.9 0.7 collective-permute-start
  28.7 0.0 collective-permute-done
  28.7 7.8 %all-to-all-done = bf16[8,128,128]{2,1,0:T(8,128)(2,1)S(1)} async-done(((bf16[8,128,128]{2,1,0:T(8,128)(2,1)}), bf16[8,128,128]{2,1,0:T(8,128)(2,1)S(1)}, u32[]{:S(2)}, u32[]{:S(2)}) %all-to-all-start) | async-done | bytes 262176 | tf_op jit(solution)/shard_map/all_to_all | solution.py:88
  36.5 1.9 %compare_select_fusion = bf16[128,1024]{1,0:T(8,128)(2,1)} fusion(bf16[128,1024]{1,0:T(8,128)(2,1)S(1)} %collective-permute-done, s32[1024]{0:T(1024)S(1)} %iota_add_fusion.1, s32[128]{0:T(128)S(1)} %fusion.7, pred[]{:T(512)S(6)} %eq.3, bf16[128,8192]{1,0:T(8,128)(2,1)} %param.2, s32[]{:T(128)S(6)} %select_n.59, s32[128]{0:T(128)S(1)} %iota_add_fusion.4, ...), kind=kLoop, calls=%fused_computation.2 | loop fusion | flops 786432 | bytes 1058821 | tf_op jit(solution)/shard_map/jit(_where)/select_n | solution.py:93
  38.4 0.0 all-gather.2.cloned.1.call-update
  38.5 0.8 compare_bitcast_fusion
  39.2 0.1 broadcast_bitcast_fusion.1
  39.4 0.7 collective-permute-start.1
  40.1 0.0 collective-permute-done.1
  40.1 1.1 compare_select_fusion.1
  41.2 1.1 broadcast_in_dim.32
  42.2 28.5 %all-to-all-start.1 = ((bf16[8,128,512]{2,1,0:T(8,128)(2,1)}), bf16[8,128,512]{2,1,0:T(8,128)(2,1)S(1)}, u32[]{:S(2)}, u32[]{:S(2)}) async-start(bf16[8,128,512]{2,1,0:T(8,128)(2,1)} %broadcast_in_dim.32), calls=%async_computation.1 | async-start | bytes 2097152 | tf_op jit(solution)/shard_map/all_to_all | solution.py:104
  70.7 29.2 %all-to-all-done.1.right_ref = bf16[8,128,512]{2,1,0:T(8,128)(2,1)S(1)} async-done(((bf16[8,128,512]{2,1,0:T(8,128)(2,1)}), bf16[8,128,512]{2,1,0:T(8,128)(2,1)S(1)}, u32[]{:S(2)}, u32[]{:S(2)}) %all-to-all-start.1) | async-done | bytes 1048608 | tf_op jit(solution)/shard_map/all_to_all | solution.py:104
  100.0 0.0 all-gather.2.cloned.1.call-done.left_ref
  100.0 0.0 copy-start
  100.0 1.6 %copy-done = bf16[1024,1024]{1,0:T(8,128)(2,1)S(1)} copy-done((bf16[1024,1024]{1,0:T(8,128)(2,1)S(1)}, bf16[1024,1024]{1,0:T(8,128)(2,1)}, u32[]{:S(2)}) %copy-start) | copy-done | bytes 2097176
  101.6 2.4 %product.1 = f32[2,4,128,512]{3,2,1,0:T(8,128)S(1)} custom-call(s32[1]{0:T(128)} %bitcast.z_ref, bf16[1024,1024]{1,0:T(8,128)(2,1)S(1)} %copy-done, bf16[8,128,512]{2,1,0:T(8,128)(2,1)S(1)} %all-to-all-done.1.right_ref), custom_call_target="tpu_custom_call" | custom-call | flops 1073741824 | bytes 5242880 | tf_op jit(solution)/shard_map/product/pallas_call | solution.py:33
  104.0 5.5 %all_to_all.15 = f32[2,4,128,512]{3,2,1,0:T(8,128)S(1)} all-to-all(f32[2,4,128,512]{3,2,1,0:T(8,128)S(1)} %product.1), channel_id=1, replica_groups=mesh['z'=8,'y'=8,'w'=2,'u'=2,'v'=2,'core'=2] {'core'}, dimensions={0} | all-to-all | bytes 4194304 | tf_op jit(solution)/shard_map/all_to_all | solution.py:107
  109.5 0.3 reduce_sum.9
  109.8 0.7 abs_reduce_fusion
  111.2 0.1 fusion.3
  111.4 4.2 %collective-permute-start.2 = (f16[144,512]{1,0:T(8,128)(2,1)S(1)}, f16[144,512]{1,0:T(8,128)(2,1)S(1)}, u32[]{:S(2)}, u32[]{:S(2)}) collective-permute-start(f16[144,512]{1,0:T(8,128)(2,1)S(1)} %concatenate.9), channel_id=1, source_target_pairs={{0,2},{2,0},{4,6},{6,4},{1,3},{3,1},{5,7},{7,5},{8,10},{10,8},{12,... | collective-permute-start | bytes 442376 | tf_op jit(solution)/shard_map/ppermute | solution.py:118
  115.6 5.2 %collective-permute-start.3 = (f16[144,512]{1,0:T(8,128)(2,1)S(1)}, f16[144,512]{1,0:T(8,128)(2,1)S(1)}, u32[]{:S(2)}, u32[]{:S(2)}) collective-permute-start(f16[144,512]{1,0:T(8,128)(2,1)S(1)} %concatenate.10), channel_id=1, source_target_pairs={{0,4},{2,6},{4,0},{6,2},{1,5},{3,7},{5,1},{7,3},{8,12},{10,14},{12... | collective-permute-start | bytes 442376 | tf_op jit(solution)/shard_map/ppermute | solution.py:118
  120.8 2.0 %collective-permute-start.4 = (f16[144,512]{1,0:T(8,128)(2,1)S(1)}, f16[144,512]{1,0:T(8,128)(2,1)S(1)}, u32[]{:S(2)}, u32[]{:S(2)}) collective-permute-start(f16[144,512]{1,0:T(8,128)(2,1)S(1)} %concatenate.11), channel_id=1, source_target_pairs={{0,6},{2,4},{4,2},{6,0},{1,7},{3,5},{5,3},{7,1},{8,14},{10,12},{12... | collective-permute-start | bytes 442376 | tf_op jit(solution)/shard_map/ppermute | solution.py:118
  122.9 0.2 collective-permute-done.2
  123.1 0.5 slice.43
  124.3 2.0 %collective-permute-done.3 = f16[144,512]{1,0:T(8,128)(2,1)S(1)} collective-permute-done((f16[144,512]{1,0:T(8,128)(2,1)S(1)}, f16[144,512]{1,0:T(8,128)(2,1)S(1)}, u32[]{:S(2)}, u32[]{:S(2)}) %collective-permute-start.3) | collective-permute-done | bytes 147488 | tf_op jit(solution)/shard_map/ppermute | solution.py:118
  126.3 0.5 slice.45
  127.5 7.2 %collective-permute-done.4 = f16[144,512]{1,0:T(8,128)(2,1)S(1)} collective-permute-done((f16[144,512]{1,0:T(8,128)(2,1)S(1)}, f16[144,512]{1,0:T(8,128)(2,1)S(1)}, u32[]{:S(2)}, u32[]{:S(2)}) %collective-permute-start.4) | collective-permute-done | bytes 147488 | tf_op jit(solution)/shard_map/ppermute | solution.py:118
  134.7 0.5 slice.47
  135.9 0.7 fusion.2
  (12 shorter events, 0.2 us)
Async XLA Ops:
  9.3 27.2 %all-to-all-start = ((bf16[8,128,128]{2,1,0:T(8,128)(2,1)}), bf16[8,128,128]{2,1,0:T(8,128)(2,1)S(1)}, u32[]{:S(2)}, u32[]{:S(2)}) async-start(bf16[8,128,128]{2,1,0:T(8,128)(2,1)} %bitcast.4), calls=%async_computation | async-start | bytes 524288 | tf_op jit(solution)/shard_map/all_to_all | solution.py:88
  26.8 73.2 %all-gather.2.cloned.1.call-start = ((), (), s32[]{:S(2)}) async-start(), calls=%async_computation.3 | async-start | bytes 2359296 | tf_op jit(solution)/shard_map/all_gather | solution.py:96
  27.9 0.7 collective-permute-start
  39.4 0.7 collective-permute-start.1
  42.2 57.7 %all-to-all-start.1 = ((bf16[8,128,512]{2,1,0:T(8,128)(2,1)}), bf16[8,128,512]{2,1,0:T(8,128)(2,1)S(1)}, u32[]{:S(2)}, u32[]{:S(2)}) async-start(bf16[8,128,512]{2,1,0:T(8,128)(2,1)} %broadcast_in_dim.32), calls=%async_computation.1 | async-start | bytes 2097152 | tf_op jit(solution)/shard_map/all_to_all | solution.py:104
  100.0 1.6 %copy-start = (bf16[1024,1024]{1,0:T(8,128)(2,1)S(1)}, bf16[1024,1024]{1,0:T(8,128)(2,1)}, u32[]{:S(2)}) copy-start(bf16[1024,1024]{1,0:T(8,128)(2,1)} %all-gather.2.cloned.1.call-done.left_ref) | copy-start | bytes 6291460
  111.4 11.7 %collective-permute-start.2 = (f16[144,512]{1,0:T(8,128)(2,1)S(1)}, f16[144,512]{1,0:T(8,128)(2,1)S(1)}, u32[]{:S(2)}, u32[]{:S(2)}) collective-permute-start(f16[144,512]{1,0:T(8,128)(2,1)S(1)} %concatenate.9), channel_id=1, source_target_pairs={{0,2},{2,0},{4,6},{6,4},{1,3},{3,1},{5,7},{7,5},{8,10},{10,8},{12,... | collective-permute-start | bytes 442376 | tf_op jit(solution)/shard_map/ppermute | solution.py:118
  115.6 10.7 %collective-permute-start.3 = (f16[144,512]{1,0:T(8,128)(2,1)S(1)}, f16[144,512]{1,0:T(8,128)(2,1)S(1)}, u32[]{:S(2)}, u32[]{:S(2)}) collective-permute-start(f16[144,512]{1,0:T(8,128)(2,1)S(1)} %concatenate.10), channel_id=1, source_target_pairs={{0,4},{2,6},{4,0},{6,2},{1,5},{3,7},{5,1},{7,3},{8,12},{10,14},{12... | collective-permute-start | bytes 442376 | tf_op jit(solution)/shard_map/ppermute | solution.py:118
  120.8 13.9 %collective-permute-start.4 = (f16[144,512]{1,0:T(8,128)(2,1)S(1)}, f16[144,512]{1,0:T(8,128)(2,1)S(1)}, u32[]{:S(2)}, u32[]{:S(2)}) collective-permute-start(f16[144,512]{1,0:T(8,128)(2,1)S(1)} %concatenate.11), channel_id=1, source_target_pairs={{0,6},{2,4},{4,2},{6,0},{1,7},{3,5},{5,3},{7,1},{8,14},{10,12},{12... | collective-permute-start | bytes 442376 | tf_op jit(solution)/shard_map/ppermute | solution.py:118
Sparse Core Ops, SparseCore 0:
  38.6 51.6 all-gather.1

commit v9 on v8

--- a/solution.py
+++ b/solution.py
@@ -62,13 +62,15 @@
     plane = nl * B
     panel = plane // nw
 
-    def upper(first_block, blocks):
-        raw = lax.dynamic_slice(stored, (0, first_block * B), (B, blocks * B))
-        present = lax.dynamic_slice(pattern, (g, first_block), (1, blocks))
-        present = jnp.repeat(present, B, axis=1) > 0
-        row = g * B + jnp.arange(B, dtype=jnp.int32)[:, None]
-        column = first_block * B + jnp.arange(blocks * B, dtype=jnp.int32)[None, :]
-        return jnp.where(present & (column >= row), raw, jnp.zeros((), raw.dtype))
+    def columns(start, width):
+        return lax.dynamic_slice(stored, (0, start), (B, width))
+
+    def here(rows, first, count, across):
+        if across:
+            found = lax.dynamic_slice(pattern, (rows, first), (1, count))
+        else:
+            found = lax.dynamic_slice(pattern, (first, rows), (count, 1)).reshape(1, count)
+        return jnp.repeat(found, B, axis=1) > 0
 
     def flat(zz, yy, r):
         return (zz * ny + yy) * (nw * nl) + r
@@ -83,23 +85,34 @@
         return found
 
     k = lax.rem(y - z + nz, nz)
-    band = upper(k * nl, nl)
+    band = columns(k * plane, plane)
+    straight = lax.ppermute(band, AXES, pairs(lambda a, b, c: (c, b), 1))
     turned = band.T.reshape(nl, B, B)
     crossed = lax.all_to_all(turned, ("u", "v", "core"), split_axis=0, concat_axis=0, tiled=True)
-    straight = lax.ppermute(band, AXES, pairs(lambda a, b, c: (c, b), 1))
+    first = y * nl + w * (nl // nw)
+    present = (
+        here(k * nl + l, z * nl, nl, True),
+        here(k * nl + l, z * nl, nl, False),
+        here(g, first, nl // nw, True),
+        here(g, first, nl // nw, False),
+    )
+    crossed, present = lax.optimization_barrier((crossed, present))
     crossed = crossed.transpose(1, 0, 2).reshape(B, plane)
+    zero = jnp.zeros((), stored.dtype)
     offset = l * B + jnp.arange(B, dtype=jnp.int32)[:, None]
     across = jnp.arange(plane, dtype=jnp.int32)[None, :]
-    left = jnp.where(
-        k * plane + offset <= z * plane + across, jnp.where(k == z, band, straight), crossed
-    )
+    above = k * plane + offset <= z * plane + across
+    kept = jnp.where(above, present[0], present[1])
+    left = jnp.where(kept, jnp.where(above, jnp.where(k == z, band, straight), crossed), zero)
     left = lax.all_gather(left, "y", axis=0, tiled=True)
 
     half = lax.dynamic_slice(crossed, (0, w * panel), (B, panel))
     half = lax.ppermute(half, AXES, pairs(lambda a, b, c: (c, a), 0))
-    tile = upper(y * nl + w * (nl // nw), nl // nw)
+    tile = columns(y * plane + w * panel, panel)
     own = y * plane + w * panel + jnp.arange(panel, dtype=jnp.int32)[None, :]
-    right = jnp.where(z * plane + offset <= own, tile, half)
+    above = z * plane + offset <= own
+    kept = jnp.where(above, present[2], present[3])
+    right = jnp.where(kept, jnp.where(above, tile, half), zero)
     right = jnp.broadcast_to(right[None], (nz, B, panel))
     right = lax.all_to_all(right, "z", split_axis=0, concat_axis=0, tiled=True)
 
@@ -111,12 +124,13 @@
     grown = jnp.exp2(-power)
     tail = jnp.broadcast_to(power.astype(jnp.float16), (TAIL, panel))
     mine = u * nv + v
-    total = lax.dynamic_index_in_dim(partial, mine, 0, keepdims=False)
+    total = 0.0
     for d in range(1, nu * nv):
         chunk = lax.dynamic_index_in_dim(partial, mine ^ d, 0, keepdims=False)
         chunk = jnp.concatenate([(chunk * grown).astype(jnp.float16), tail], axis=0)
         got = lax.ppermute(chunk, ("u", "v"), [(a, a ^ d) for a in range(nu * nv)])
-        total = total + got[:B].astype(jnp.float32) * jnp.exp2(got[B:, :1].astype(jnp.float32)[:1])
+        total = total + got.astype(jnp.float32) * jnp.exp2(got[B, 0].astype(jnp.float32))
+    total = total[:B] + lax.dynamic_index_in_dim(partial, mine, 0, keepdims=False)
     return total.astype(jnp.bfloat16)
 
 

time: 144 us -> 142 us (0.986)
  waiting for transfers between devices: 46.5 us -> 43.1 us
  local copies, waits for them, and re-layouts: 5.32 us -> 7.42 us
    all_to_all x1, waiting for transfers between devices: 7.83 us -> 4.41 us  [body(): lax.all_to_all(turned, ('u', 'v', 'core'), split_axis=0, concat_axis=0, t...]
    gt x2 -> x4, other arithmetic: 1.53 us -> 3.28 us  [here(): return jnp.repeat(found, B, axis=1) > 0]
    select_n x3 -> x2, other arithmetic: 4.11 us -> 2.92 us  [the longest x1 1.87 us: body(): jnp.where(kept, jnp.where(above, jnp.where(k == z, band, straight), cross...]
  transfers between devices with their start and end apart: 8 -> 8, of which waited for: 5 -> 5; matrix products, arithmetic and copies ran while one was open for 4% -> 6% of each run, Pallas kernels for 0% -> 0%
where the time goes in v9:
time: 142 us; the launch traced here: 141 us
  starting transfers between devices  58.4 us (41%)
  waiting for transfers between devices  43.1 us (30%)
  between operations  16.4 us (12%)
  other arithmetic  8.11 us (6%)
  local copies, waits for them, and re-layouts  7.42 us (5%)
  blocking collectives  5.53 us (4%)
  Pallas kernels  2.42 us (2%)
    all_to_all x1, waiting for transfers between devices, body(): right = lax.all_to_all(right, 'z', split_axis=0, concat_axis=0, tiled=True)  29.2 us
    all_to_all x1, starting transfers between devices, body(): right = lax.all_to_all(right, 'z', split_axis=0, concat_axis=0, tiled=True)  28.2 us
    all_to_all x1, starting transfers between devices, body(): lax.all_to_all(turned, ('u', 'v', 'core'), split_axis=0, concat_axis=0, t...  17.5 us
    ppermute x3, starting transfers between devices, body(): got = lax.ppermute(chunk, ('u', 'v'), [(a, a ^ d) for a in range(nu * nv)])  11.4 us
    ppermute x3, waiting for transfers between devices, body(): got = lax.ppermute(chunk, ('u', 'v'), [(a, a ^ d) for a in range(nu * nv)])  9.44 us
    all_to_all x1, blocking collectives, body(): lax.all_to_all(partial, 'core', split_axis=0, concat_axis=0, tiled=True)  5.53 us
    all_to_all x1, waiting for transfers between devices, body(): lax.all_to_all(turned, ('u', 'v', 'core'), split_axis=0, concat_axis=0, t...  4.41 us
    gt x4, other arithmetic, here(): return jnp.repeat(found, B, axis=1) > 0  3.28 us
  transfers between devices with their start and end apart: 8, of which 5 were waited for; matrix products, arithmetic and copies ran while one was open for 6% of the time, Pallas kernels for 0%

profile of v9, /device:TPU:1, one launch (start us, length us, event | category | flops | bytes accessed | tf_op | source)
XLA Modules:
  0.0 141.4 jit_solution(5515138176413622678)
XLA Ops:
  6.5 1.0 fusion.10
  7.5 0.8 copy.6
  8.3 17.5 %all-to-all-start = ((bf16[8,128,128]{2,1,0:T(8,128)(2,1)}), bf16[8,128,128]{2,1,0:T(8,128)(2,1)S(1)}, u32[]{:S(2)}, u32[]{:S(2)}) async-start(bf16[8,128,128]{2,1,0:T(8,128)(2,1)} %bitcast.2), calls=%async_computation | async-start | bytes 524288 | tf_op jit(solution)/shard_map/all_to_all | solution.py:91
  25.8 0.0 all-gather.2.cloned.1.call-start
  25.8 1.0 constant_dynamic-slice_fusion.1
  26.8 0.7 collective-permute-start
  27.5 0.9 fusion.6
  28.4 0.8 compare_bitcast_fusion.1
  29.1 0.9 fusion.7
  30.0 0.8 compare_bitcast_fusion
  30.8 0.1 broadcast_bitcast_fusion
  30.8 0.1 broadcast_bitcast_fusion.2
  30.9 0.1 broadcast_bitcast_fusion.3
  31.0 0.1 broadcast_bitcast_fusion.1
  31.1 4.4 %all-to-all-done = bf16[8,128,128]{2,1,0:T(8,128)(2,1)S(1)} async-done(((bf16[8,128,128]{2,1,0:T(8,128)(2,1)}), bf16[8,128,128]{2,1,0:T(8,128)(2,1)S(1)}, u32[]{:S(2)}, u32[]{:S(2)}) %all-to-all-start) | async-done | bytes 262176 | tf_op jit(solution)/shard_map/all_to_all | solution.py:91
  35.5 0.0 collective-permute-done
  35.6 1.9 %fusion = bf16[128,1024]{1,0:T(8,128)(2,1)} fusion(bf16[128,1024]{1,0:T(8,128)(2,1)S(1)} %collective-permute-done, s32[1024]{0:T(1024)S(1)} %iota_add_fusion, s32[128]{0:T(128)S(1)} %fusion.9, pred[]{:T(512)S(6)} %eq.3, pred[1024]{0:T(1024)(128)(4,1)S(1)} %reduce.3, pred[1024]{0:T(1024)(128)(4,1)S(1)} %reduce.2, bf16[128,8192]{1,0:T(8,128)(2,1)} %param.2, ...), kind=kLoop, calls=%fused_computation.3 | loop fusion | flops 655360 | bytes 1055237 | tf_op jit(solution)/shard_map/jit(_where)/select_n | solution.py:106
  37.4 0.0 all-gather.2.cloned.1.call-update
  37.5 0.7 collective-permute-start.1
  38.3 0.0 collective-permute-done.1
  38.3 1.0 fusion.2
  39.3 1.1 broadcast_in_dim.84
  40.4 28.2 %all-to-all-start.1 = ((bf16[8,128,512]{2,1,0:T(8,128)(2,1)}), bf16[8,128,512]{2,1,0:T(8,128)(2,1)S(1)}, u32[]{:S(2)}, u32[]{:S(2)}) async-start(bf16[8,128,512]{2,1,0:T(8,128)(2,1)} %broadcast_in_dim.84), calls=%async_computation.1 | async-start | bytes 2097152 | tf_op jit(solution)/shard_map/all_to_all | solution.py:117
  68.6 29.2 %all-to-all-done.1.right_ref = bf16[8,128,512]{2,1,0:T(8,128)(2,1)S(1)} async-done(((bf16[8,128,512]{2,1,0:T(8,128)(2,1)}), bf16[8,128,512]{2,1,0:T(8,128)(2,1)S(1)}, u32[]{:S(2)}, u32[]{:S(2)}) %all-to-all-start.1) | async-done | bytes 1048608 | tf_op jit(solution)/shard_map/all_to_all | solution.py:117
  97.9 0.0 all-gather.2.cloned.1.call-done.left_ref
  97.9 0.0 copy-start
  97.9 1.6 %copy-done = bf16[1024,1024]{1,0:T(8,128)(2,1)S(1)} copy-done((bf16[1024,1024]{1,0:T(8,128)(2,1)S(1)}, bf16[1024,1024]{1,0:T(8,128)(2,1)}, u32[]{:S(2)}) %copy-start) | copy-done | bytes 2097176
  99.5 2.4 %product.1 = f32[2,4,128,512]{3,2,1,0:T(8,128)S(1)} custom-call(s32[1]{0:T(128)} %bitcast.z_ref, bf16[1024,1024]{1,0:T(8,128)(2,1)S(1)} %copy-done, bf16[8,128,512]{2,1,0:T(8,128)(2,1)S(1)} %all-to-all-done.1.right_ref), custom_call_target="tpu_custom_call" | custom-call | flops 1073741824 | bytes 5242880 | tf_op jit(solution)/shard_map/product/pallas_call | solution.py:33
  101.9 5.5 %all_to_all.15 = f32[2,4,128,512]{3,2,1,0:T(8,128)S(1)} all-to-all(f32[2,4,128,512]{3,2,1,0:T(8,128)S(1)} %product.1), channel_id=1, replica_groups=mesh['z'=8,'y'=8,'w'=2,'u'=2,'v'=2,'core'=2] {'core'}, dimensions={0} | all-to-all | bytes 4194304 | tf_op jit(solution)/shard_map/all_to_all | solution.py:120
  107.4 0.3 reduce_sum.9
  107.7 0.7 abs_reduce_fusion
  109.1 0.1 fusion.3
  109.3 4.2 %collective-permute-start.2 = (f16[144,512]{1,0:T(8,128)(2,1)S(1)}, f16[144,512]{1,0:T(8,128)(2,1)S(1)}, u32[]{:S(2)}, u32[]{:S(2)}) collective-permute-start(f16[144,512]{1,0:T(8,128)(2,1)S(1)} %concatenate.9), channel_id=1, source_target_pairs={{0,2},{2,0},{4,6},{6,4},{1,3},{3,1},{5,7},{7,5},{8,10},{10,8},{12,... | collective-permute-start | bytes 442376 | tf_op jit(solution)/shard_map/ppermute | solution.py:131
  113.5 5.2 %collective-permute-start.3 = (f16[144,512]{1,0:T(8,128)(2,1)S(1)}, f16[144,512]{1,0:T(8,128)(2,1)S(1)}, u32[]{:S(2)}, u32[]{:S(2)}) collective-permute-start(f16[144,512]{1,0:T(8,128)(2,1)S(1)} %concatenate.10), channel_id=1, source_target_pairs={{0,4},{2,6},{4,0},{6,2},{1,5},{3,7},{5,1},{7,3},{8,12},{10,14},{12... | collective-permute-start | bytes 442376 | tf_op jit(solution)/shard_map/ppermute | solution.py:131
  118.7 2.0 %collective-permute-start.4 = (f16[144,512]{1,0:T(8,128)(2,1)S(1)}, f16[144,512]{1,0:T(8,128)(2,1)S(1)}, u32[]{:S(2)}, u32[]{:S(2)}) collective-permute-start(f16[144,512]{1,0:T(8,128)(2,1)S(1)} %concatenate.11), channel_id=1, source_target_pairs={{0,6},{2,4},{4,2},{6,0},{1,7},{3,5},{5,3},{7,1},{8,14},{10,12},{12... | collective-permute-start | bytes 442376 | tf_op jit(solution)/shard_map/ppermute | solution.py:131
  120.7 0.2 collective-permute-done.2
  120.9 0.5 slice.16
  122.2 2.0 %collective-permute-done.3 = f16[144,512]{1,0:T(8,128)(2,1)S(1)} collective-permute-done((f16[144,512]{1,0:T(8,128)(2,1)S(1)}, f16[144,512]{1,0:T(8,128)(2,1)S(1)}, u32[]{:S(2)}, u32[]{:S(2)}) %collective-permute-start.3) | collective-permute-done | bytes 147488 | tf_op jit(solution)/shard_map/ppermute | solution.py:131
  124.2 0.5 slice.17
  125.4 7.2 %collective-permute-done.4 = f16[144,512]{1,0:T(8,128)(2,1)S(1)} collective-permute-done((f16[144,512]{1,0:T(8,128)(2,1)S(1)}, f16[144,512]{1,0:T(8,128)(2,1)S(1)}, u32[]{:S(2)}, u32[]{:S(2)}) %collective-permute-start.4) | collective-permute-done | bytes 147488 | tf_op jit(solution)/shard_map/ppermute | solution.py:131
  132.6 0.5 slice.18
  133.8 0.7 fusion.1
  (15 shorter events, 0.3 us)
Async XLA Ops:
  8.3 27.2 %all-to-all-start = ((bf16[8,128,128]{2,1,0:T(8,128)(2,1)}), bf16[8,128,128]{2,1,0:T(8,128)(2,1)S(1)}, u32[]{:S(2)}, u32[]{:S(2)}) async-start(bf16[8,128,128]{2,1,0:T(8,128)(2,1)} %bitcast.2), calls=%async_computation | async-start | bytes 524288 | tf_op jit(solution)/shard_map/all_to_all | solution.py:91
  25.8 72.1 %all-gather.2.cloned.1.call-start = ((), (), s32[]{:S(2)}) async-start(), calls=%async_computation.3 | async-start | bytes 2359296 | tf_op jit(solution)/shard_map/all_gather | solution.py:107
  26.8 8.8 %collective-permute-start = (bf16[128,1024]{1,0:T(8,128)(2,1)S(1)}, bf16[128,1024]{1,0:T(8,128)(2,1)S(1)}, u32[]{:S(2)}, u32[]{:S(2)}) collective-permute-start(bf16[128,1024]{1,0:T(8,128)(2,1)S(1)} %constant_dynamic-slice_fusion.1), channel_id=1, source_target_pairs={{16,144},{17,145},{18,146},{19,147},{20,148},{21,149},{22,150},{23... | collective-permute-start | bytes 786440 | tf_op jit(solution)/shard_map/ppermute | solution.py:89
  37.5 0.8 collective-permute-start.1
  40.4 57.5 %all-to-all-start.1 = ((bf16[8,128,512]{2,1,0:T(8,128)(2,1)}), bf16[8,128,512]{2,1,0:T(8,128)(2,1)S(1)}, u32[]{:S(2)}, u32[]{:S(2)}) async-start(bf16[8,128,512]{2,1,0:T(8,128)(2,1)} %broadcast_in_dim.84), calls=%async_computation.1 | async-start | bytes 2097152 | tf_op jit(solution)/shard_map/all_to_all | solution.py:117
  97.9 1.6 %copy-start = (bf16[1024,1024]{1,0:T(8,128)(2,1)S(1)}, bf16[1024,1024]{1,0:T(8,128)(2,1)}, u32[]{:S(2)}) copy-start(bf16[1024,1024]{1,0:T(8,128)(2,1)} %all-gather.2.cloned.1.call-done.left_ref) | copy-start | bytes 6291460
  109.3 11.7 %collective-permute-start.2 = (f16[144,512]{1,0:T(8,128)(2,1)S(1)}, f16[144,512]{1,0:T(8,128)(2,1)S(1)}, u32[]{:S(2)}, u32[]{:S(2)}) collective-permute-start(f16[144,512]{1,0:T(8,128)(2,1)S(1)} %concatenate.9), channel_id=1, source_target_pairs={{0,2},{2,0},{4,6},{6,4},{1,3},{3,1},{5,7},{7,5},{8,10},{10,8},{12,... | collective-permute-start | bytes 442376 | tf_op jit(solution)/shard_map/ppermute | solution.py:131
  113.5 10.7 %collective-permute-start.3 = (f16[144,512]{1,0:T(8,128)(2,1)S(1)}, f16[144,512]{1,0:T(8,128)(2,1)S(1)}, u32[]{:S(2)}, u32[]{:S(2)}) collective-permute-start(f16[144,512]{1,0:T(8,128)(2,1)S(1)} %concatenate.10), channel_id=1, source_target_pairs={{0,4},{2,6},{4,0},{6,2},{1,5},{3,7},{5,1},{7,3},{8,12},{10,14},{12... | collective-permute-start | bytes 442376 | tf_op jit(solution)/shard_map/ppermute | solution.py:131
  118.7 13.9 %collective-permute-start.4 = (f16[144,512]{1,0:T(8,128)(2,1)S(1)}, f16[144,512]{1,0:T(8,128)(2,1)S(1)}, u32[]{:S(2)}, u32[]{:S(2)}) collective-permute-start(f16[144,512]{1,0:T(8,128)(2,1)S(1)} %concatenate.11), channel_id=1, source_target_pairs={{0,6},{2,4},{4,2},{6,0},{1,7},{3,5},{5,3},{7,1},{8,14},{10,12},{12... | collective-permute-start | bytes 442376 | tf_op jit(solution)/shard_map/ppermute | solution.py:131
Sparse Core Ops, SparseCore 0:
  37.6 51.4 all-gather.1

commit v10 on v9

--- a/solution.py
+++ b/solution.py
@@ -10,20 +10,85 @@
 TAIL = 16
 
 
-def product_kernel(z_ref, left_ref, right_ref, out_ref, ordered):
+def blocks_kernel(k_ref, stored_ref, band_ref, turned_ref):
+    band_ref[...] = stored_ref[...]
+    for j in range(turned_ref.shape[0]):
+        turned_ref[j] = stored_ref[:, j * B : (j + 1) * B].T
+
+
+def blocks(stored, k, wide):
+    count = wide // B
+    return pl.pallas_call(
+        blocks_kernel,
+        grid_spec=pltpu.PrefetchScalarGridSpec(
+            num_scalar_prefetch=1,
+            grid=(1,),
+            in_specs=[pl.BlockSpec((B, wide), lambda m, k_ref: (0, k_ref[0]))],
+            out_specs=[
+                pl.BlockSpec((B, wide), lambda m, _: (0, 0)),
+                pl.BlockSpec((count, B, B), lambda m, _: (0, 0, 0)),
+            ],
+        ),
+        out_shape=[
+            jax.ShapeDtypeStruct((B, wide), stored.dtype),
+            jax.ShapeDtypeStruct((count, B, B), stored.dtype),
+        ],
+        cost_estimate=pl.CostEstimate(flops=0, bytes_accessed=6 * B * wide, transcendentals=0),
+        name="blocks",
+    )(k.reshape(1), stored)
+
+
+def left_kernel(at_ref, band_ref, straight_ref, crossed_ref, row_ref, column_ref, out_ref):
+    k, z, l = at_ref[0], at_ref[1], at_ref[2]
+    count = crossed_ref.shape[0]
+    position = k * count * B + l * B + lax.broadcasted_iota(jnp.int32, (B, B), 0)
+    for j in range(count):
+        part = slice(j * B, (j + 1) * B)
+        across = (z * count + j) * B + lax.broadcasted_iota(jnp.int32, (B, B), 1)
+        band = band_ref[:, part].astype(jnp.float32)
+        straight = jnp.where(k == z, band, straight_ref[:, part].astype(jnp.float32))
+        straight = straight * row_ref[:, part]
+        crossed = crossed_ref[j].astype(jnp.float32) * column_ref[:, part]
+        out_ref[:, part] = jnp.where(position <= across, straight, crossed).astype(out_ref.dtype)
+
+
+def left_piece(at, band, straight, crossed, row, column):
+    rows, wide = band.shape
+    whole = pl.BlockSpec((rows, wide), lambda m, _: (0, 0))
+    vector = pl.BlockSpec((1, wide), lambda m, _: (0, 0))
+    return pl.pallas_call(
+        left_kernel,
+        grid_spec=pltpu.PrefetchScalarGridSpec(
+            num_scalar_prefetch=1,
+            grid=(1,),
+            in_specs=[whole, whole, pl.BlockSpec(crossed.shape, lambda m, _: (0, 0, 0)), vector, vector],
+            out_specs=whole,
+        ),
+        out_shape=jax.ShapeDtypeStruct((rows, wide), band.dtype),
+        cost_estimate=pl.CostEstimate(flops=0, bytes_accessed=8 * rows * wide, transcendentals=0),
+        name="left_piece",
+    )(at, band, straight, crossed, row, column)
+
+
+def product_kernel(z_ref, left_ref, right_ref, out_ref, ordered, buffer, arrived):
     n, depth, _ = right_ref.shape
+    count, _, step = buffer.shape
     z = z_ref[0]
-
-    @pl.when(pl.program_id(0) == 0)
-    def _():
-        for p in range(n):
-            ordered[p * depth : (p + 1) * depth, :] = right_ref[lax.rem(p - z + n, n)]
-
-    total = lax.dot_general(
-        left_ref[...], ordered[...], (((0,), (0,)), ((), ())), preferred_element_type=jnp.float32
-    )
-    for a in range(out_ref.shape[0]):
-        out_ref[a, 0] = total[a * B : (a + 1) * B]
+    copies = [
+        pltpu.make_async_copy(left_ref.at[:, m * step : (m + 1) * step], buffer.at[m], arrived.at[m])
+        for m in range(count)
+    ]
+    for copy in copies:
+        copy.start()
+    for p in range(n):
+        ordered[p * depth : (p + 1) * depth, :] = right_ref[lax.rem(p - z + n, n)]
+    for m, copy in enumerate(copies):
+        copy.wait()
+        total = lax.dot_general(
+            buffer[m], ordered[...], (((0,), (0,)), ((), ())), preferred_element_type=jnp.float32
+        )
+        for a in range(out_ref.shape[0]):
+            out_ref[a, m] = total[a * B : (a + 1) * B]
 
 
 def product(left, right, z, cores):
@@ -32,16 +97,17 @@
     step = cores * B
     return pl.pallas_call(
         product_kernel,
-        grid_spec=pltpu.PrefetchScalarGridSpec(
-            num_scalar_prefetch=1,
-            grid=(wide // step,),
-            in_specs=[
-                pl.BlockSpec((n * depth, step), lambda m, _: (0, m)),
-                pl.BlockSpec((n, depth, panel), lambda m, _: (0, 0, 0)),
-            ],
-            out_specs=pl.BlockSpec((cores, 1, B, panel), lambda m, _: (0, m, 0, 0)),
-            scratch_shapes=[pltpu.VMEM((n * depth, panel), left.dtype)],
-        ),
+        in_specs=[
+            pl.BlockSpec(memory_space=pltpu.SMEM),
+            pl.BlockSpec(memory_space=pltpu.HBM),
+            pl.BlockSpec(memory_space=pltpu.VMEM),
+        ],
+        out_specs=pl.BlockSpec(memory_space=pltpu.VMEM),
+        scratch_shapes=[
+            pltpu.VMEM((n * depth, panel), left.dtype),
+            pltpu.VMEM((wide // step, n * depth, step), left.dtype),
+            pltpu.SemaphoreType.DMA((wide // step,)),
+        ],
         out_shape=jax.ShapeDtypeStruct((cores, wide // step, B, panel), jnp.float32),
         compiler_params=pltpu.CompilerParams(vmem_limit_bytes=24 * 1024 * 1024),
         cost_estimate=pl.CostEstimate(
@@ -85,34 +151,36 @@
         return found
 
     k = lax.rem(y - z + nz, nz)
-    band = columns(k * plane, plane)
+    band, turned = blocks(stored, k, plane)
     straight = lax.ppermute(band, AXES, pairs(lambda a, b, c: (c, b), 1))
-    turned = band.T.reshape(nl, B, B)
     crossed = lax.all_to_all(turned, ("u", "v", "core"), split_axis=0, concat_axis=0, tiled=True)
     first = y * nl + w * (nl // nw)
     present = (
-        here(k * nl + l, z * nl, nl, True),
-        here(k * nl + l, z * nl, nl, False),
+        here(k * nl + l, z * nl, nl, True).astype(jnp.float32),
+        here(k * nl + l, z * nl, nl, False).astype(jnp.float32),
         here(g, first, nl // nw, True),
         here(g, first, nl // nw, False),
     )
     crossed, present = lax.optimization_barrier((crossed, present))
-    crossed = crossed.transpose(1, 0, 2).reshape(B, plane)
-    zero = jnp.zeros((), stored.dtype)
-    offset = l * B + jnp.arange(B, dtype=jnp.int32)[:, None]
-    across = jnp.arange(plane, dtype=jnp.int32)[None, :]
-    above = k * plane + offset <= z * plane + across
-    kept = jnp.where(above, present[0], present[1])
-    left = jnp.where(kept, jnp.where(above, jnp.where(k == z, band, straight), crossed), zero)
+    left = left_piece(
+        jnp.stack([k, z, l]),
+        band,
+        straight,
+        crossed,
+        present[0],
+        present[1],
+    )
     left = lax.all_gather(left, "y", axis=0, tiled=True)
 
-    half = lax.dynamic_slice(crossed, (0, w * panel), (B, panel))
+    half = lax.dynamic_slice(crossed, (w * (nl // nw), 0, 0), (nl // nw, B, B))
+    half = half.transpose(1, 0, 2).reshape(B, panel)
     half = lax.ppermute(half, AXES, pairs(lambda a, b, c: (c, a), 0))
     tile = columns(y * plane + w * panel, panel)
     own = y * plane + w * panel + jnp.arange(panel, dtype=jnp.int32)[None, :]
+    offset = l * B + jnp.arange(B, dtype=jnp.int32)[:, None]
     above = z * plane + offset <= own
     kept = jnp.where(above, present[2], present[3])
-    right = jnp.where(kept, jnp.where(above, tile, half), zero)
+    right = jnp.where(kept, jnp.where(above, tile, half), jnp.zeros((), stored.dtype))
     right = jnp.broadcast_to(right[None], (nz, B, panel))
     right = lax.all_to_all(right, "z", split_axis=0, concat_axis=0, tiled=True)
 

time: 142 us -> 145 us (1.021)
  Pallas kernels: 2.42 us -> 6.74 us
  other arithmetic: 8.11 us -> 6.01 us
  starting transfers between devices: 58.4 us -> 56.9 us
    pallas_call x1 -> x3, Pallas kernels: 2.42 us -> 6.74 us  [the longest x1 2.67 us: left_piece(): pl.pallas_call(left_kernel, grid_spec=pltpu.PrefetchScalarGridSpec(num_sc...]
    select_n x2 -> x1, other arithmetic: 2.92 us -> 0.27 us  [body(): jnp.where(kept, jnp.where(above, tile, half), jnp.zeros((), stored.dtype))]
    gt x4 -> x2, other arithmetic: 3.28 us -> 1.64 us  [here(): return jnp.repeat(found, B, axis=1) > 0]
    convert_element_type x0 -> x2, other arithmetic: none -> 1.63 us  [the longest x1 0.87 us: body(): here(k * nl + l, z * nl, nl, False).astype(jnp.float32)]
    all_to_all x1, starting transfers between devices: 28.2 us -> 26.7 us  [body(): right = lax.all_to_all(right, 'z', split_axis=0, concat_axis=0, tiled=True)]
  transfers between devices with their start and end apart: 8 -> 8, of which waited for: 5 -> 4; matrix products, arithmetic and copies ran while one was open for 6% -> 7% of each run, Pallas kernels for 0% -> 0%
where the time goes in v10:
time: 145 us; the launch traced here: 144 us
  starting transfers between devices  56.9 us (39%)
  waiting for transfers between devices  43.7 us (30%)
  between operations  16.4 us (11%)
  local copies, waits for them, and re-layouts  8.71 us (6%)
  Pallas kernels  6.74 us (5%)
  other arithmetic  6.01 us (4%)
  blocking collectives  5.53 us (4%)
    all_to_all x1, waiting for transfers between devices, body(): right = lax.all_to_all(right, 'z', split_axis=0, concat_axis=0, tiled=True)  29.2 us
    all_to_all x1, starting transfers between devices, body(): right = lax.all_to_all(right, 'z', split_axis=0, concat_axis=0, tiled=True)  26.7 us
    all_to_all x1, starting transfers between devices, body(): lax.all_to_all(turned, ('u', 'v', 'core'), split_axis=0, concat_axis=0, t...  17.5 us
    ppermute x3, starting transfers between devices, body(): got = lax.ppermute(chunk, ('u', 'v'), [(a, a ^ d) for a in range(nu * nv)])  11.4 us
    ppermute x3, waiting for transfers between devices, body(): got = lax.ppermute(chunk, ('u', 'v'), [(a, a ^ d) for a in range(nu * nv)])  9.44 us
    all_to_all x1, blocking collectives, body(): lax.all_to_all(partial, 'core', split_axis=0, concat_axis=0, tiled=True)  5.53 us
    all_to_all x1, waiting for transfers between devices, body(): lax.all_to_all(turned, ('u', 'v', 'core'), split_axis=0, concat_axis=0, t...  4.96 us
  transfers between devices with their start and end apart: 8, of which 4 were waited for; matrix products, arithmetic and copies ran while one was open for 7% of the time, Pallas kernels for 0%

profile of v10, /device:TPU:1, one launch (start us, length us, event | category | flops | bytes accessed | tf_op | source)
XLA Modules:
  0.0 143.9 jit_solution(10564598192344310873)
XLA Ops:
  6.5 1.8 %blocks.1 = (bf16[128,1024]{1,0:T(8,128)(2,1)}, bf16[8,128,128]{2,1,0:T(8,128)(2,1)}) custom-call(s32[1]{0:T(128)} %bitcast.1.k_ref, bf16[128,8192]{1,0:T(8,128)(2,1)} %stored_ref.1), custom_call_target="tpu_custom_call" | custom-call | bytes 786432 | tf_op jit(solution)/shard_map/blocks/pallas_call | solution.py:21
  8.3 17.5 %all-to-all-start = ((bf16[8,128,128]{2,1,0:T(8,128)(2,1)}), bf16[8,128,128]{2,1,0:T(8,128)(2,1)S(1)}, u32[]{:S(2)}, u32[]{:S(2)}) async-start(bf16[8,128,128]{2,1,0:T(8,128)(2,1)} %get-tuple-element.13), calls=%async_computation | async-start | bytes 524288 | tf_op jit(solution)/shard_map/all_to_all | solution.py:156
  25.8 0.0 all-gather.2.cloned.1.call-start
  25.8 0.7 collective-permute-start
  26.5 0.9 fusion.5
  27.4 0.8 compare_bitcast_fusion
  28.2 0.1 broadcast_bitcast_fusion
  28.2 0.1 broadcast_bitcast_fusion.1
  28.3 0.8 fusion.6
  29.1 0.6 pad_add_fusion.at_ref
  29.7 0.9 convert_reduce_fusion
  30.5 5.0 %all-to-all-done.crossed_ref = bf16[8,128,128]{2,1,0:T(8,128)(2,1)S(1)} async-done(((bf16[8,128,128]{2,1,0:T(8,128)(2,1)}), bf16[8,128,128]{2,1,0:T(8,128)(2,1)S(1)}, u32[]{:S(2)}, u32[]{:S(2)}) %all-to-all-start) | async-done | bytes 262176 | tf_op jit(solution)/shard_map/all_to_all | solution.py:156
  35.5 0.0 copy-start.1
  35.5 0.7 broadcast_in_dim.45
  36.2 0.7 broadcast_in_dim.46
  36.8 0.0 collective-permute-done.straight_ref
  36.8 0.0 copy-done.1
  36.8 0.0 copy-start.2
  36.9 0.7 copy-done.2
  37.6 2.7 %left_piece.1 = bf16[128,1024]{1,0:T(8,128)(2,1)} custom-call(s32[3]{0:T(128)} %pad_add_fusion.at_ref, bf16[128,1024]{1,0:T(8,128)(2,1)} %get-tuple-element.12.band_ref, bf16[128,1024]{1,0:T(8,128)(2,1)} %copy-done.2, bf16[8,128,128]{2,1,0:T(8,128)(2,1)} %copy-done.1, f32[1,1024]{1,0:T(1,128)} %bitcast.36, f32[1,1024]{1,0:T(1,128)} %bitcast.37), custom_call_target="tpu_custom_call" | custom-call | bytes 1048576 | tf_op jit(solution)/shard_map/left_piece/pallas_call | solution.py:59
  40.2 0.0 all-gather.2.cloned.1.call-update
  40.3 0.9 constant_dynamic-slice_fusion
  41.2 0.9 dynamic-slice_bitcast_fusion
  42.1 0.1 copy.4
  42.2 0.7 collective-permute-start.1
  42.9 0.1 copy.6
  43.1 0.0 collective-permute-done.1
  43.1 0.3 fusion.1
  43.4 0.1 copy.5
  43.5 1.1 broadcast_in_dim.54
  44.6 26.7 %all-to-all-start.1 = ((bf16[8,128,512]{2,1,0:T(8,128)(2,1)}), bf16[8,128,512]{2,1,0:T(8,128)(2,1)S(1)}, u32[]{:S(2)}, u32[]{:S(2)}) async-start(bf16[8,128,512]{2,1,0:T(8,128)(2,1)} %broadcast_in_dim.54), calls=%async_computation.1 | async-start | bytes 2097152 | tf_op jit(solution)/shard_map/all_to_all | solution.py:185
  71.3 29.2 %all-to-all-done.1.right_ref = bf16[8,128,512]{2,1,0:T(8,128)(2,1)S(1)} async-done(((bf16[8,128,512]{2,1,0:T(8,128)(2,1)}), bf16[8,128,512]{2,1,0:T(8,128)(2,1)S(1)}, u32[]{:S(2)}, u32[]{:S(2)}) %all-to-all-start.1) | async-done | bytes 1048608 | tf_op jit(solution)/shard_map/all_to_all | solution.py:185
  100.5 1.6 %copy-done = bf16[1024,1024]{1,0:T(8,128)(2,1)S(1)} copy-done((bf16[1024,1024]{1,0:T(8,128)(2,1)S(1)}, bf16[1024,1024]{1,0:T(8,128)(2,1)}, u32[]{:S(2)}) %copy-start) | copy-done | bytes 2097176
  102.1 2.3 %product.1 = f32[2,4,128,512]{3,2,1,0:T(8,128)S(1)} custom-call(s32[1]{0:T(128)} %bitcast.z_ref, bf16[1024,1024]{1,0:T(8,128)(2,1)S(1)} %copy-done, bf16[8,128,512]{2,1,0:T(8,128)(2,1)S(1)} %all-to-all-done.1.right_ref), custom_call_target="tpu_custom_call" | custom-call | flops 1073741824 | bytes 5242880 | tf_op jit(solution)/shard_map/product/pallas_call | solution.py:98
  104.4 5.5 %all_to_all.15 = f32[2,4,128,512]{3,2,1,0:T(8,128)S(1)} all-to-all(f32[2,4,128,512]{3,2,1,0:T(8,128)S(1)} %product.1), channel_id=1, replica_groups=mesh['z'=8,'y'=8,'w'=2,'u'=2,'v'=2,'core'=2] {'core'}, dimensions={0} | all-to-all | bytes 4194304 | tf_op jit(solution)/shard_map/all_to_all | solution.py:188
  109.9 0.3 reduce_sum.9
  110.2 0.7 abs_reduce_fusion
  111.6 0.1 fusion.2
  111.8 3.7 %collective-permute-start.2 = (f16[144,512]{1,0:T(8,128)(2,1)S(1)}, f16[144,512]{1,0:T(8,128)(2,1)S(1)}, u32[]{:S(2)}, u32[]{:S(2)}) collective-permute-start(f16[144,512]{1,0:T(8,128)(2,1)S(1)} %concatenate.9), channel_id=1, source_target_pairs={{0,2},{2,0},{4,6},{6,4},{1,3},{3,1},{5,7},{7,5},{8,10},{10,8},{12,... | collective-permute-start | bytes 442376 | tf_op jit(solution)/shard_map/ppermute | solution.py:199
  115.5 5.2 %collective-permute-start.3 = (f16[144,512]{1,0:T(8,128)(2,1)S(1)}, f16[144,512]{1,0:T(8,128)(2,1)S(1)}, u32[]{:S(2)}, u32[]{:S(2)}) collective-permute-start(f16[144,512]{1,0:T(8,128)(2,1)S(1)} %concatenate.10), channel_id=1, source_target_pairs={{0,4},{2,6},{4,0},{6,2},{1,5},{3,7},{5,1},{7,3},{8,12},{10,14},{12... | collective-permute-start | bytes 442376 | tf_op jit(solution)/shard_map/ppermute | solution.py:199
  120.7 2.5 %collective-permute-start.4 = (f16[144,512]{1,0:T(8,128)(2,1)S(1)}, f16[144,512]{1,0:T(8,128)(2,1)S(1)}, u32[]{:S(2)}, u32[]{:S(2)}) collective-permute-start(f16[144,512]{1,0:T(8,128)(2,1)S(1)} %concatenate.11), channel_id=1, source_target_pairs={{0,6},{2,4},{4,2},{6,0},{1,7},{3,5},{5,3},{7,1},{8,14},{10,12},{12... | collective-permute-start | bytes 442376 | tf_op jit(solution)/shard_map/ppermute | solution.py:199
  123.3 0.0 collective-permute-done.2
  123.3 0.5 slice.16
  124.5 1.7 %collective-permute-done.3 = f16[144,512]{1,0:T(8,128)(2,1)S(1)} collective-permute-done((f16[144,512]{1,0:T(8,128)(2,1)S(1)}, f16[144,512]{1,0:T(8,128)(2,1)S(1)}, u32[]{:S(2)}, u32[]{:S(2)}) %collective-permute-start.3) | collective-permute-done | bytes 147488 | tf_op jit(solution)/shard_map/ppermute | solution.py:199
  126.2 0.5 slice.17
  127.4 7.7 %collective-permute-done.4 = f16[144,512]{1,0:T(8,128)(2,1)S(1)} collective-permute-done((f16[144,512]{1,0:T(8,128)(2,1)S(1)}, f16[144,512]{1,0:T(8,128)(2,1)S(1)}, u32[]{:S(2)}, u32[]{:S(2)}) %collective-permute-start.4) | collective-permute-done | bytes 147488 | tf_op jit(solution)/shard_map/ppermute | solution.py:199
  135.1 0.5 slice.18
  136.3 0.7 fusion
  (10 shorter events, 0.1 us)
Async XLA Ops:
  8.3 27.2 %all-to-all-start = ((bf16[8,128,128]{2,1,0:T(8,128)(2,1)}), bf16[8,128,128]{2,1,0:T(8,128)(2,1)S(1)}, u32[]{:S(2)}, u32[]{:S(2)}) async-start(bf16[8,128,128]{2,1,0:T(8,128)(2,1)} %get-tuple-element.13), calls=%async_computation | async-start | bytes 524288 | tf_op jit(solution)/shard_map/all_to_all | solution.py:156
  25.8 74.7 %all-gather.2.cloned.1.call-start = ((), (), s32[]{:S(2)}) async-start(), calls=%async_computation.3 | async-start | bytes 2359296 | tf_op jit(solution)/shard_map/all_gather | solution.py:173
  25.8 11.0 %collective-permute-start = (bf16[128,1024]{1,0:T(8,128)(2,1)}, bf16[128,1024]{1,0:T(8,128)(2,1)S(1)}, u32[]{:S(2)}, u32[]{:S(2)}) collective-permute-start(bf16[128,1024]{1,0:T(8,128)(2,1)} %get-tuple-element.12.band_ref), channel_id=1, source_target_pairs={{16,144},{17,145},{18,146},{19,147},{20,148},{21,149},{22,150},{23... | collective-permute-start | bytes 786440 | tf_op jit(solution)/shard_map/ppermute | solution.py:155
  35.5 1.3 copy-start.1
  36.8 0.7 copy-start.2
  42.2 0.9 collective-permute-start.1
  44.6 55.9 %all-to-all-start.1 = ((bf16[8,128,512]{2,1,0:T(8,128)(2,1)}), bf16[8,128,512]{2,1,0:T(8,128)(2,1)S(1)}, u32[]{:S(2)}, u32[]{:S(2)}) async-start(bf16[8,128,512]{2,1,0:T(8,128)(2,1)} %broadcast_in_dim.54), calls=%async_computation.1 | async-start | bytes 2097152 | tf_op jit(solution)/shard_map/all_to_all | solution.py:185
  100.5 1.6 %copy-start = (bf16[1024,1024]{1,0:T(8,128)(2,1)S(1)}, bf16[1024,1024]{1,0:T(8,128)(2,1)}, u32[]{:S(2)}) copy-start(bf16[1024,1024]{1,0:T(8,128)(2,1)} %all-gather.2.cloned.1.call-done.left_ref) | copy-start | bytes 6291460
  111.8 11.5 %collective-permute-start.2 = (f16[144,512]{1,0:T(8,128)(2,1)S(1)}, f16[144,512]{1,0:T(8,128)(2,1)S(1)}, u32[]{:S(2)}, u32[]{:S(2)}) collective-permute-start(f16[144,512]{1,0:T(8,128)(2,1)S(1)} %concatenate.9), channel_id=1, source_target_pairs={{0,2},{2,0},{4,6},{6,4},{1,3},{3,1},{5,7},{7,5},{8,10},{10,8},{12,... | collective-permute-start | bytes 442376 | tf_op jit(solution)/shard_map/ppermute | solution.py:199
  115.5 10.7 %collective-permute-start.3 = (f16[144,512]{1,0:T(8,128)(2,1)S(1)}, f16[144,512]{1,0:T(8,128)(2,1)S(1)}, u32[]{:S(2)}, u32[]{:S(2)}) collective-permute-start(f16[144,512]{1,0:T(8,128)(2,1)S(1)} %concatenate.10), channel_id=1, source_target_pairs={{0,4},{2,6},{4,0},{6,2},{1,5},{3,7},{5,1},{7,3},{8,12},{10,14},{12... | collective-permute-start | bytes 442376 | tf_op jit(solution)/shard_map/ppermute | solution.py:199
  120.7 14.4 %collective-permute-start.4 = (f16[144,512]{1,0:T(8,128)(2,1)S(1)}, f16[144,512]{1,0:T(8,128)(2,1)S(1)}, u32[]{:S(2)}, u32[]{:S(2)}) collective-permute-start(f16[144,512]{1,0:T(8,128)(2,1)S(1)} %concatenate.11), channel_id=1, source_target_pairs={{0,6},{2,4},{4,2},{6,0},{1,7},{3,5},{5,3},{7,1},{8,14},{10,12},{12... | collective-permute-start | bytes 442376 | tf_op jit(solution)/shard_map/ppermute | solution.py:199
Sparse Core Ops, SparseCore 0:
  40.4 49.3 all-gather.1

commit v11 on v9

--- a/solution.py
+++ b/solution.py
@@ -3,6 +3,7 @@
 from jax import lax
 from jax.experimental import pallas as pl
 from jax.experimental.pallas import tpu as pltpu
+from jax.experimental.layout import Layout, with_layout_constraint
 from jax.sharding import Mesh, PartitionSpec as P
 
 B = 128
@@ -19,16 +20,18 @@
         for p in range(n):
             ordered[p * depth : (p + 1) * depth, :] = right_ref[lax.rem(p - z + n, n)]
 
-    total = lax.dot_general(
-        left_ref[...], ordered[...], (((0,), (0,)), ((), ())), preferred_element_type=jnp.float32
-    )
     for a in range(out_ref.shape[0]):
-        out_ref[a, 0] = total[a * B : (a + 1) * B]
+        out_ref[a, 0] = lax.dot_general(
+            left_ref[:, a].reshape(n * depth, B),
+            ordered[...],
+            (((0,), (0,)), ((), ())),
+            preferred_element_type=jnp.float32,
+        )
 
 
 def product(left, right, z, cores):
     n, depth, panel = right.shape
-    wide = left.shape[1]
+    wide = left.shape[1] * B
     step = cores * B
     return pl.pallas_call(
         product_kernel,
@@ -36,14 +39,14 @@
             num_scalar_prefetch=1,
             grid=(wide // step,),
             in_specs=[
-                pl.BlockSpec((n * depth, step), lambda m, _: (0, m)),
+                pl.BlockSpec((n, cores, depth, B), lambda m, _: (0, m, 0, 0)),
                 pl.BlockSpec((n, depth, panel), lambda m, _: (0, 0, 0)),
             ],
             out_specs=pl.BlockSpec((cores, 1, B, panel), lambda m, _: (0, m, 0, 0)),
             scratch_shapes=[pltpu.VMEM((n * depth, panel), left.dtype)],
         ),
         out_shape=jax.ShapeDtypeStruct((cores, wide // step, B, panel), jnp.float32),
-        compiler_params=pltpu.CompilerParams(vmem_limit_bytes=24 * 1024 * 1024),
+        compiler_params=pltpu.CompilerParams(vmem_limit_bytes=56 * 1024 * 1024),
         cost_estimate=pl.CostEstimate(
             flops=2 * n * depth * wide * panel,
             bytes_accessed=2 * n * depth * (wide + panel) + 4 * wide * panel,
@@ -85,9 +88,9 @@
         return found
 
     k = lax.rem(y - z + nz, nz)
-    band = columns(k * plane, plane)
+    band = columns(k * plane, plane).reshape(B, nl, B).transpose(1, 0, 2)
     straight = lax.ppermute(band, AXES, pairs(lambda a, b, c: (c, b), 1))
-    turned = band.T.reshape(nl, B, B)
+    turned = columns(k * plane, plane).T.reshape(nl, B, B)
     crossed = lax.all_to_all(turned, ("u", "v", "core"), split_axis=0, concat_axis=0, tiled=True)
     first = y * nl + w * (nl // nw)
     present = (
@@ -97,20 +100,20 @@
         here(g, first, nl // nw, False),
     )
     crossed, present = lax.optimization_barrier((crossed, present))
-    crossed = crossed.transpose(1, 0, 2).reshape(B, plane)
     zero = jnp.zeros((), stored.dtype)
-    offset = l * B + jnp.arange(B, dtype=jnp.int32)[:, None]
-    across = jnp.arange(plane, dtype=jnp.int32)[None, :]
-    above = k * plane + offset <= z * plane + across
-    kept = jnp.where(above, present[0], present[1])
+    offset = l * B + jnp.arange(B, dtype=jnp.int32)
+    across = jnp.arange(plane, dtype=jnp.int32).reshape(nl, 1, B)
+    above = k * plane + offset[None, :, None] <= z * plane + across
+    kept = jnp.where(above, present[0].reshape(nl, 1, B), present[1].reshape(nl, 1, B))
     left = jnp.where(kept, jnp.where(above, jnp.where(k == z, band, straight), crossed), zero)
-    left = lax.all_gather(left, "y", axis=0, tiled=True)
+    left = lax.all_gather(left, "y", axis=0, tiled=True).reshape(ny, nl, B, B)
 
-    half = lax.dynamic_slice(crossed, (0, w * panel), (B, panel))
+    half = with_layout_constraint(crossed.transpose(1, 0, 2).reshape(B, plane), Layout((0, 1)))
+    half = lax.dynamic_slice(half, (0, w * panel), (B, panel))
     half = lax.ppermute(half, AXES, pairs(lambda a, b, c: (c, a), 0))
     tile = columns(y * plane + w * panel, panel)
     own = y * plane + w * panel + jnp.arange(panel, dtype=jnp.int32)[None, :]
-    above = z * plane + offset <= own
+    above = z * plane + offset[:, None] <= own
     kept = jnp.where(above, present[2], present[3])
     right = jnp.where(kept, jnp.where(above, tile, half), zero)
     right = jnp.broadcast_to(right[None], (nz, B, panel))

time: 142 us -> 145 us (1.021)
  Pallas kernels: 2.42 us -> 5.07 us
    pallas_call x1, Pallas kernels: 2.42 us -> 5.07 us  [product(): pl.pallas_call(product_kernel, grid_spec=pltpu.PrefetchScalarGridSpec(num...]
where the time goes in v11:
time: 145 us; the launch traced here: 144 us
  starting transfers between devices  58.6 us (40%)
  waiting for transfers between devices  42.9 us (30%)
  between operations  16.4 us (11%)
  other arithmetic  7.17 us (5%)
  local copies, waits for them, and re-layouts  6.98 us (5%)
  blocking collectives  6.74 us (5%)
  Pallas kernels  5.07 us (3%)
    all_to_all x1, waiting for transfers between devices, body(): right = lax.all_to_all(right, 'z', split_axis=0, concat_axis=0, tiled=True)  29.2 us
    all_to_all x1, starting transfers between devices, body(): right = lax.all_to_all(right, 'z', split_axis=0, concat_axis=0, tiled=True)  28.4 us
    all_to_all x1, starting transfers between devices, body(): lax.all_to_all(turned, ('u', 'v', 'core'), split_axis=0, concat_axis=0, t...  17.5 us
    ppermute x3, starting transfers between devices, body(): got = lax.ppermute(chunk, ('u', 'v'), [(a, a ^ d) for a in range(nu * nv)])  11.4 us
    ppermute x3, waiting for transfers between devices, body(): got = lax.ppermute(chunk, ('u', 'v'), [(a, a ^ d) for a in range(nu * nv)])  9.44 us
    all_to_all x1, blocking collectives, body(): lax.all_to_all(partial, 'core', split_axis=0, concat_axis=0, tiled=True)  6.74 us
    pallas_call x1, Pallas kernels, product(): pl.pallas_call(product_kernel, grid_spec=pltpu.PrefetchScalarGridSpec(num...  5.07 us
    all_to_all x1, waiting for transfers between devices, body(): lax.all_to_all(turned, ('u', 'v', 'core'), split_axis=0, concat_axis=0, t...  4.21 us
  transfers between devices with their start and end apart: 8, of which 5 were waited for; matrix products, arithmetic and copies ran while one was open for 6% of the time, Pallas kernels for 0%

profile of v11, /device:TPU:1, one launch (start us, length us, event | category | flops | bytes accessed | tf_op | source)
XLA Modules:
  0.0 143.9 jit_solution(4960888538059210067)
XLA Ops:
  6.5 1.0 constant_dynamic-slice_fusion.1
  7.5 0.8 copy.14
  8.3 17.5 %all-to-all-start = ((bf16[8,128,128]{2,1,0:T(8,128)(2,1)}), bf16[8,128,128]{2,1,0:T(8,128)(2,1)S(1)}, u32[]{:S(2)}, u32[]{:S(2)}) async-start(bf16[8,128,128]{2,1,0:T(8,128)(2,1)} %bitcast.2), calls=%async_computation | async-start | bytes 524288 | tf_op jit(solution)/shard_map/all_to_all | solution.py:94
  25.8 0.0 all-gather.2.cloned.1.call-start
  25.8 1.1 copy.12
  27.0 0.7 collective-permute-start
  27.7 0.9 fusion.6
  28.6 0.8 compare_bitcast_fusion.1
  29.3 0.9 fusion.7
  30.2 0.8 compare_bitcast_fusion
  31.0 0.1 broadcast_bitcast_fusion
  31.0 0.1 broadcast_bitcast_fusion.2
  31.1 0.1 broadcast_bitcast_fusion.3
  31.2 0.1 broadcast_bitcast_fusion.1
  31.3 4.2 %all-to-all-done = bf16[8,128,128]{2,1,0:T(8,128)(2,1)S(1)} async-done(((bf16[8,128,128]{2,1,0:T(8,128)(2,1)}), bf16[8,128,128]{2,1,0:T(8,128)(2,1)S(1)}, u32[]{:S(2)}, u32[]{:S(2)}) %all-to-all-start) | async-done | bytes 262176 | tf_op jit(solution)/shard_map/all_to_all | solution.py:94
  35.5 0.0 collective-permute-done
  35.6 0.9 fusion
  36.5 0.0 all-gather.2.cloned.1.call-update
  36.6 0.7 collective-permute-start.1
  37.3 0.0 collective-permute-done.1
  37.3 1.0 fusion.2
  38.4 1.1 broadcast_in_dim.84
  39.5 28.4 %all-to-all-start.1 = ((bf16[8,128,512]{2,1,0:T(8,128)(2,1)}), bf16[8,128,512]{2,1,0:T(8,128)(2,1)S(1)}, u32[]{:S(2)}, u32[]{:S(2)}) async-start(bf16[8,128,512]{2,1,0:T(8,128)(2,1)} %broadcast_in_dim.84), calls=%async_computation.1 | async-start | bytes 2097152 | tf_op jit(solution)/shard_map/all_to_all | solution.py:120
  67.9 29.2 %all-to-all-done.1.right_ref = bf16[8,128,512]{2,1,0:T(8,128)(2,1)S(1)} async-done(((bf16[8,128,512]{2,1,0:T(8,128)(2,1)}), bf16[8,128,512]{2,1,0:T(8,128)(2,1)S(1)}, u32[]{:S(2)}, u32[]{:S(2)}) %all-to-all-start.1) | async-done | bytes 1048608 | tf_op jit(solution)/shard_map/all_to_all | solution.py:120
  97.1 0.0 copy-start
  97.1 0.0 all-gather.2.cloned.1.call-done
  97.1 1.0 copy-done
  98.1 5.1 %product.1 = f32[2,4,128,512]{3,2,1,0:T(8,128)} custom-call(s32[1]{0:T(128)} %bitcast.z_ref, bf16[8,8,128,128]{3,2,1,0:T(8,128)(2,1)} %bitcast.53, bf16[8,128,512]{2,1,0:T(8,128)(2,1)} %copy-done), custom_call_target="tpu_custom_call" | custom-call | flops 1073741824 | bytes 5242880 | tf_op jit(solution)/shard_map/product/pallas_call | solution.py:36
  103.1 6.7 %all_to_all.15 = f32[2,4,128,512]{3,2,1,0:T(8,128)S(1)} all-to-all(f32[2,4,128,512]{3,2,1,0:T(8,128)} %product.1), channel_id=1, replica_groups=mesh['z'=8,'y'=8,'w'=2,'u'=2,'v'=2,'core'=2] {'core'}, dimensions={0} | all-to-all | bytes 4194304 | tf_op jit(solution)/shard_map/all_to_all | solution.py:123
  109.9 0.3 reduce_sum.9
  110.2 0.7 abs_reduce_fusion
  111.6 0.1 fusion.3
  111.7 4.2 %collective-permute-start.2 = (f16[144,512]{1,0:T(8,128)(2,1)S(1)}, f16[144,512]{1,0:T(8,128)(2,1)S(1)}, u32[]{:S(2)}, u32[]{:S(2)}) collective-permute-start(f16[144,512]{1,0:T(8,128)(2,1)S(1)} %concatenate.9), channel_id=1, source_target_pairs={{0,2},{2,0},{4,6},{6,4},{1,3},{3,1},{5,7},{7,5},{8,10},{10,8},{12,... | collective-permute-start | bytes 442376 | tf_op jit(solution)/shard_map/ppermute | solution.py:134
  115.9 5.2 %collective-permute-start.3 = (f16[144,512]{1,0:T(8,128)(2,1)S(1)}, f16[144,512]{1,0:T(8,128)(2,1)S(1)}, u32[]{:S(2)}, u32[]{:S(2)}) collective-permute-start(f16[144,512]{1,0:T(8,128)(2,1)S(1)} %concatenate.10), channel_id=1, source_target_pairs={{0,4},{2,6},{4,0},{6,2},{1,5},{3,7},{5,1},{7,3},{8,12},{10,14},{12... | collective-permute-start | bytes 442376 | tf_op jit(solution)/shard_map/ppermute | solution.py:134
  121.2 2.0 %collective-permute-start.4 = (f16[144,512]{1,0:T(8,128)(2,1)S(1)}, f16[144,512]{1,0:T(8,128)(2,1)S(1)}, u32[]{:S(2)}, u32[]{:S(2)}) collective-permute-start(f16[144,512]{1,0:T(8,128)(2,1)S(1)} %concatenate.11), channel_id=1, source_target_pairs={{0,6},{2,4},{4,2},{6,0},{1,7},{3,5},{5,3},{7,1},{8,14},{10,12},{12... | collective-permute-start | bytes 442376 | tf_op jit(solution)/shard_map/ppermute | solution.py:134
  123.2 0.2 collective-permute-done.2
  123.4 0.5 slice.16
  124.6 2.0 %collective-permute-done.3 = f16[144,512]{1,0:T(8,128)(2,1)S(1)} collective-permute-done((f16[144,512]{1,0:T(8,128)(2,1)S(1)}, f16[144,512]{1,0:T(8,128)(2,1)S(1)}, u32[]{:S(2)}, u32[]{:S(2)}) %collective-permute-start.3) | collective-permute-done | bytes 147488 | tf_op jit(solution)/shard_map/ppermute | solution.py:134
  126.6 0.5 slice.17
  127.9 7.2 %collective-permute-done.4 = f16[144,512]{1,0:T(8,128)(2,1)S(1)} collective-permute-done((f16[144,512]{1,0:T(8,128)(2,1)S(1)}, f16[144,512]{1,0:T(8,128)(2,1)S(1)}, u32[]{:S(2)}, u32[]{:S(2)}) %collective-permute-start.4) | collective-permute-done | bytes 147488 | tf_op jit(solution)/shard_map/ppermute | solution.py:134
  135.1 0.5 slice.18
  136.3 0.7 fusion.1
  (15 shorter events, 0.3 us)
Async XLA Ops:
  8.3 27.2 %all-to-all-start = ((bf16[8,128,128]{2,1,0:T(8,128)(2,1)}), bf16[8,128,128]{2,1,0:T(8,128)(2,1)S(1)}, u32[]{:S(2)}, u32[]{:S(2)}) async-start(bf16[8,128,128]{2,1,0:T(8,128)(2,1)} %bitcast.2), calls=%async_computation | async-start | bytes 524288 | tf_op jit(solution)/shard_map/all_to_all | solution.py:94
  25.8 71.3 %all-gather.2.cloned.1.call-start = ((), (), s32[]{:S(2)}) async-start(), calls=%async_computation.3 | async-start | bytes 2359296 | tf_op jit(solution)/shard_map/all_gather | solution.py:109
  27.0 8.6 %collective-permute-start = (bf16[8,128,128]{2,1,0:T(8,128)(2,1)S(1)}, bf16[8,128,128]{2,1,0:T(8,128)(2,1)S(1)}, u32[]{:S(2)}, u32[]{:S(2)}) collective-permute-start(bf16[8,128,128]{2,1,0:T(8,128)(2,1)S(1)} %bitcast.54), channel_id=1, source_target_pairs={{16,144},{17,145},{18,146},{19,147},{20,148},{21,149},{22,150},{23... | collective-permute-start | bytes 786440 | tf_op jit(solution)/shard_map/ppermute | solution.py:92
  36.6 0.8 collective-permute-start.1
  39.5 57.6 %all-to-all-start.1 = ((bf16[8,128,512]{2,1,0:T(8,128)(2,1)}), bf16[8,128,512]{2,1,0:T(8,128)(2,1)S(1)}, u32[]{:S(2)}, u32[]{:S(2)}) async-start(bf16[8,128,512]{2,1,0:T(8,128)(2,1)} %broadcast_in_dim.84), calls=%async_computation.1 | async-start | bytes 2097152 | tf_op jit(solution)/shard_map/all_to_all | solution.py:120
  97.1 1.0 copy-start
  111.7 11.7 %collective-permute-start.2 = (f16[144,512]{1,0:T(8,128)(2,1)S(1)}, f16[144,512]{1,0:T(8,128)(2,1)S(1)}, u32[]{:S(2)}, u32[]{:S(2)}) collective-permute-start(f16[144,512]{1,0:T(8,128)(2,1)S(1)} %concatenate.9), channel_id=1, source_target_pairs={{0,2},{2,0},{4,6},{6,4},{1,3},{3,1},{5,7},{7,5},{8,10},{10,8},{12,... | collective-permute-start | bytes 442376 | tf_op jit(solution)/shard_map/ppermute | solution.py:134
  115.9 10.7 %collective-permute-start.3 = (f16[144,512]{1,0:T(8,128)(2,1)S(1)}, f16[144,512]{1,0:T(8,128)(2,1)S(1)}, u32[]{:S(2)}, u32[]{:S(2)}) collective-permute-start(f16[144,512]{1,0:T(8,128)(2,1)S(1)} %concatenate.10), channel_id=1, source_target_pairs={{0,4},{2,6},{4,0},{6,2},{1,5},{3,7},{5,1},{7,3},{8,12},{10,14},{12... | collective-permute-start | bytes 442376 | tf_op jit(solution)/shard_map/ppermute | solution.py:134
  121.2 13.9 %collective-permute-start.4 = (f16[144,512]{1,0:T(8,128)(2,1)S(1)}, f16[144,512]{1,0:T(8,128)(2,1)S(1)}, u32[]{:S(2)}, u32[]{:S(2)}) collective-permute-start(f16[144,512]{1,0:T(8,128)(2,1)S(1)} %concatenate.11), channel_id=1, source_target_pairs={{0,6},{2,4},{4,2},{6,0},{1,7},{3,5},{5,3},{7,1},{8,14},{10,12},{12... | collective-permute-start | bytes 442376 | tf_op jit(solution)/shard_map/ppermute | solution.py:134
Sparse Core Ops, SparseCore 0:
  36.6 51.6 all-gather.1

commit v12 on v11

--- a/solution.py
+++ b/solution.py
@@ -46,7 +46,7 @@
             scratch_shapes=[pltpu.VMEM((n * depth, panel), left.dtype)],
         ),
         out_shape=jax.ShapeDtypeStruct((cores, wide // step, B, panel), jnp.float32),
-        compiler_params=pltpu.CompilerParams(vmem_limit_bytes=56 * 1024 * 1024),
+        compiler_params=pltpu.CompilerParams(vmem_limit_bytes=24 * 1024 * 1024),
         cost_estimate=pl.CostEstimate(
             flops=2 * n * depth * wide * panel,
             bytes_accessed=2 * n * depth * (wide + panel) + 4 * wide * panel,
@@ -132,7 +132,7 @@
         chunk = lax.dynamic_index_in_dim(partial, mine ^ d, 0, keepdims=False)
         chunk = jnp.concatenate([(chunk * grown).astype(jnp.float16), tail], axis=0)
         got = lax.ppermute(chunk, ("u", "v"), [(a, a ^ d) for a in range(nu * nv)])
-        total = total + got.astype(jnp.float32) * jnp.exp2(got[B, 0].astype(jnp.float32))
+        total = total + got.astype(jnp.float32) * jnp.exp2(got[B : B + 1].astype(jnp.float32))
     total = total[:B] + lax.dynamic_index_in_dim(partial, mine, 0, keepdims=False)
     return total.astype(jnp.bfloat16)
 

time: 145 us -> 140 us (0.966)
  Pallas kernels: 5.07 us -> 2.28 us
  waiting for transfers between devices: 42.9 us -> 45.3 us
  between operations: 16.4 us -> 14.3 us
    pallas_call x1, Pallas kernels: 5.07 us -> 2.28 us  [product(): pl.pallas_call(product_kernel, grid_spec=pltpu.PrefetchScalarGridSpec(num...]
    ppermute x3, waiting for transfers between devices: 9.44 us -> 11.8 us  [body(): got = lax.ppermute(chunk, ('u', 'v'), [(a, a ^ d) for a in range(nu * nv)])]
    slice x3 -> x0, local copies, waits for them, and re-layouts: 1.54 us -> none  [body(): got[B, 0].astype(jnp.float32)]
  transfers between devices with their start and end apart: 8 -> 8, of which waited for: 5 -> 5; matrix products, arithmetic and copies ran while one was open for 6% -> 5% of each run, Pallas kernels for 0% -> 0%
where the time goes in v12:
time: 140 us; the launch traced here: 139 us
  starting transfers between devices  58.6 us (42%)
  waiting for transfers between devices  45.3 us (32%)
  between operations  14.3 us (10%)
  other arithmetic  7.2 us (5%)
  local copies, waits for them, and re-layouts  6.06 us (4%)
  blocking collectives  5.54 us (4%)
  Pallas kernels  2.28 us (2%)
    all_to_all x1, waiting for transfers between devices, body(): right = lax.all_to_all(right, 'z', split_axis=0, concat_axis=0, tiled=True)  29.2 us
    all_to_all x1, starting transfers between devices, body(): right = lax.all_to_all(right, 'z', split_axis=0, concat_axis=0, tiled=True)  28.4 us
    all_to_all x1, starting transfers between devices, body(): lax.all_to_all(turned, ('u', 'v', 'core'), split_axis=0, concat_axis=0, t...  17.5 us
    ppermute x3, waiting for transfers between devices, body(): got = lax.ppermute(chunk, ('u', 'v'), [(a, a ^ d) for a in range(nu * nv)])  11.8 us
    ppermute x3, starting transfers between devices, body(): got = lax.ppermute(chunk, ('u', 'v'), [(a, a ^ d) for a in range(nu * nv)])  11.4 us
    all_to_all x1, blocking collectives, body(): lax.all_to_all(partial, 'core', split_axis=0, concat_axis=0, tiled=True)  5.54 us
    all_to_all x1, waiting for transfers between devices, body(): lax.all_to_all(turned, ('u', 'v', 'core'), split_axis=0, concat_axis=0, t...  4.21 us
    gt x4, other arithmetic, here(): return jnp.repeat(found, B, axis=1) > 0  3.28 us
  transfers between devices with their start and end apart: 8, of which 5 were waited for; matrix products, arithmetic and copies ran while one was open for 5% of the time, Pallas kernels for 0%

profile of v12, /device:TPU:1, one launch (start us, length us, event | category | flops | bytes accessed | tf_op | source)
XLA Modules:
  0.0 139.3 jit_solution(13483602973331360868)
XLA Ops:
  6.5 1.0 constant_dynamic-slice_fusion.1
  7.5 0.8 copy.14
  8.3 17.5 %all-to-all-start = ((bf16[8,128,128]{2,1,0:T(8,128)(2,1)}), bf16[8,128,128]{2,1,0:T(8,128)(2,1)S(1)}, u32[]{:S(2)}, u32[]{:S(2)}) async-start(bf16[8,128,128]{2,1,0:T(8,128)(2,1)} %bitcast.2), calls=%async_computation | async-start | bytes 524288 | tf_op jit(solution)/shard_map/all_to_all | solution.py:94
  25.8 0.0 all-gather.2.cloned.1.call-start
  25.8 1.1 copy.12
  27.0 0.7 collective-permute-start
  27.7 0.9 fusion.6
  28.6 0.8 compare_bitcast_fusion.1
  29.3 0.9 fusion.13
  30.2 0.8 compare_bitcast_fusion
  31.0 0.1 broadcast_bitcast_fusion
  31.0 0.1 broadcast_bitcast_fusion.2
  31.1 0.1 broadcast_bitcast_fusion.3
  31.2 0.1 broadcast_bitcast_fusion.1
  31.3 4.2 %all-to-all-done = bf16[8,128,128]{2,1,0:T(8,128)(2,1)S(1)} async-done(((bf16[8,128,128]{2,1,0:T(8,128)(2,1)}), bf16[8,128,128]{2,1,0:T(8,128)(2,1)S(1)}, u32[]{:S(2)}, u32[]{:S(2)}) %all-to-all-start) | async-done | bytes 262176 | tf_op jit(solution)/shard_map/all_to_all | solution.py:94
  35.5 0.0 collective-permute-done
  35.6 0.9 fusion
  36.5 0.0 all-gather.2.cloned.1.call-update
  36.6 0.7 collective-permute-start.1
  37.3 0.0 collective-permute-done.1
  37.3 1.0 fusion.2
  38.4 1.1 broadcast_in_dim.84
  39.5 28.4 %all-to-all-start.1 = ((bf16[8,128,512]{2,1,0:T(8,128)(2,1)}), bf16[8,128,512]{2,1,0:T(8,128)(2,1)S(1)}, u32[]{:S(2)}, u32[]{:S(2)}) async-start(bf16[8,128,512]{2,1,0:T(8,128)(2,1)} %broadcast_in_dim.84), calls=%async_computation.1 | async-start | bytes 2097152 | tf_op jit(solution)/shard_map/all_to_all | solution.py:120
  67.9 29.2 %all-to-all-done.1.right_ref = bf16[8,128,512]{2,1,0:T(8,128)(2,1)S(1)} async-done(((bf16[8,128,512]{2,1,0:T(8,128)(2,1)}), bf16[8,128,512]{2,1,0:T(8,128)(2,1)S(1)}, u32[]{:S(2)}, u32[]{:S(2)}) %all-to-all-start.1) | async-done | bytes 1048608 | tf_op jit(solution)/shard_map/all_to_all | solution.py:120
  97.1 0.0 all-gather.2.cloned.1.call-done
  97.1 0.0 copy-start
  97.1 1.6 %copy-done = bf16[64,128,128]{2,1,0:T(8,128)(2,1)S(1)} copy-done((bf16[64,128,128]{2,1,0:T(8,128)(2,1)S(1)}, bf16[64,128,128]{2,1,0:T(8,128)(2,1)}, u32[]{:S(2)}) %copy-start) | copy-done | bytes 2097176
  98.7 2.3 %product.1 = f32[2,4,128,512]{3,2,1,0:T(8,128)S(1)} custom-call(s32[1]{0:T(128)} %bitcast.z_ref, bf16[8,8,128,128]{3,2,1,0:T(8,128)(2,1)S(1)} %bitcast.53, bf16[8,128,512]{2,1,0:T(8,128)(2,1)S(1)} %all-to-all-done.1.right_ref), custom_call_target="tpu_custom_call" | custom-call | flops 1073741824 | bytes 5242880 | tf_op jit(solution)/shard_map/product/pallas_call | solution.py:36
  101.0 5.5 %all_to_all.15 = f32[2,4,128,512]{3,2,1,0:T(8,128)S(1)} all-to-all(f32[2,4,128,512]{3,2,1,0:T(8,128)S(1)} %product.1), channel_id=1, replica_groups=mesh['z'=8,'y'=8,'w'=2,'u'=2,'v'=2,'core'=2] {'core'}, dimensions={0} | all-to-all | bytes 4194304 | tf_op jit(solution)/shard_map/all_to_all | solution.py:123
  106.5 0.3 reduce_sum.9
  106.8 0.7 abs_reduce_fusion
  108.2 0.1 fusion.3
  108.4 4.2 %collective-permute-start.2 = (f16[144,512]{1,0:T(8,128)(2,1)S(1)}, f16[144,512]{1,0:T(8,128)(2,1)S(1)}, u32[]{:S(2)}, u32[]{:S(2)}) collective-permute-start(f16[144,512]{1,0:T(8,128)(2,1)S(1)} %concatenate.9), channel_id=1, source_target_pairs={{0,2},{2,0},{4,6},{6,4},{1,3},{3,1},{5,7},{7,5},{8,10},{10,8},{12,... | collective-permute-start | bytes 442376 | tf_op jit(solution)/shard_map/ppermute | solution.py:134
  112.6 5.2 %collective-permute-start.3 = (f16[144,512]{1,0:T(8,128)(2,1)S(1)}, f16[144,512]{1,0:T(8,128)(2,1)S(1)}, u32[]{:S(2)}, u32[]{:S(2)}) collective-permute-start(f16[144,512]{1,0:T(8,128)(2,1)S(1)} %concatenate.10), channel_id=1, source_target_pairs={{0,4},{2,6},{4,0},{6,2},{1,5},{3,7},{5,1},{7,3},{8,12},{10,14},{12... | collective-permute-start | bytes 442376 | tf_op jit(solution)/shard_map/ppermute | solution.py:134
  117.8 2.0 %collective-permute-start.4 = (f16[144,512]{1,0:T(8,128)(2,1)S(1)}, f16[144,512]{1,0:T(8,128)(2,1)S(1)}, u32[]{:S(2)}, u32[]{:S(2)}) collective-permute-start(f16[144,512]{1,0:T(8,128)(2,1)S(1)} %concatenate.11), channel_id=1, source_target_pairs={{0,6},{2,4},{4,2},{6,0},{1,7},{3,5},{5,3},{7,1},{8,14},{10,12},{12... | collective-permute-start | bytes 442376 | tf_op jit(solution)/shard_map/ppermute | solution.py:134
  119.9 0.2 collective-permute-done.2
  120.1 3.2 %collective-permute-done.3 = f16[144,512]{1,0:T(8,128)(2,1)S(1)} collective-permute-done((f16[144,512]{1,0:T(8,128)(2,1)S(1)}, f16[144,512]{1,0:T(8,128)(2,1)S(1)}, u32[]{:S(2)}, u32[]{:S(2)}) %collective-permute-start.3) | collective-permute-done | bytes 147488 | tf_op jit(solution)/shard_map/ppermute | solution.py:134
  123.3 8.4 %collective-permute-done.4 = f16[144,512]{1,0:T(8,128)(2,1)S(1)} collective-permute-done((f16[144,512]{1,0:T(8,128)(2,1)S(1)}, f16[144,512]{1,0:T(8,128)(2,1)S(1)}, u32[]{:S(2)}, u32[]{:S(2)}) %collective-permute-start.4) | collective-permute-done | bytes 147488 | tf_op jit(solution)/shard_map/ppermute | solution.py:134
  131.7 0.8 fusion.1
  (18 shorter events, 0.3 us)
Async XLA Ops:
  8.3 27.2 %all-to-all-start = ((bf16[8,128,128]{2,1,0:T(8,128)(2,1)}), bf16[8,128,128]{2,1,0:T(8,128)(2,1)S(1)}, u32[]{:S(2)}, u32[]{:S(2)}) async-start(bf16[8,128,128]{2,1,0:T(8,128)(2,1)} %bitcast.2), calls=%async_computation | async-start | bytes 524288 | tf_op jit(solution)/shard_map/all_to_all | solution.py:94
  25.8 71.3 %all-gather.2.cloned.1.call-start = ((), (), s32[]{:S(2)}) async-start(), calls=%async_computation.3 | async-start | bytes 2359296 | tf_op jit(solution)/shard_map/all_gather | solution.py:109
  27.0 8.6 %collective-permute-start = (bf16[8,128,128]{2,1,0:T(8,128)(2,1)S(1)}, bf16[8,128,128]{2,1,0:T(8,128)(2,1)S(1)}, u32[]{:S(2)}, u32[]{:S(2)}) collective-permute-start(bf16[8,128,128]{2,1,0:T(8,128)(2,1)S(1)} %bitcast.54), channel_id=1, source_target_pairs={{16,144},{17,145},{18,146},{19,147},{20,148},{21,149},{22,150},{23... | collective-permute-start | bytes 786440 | tf_op jit(solution)/shard_map/ppermute | solution.py:92
  36.6 0.8 collective-permute-start.1
  39.5 57.6 %all-to-all-start.1 = ((bf16[8,128,512]{2,1,0:T(8,128)(2,1)}), bf16[8,128,512]{2,1,0:T(8,128)(2,1)S(1)}, u32[]{:S(2)}, u32[]{:S(2)}) async-start(bf16[8,128,512]{2,1,0:T(8,128)(2,1)} %broadcast_in_dim.84), calls=%async_computation.1 | async-start | bytes 2097152 | tf_op jit(solution)/shard_map/all_to_all | solution.py:120
  97.1 1.6 %copy-start = (bf16[64,128,128]{2,1,0:T(8,128)(2,1)S(1)}, bf16[64,128,128]{2,1,0:T(8,128)(2,1)}, u32[]{:S(2)}) copy-start(bf16[64,128,128]{2,1,0:T(8,128)(2,1)} %all-gather.2.cloned.1.call-done) | copy-start | bytes 6291460
  108.4 11.7 %collective-permute-start.2 = (f16[144,512]{1,0:T(8,128)(2,1)S(1)}, f16[144,512]{1,0:T(8,128)(2,1)S(1)}, u32[]{:S(2)}, u32[]{:S(2)}) collective-permute-start(f16[144,512]{1,0:T(8,128)(2,1)S(1)} %concatenate.9), channel_id=1, source_target_pairs={{0,2},{2,0},{4,6},{6,4},{1,3},{3,1},{5,7},{7,5},{8,10},{10,8},{12,... | collective-permute-start | bytes 442376 | tf_op jit(solution)/shard_map/ppermute | solution.py:134
  112.6 10.7 %collective-permute-start.3 = (f16[144,512]{1,0:T(8,128)(2,1)S(1)}, f16[144,512]{1,0:T(8,128)(2,1)S(1)}, u32[]{:S(2)}, u32[]{:S(2)}) collective-permute-start(f16[144,512]{1,0:T(8,128)(2,1)S(1)} %concatenate.10), channel_id=1, source_target_pairs={{0,4},{2,6},{4,0},{6,2},{1,5},{3,7},{5,1},{7,3},{8,12},{10,14},{12... | collective-permute-start | bytes 442376 | tf_op jit(solution)/shard_map/ppermute | solution.py:134
  117.8 13.9 %collective-permute-start.4 = (f16[144,512]{1,0:T(8,128)(2,1)S(1)}, f16[144,512]{1,0:T(8,128)(2,1)S(1)}, u32[]{:S(2)}, u32[]{:S(2)}) collective-permute-start(f16[144,512]{1,0:T(8,128)(2,1)S(1)} %concatenate.11), channel_id=1, source_target_pairs={{0,6},{2,4},{4,2},{6,0},{1,7},{3,5},{5,3},{7,1},{8,14},{10,12},{12... | collective-permute-start | bytes 442376 | tf_op jit(solution)/shard_map/ppermute | solution.py:134
Sparse Core Ops, SparseCore 0:
  36.6 51.6 all-gather.1

commit v13 on v12

--- a/solution.py
+++ b/solution.py
@@ -46,7 +46,7 @@
             scratch_shapes=[pltpu.VMEM((n * depth, panel), left.dtype)],
         ),
         out_shape=jax.ShapeDtypeStruct((cores, wide // step, B, panel), jnp.float32),
-        compiler_params=pltpu.CompilerParams(vmem_limit_bytes=24 * 1024 * 1024),
+        compiler_params=pltpu.CompilerParams(vmem_limit_bytes=50 * 1024 * 1024),
         cost_estimate=pl.CostEstimate(
             flops=2 * n * depth * wide * panel,
             bytes_accessed=2 * n * depth * (wide + panel) + 4 * wide * panel,
@@ -128,7 +128,7 @@
     tail = jnp.broadcast_to(power.astype(jnp.float16), (TAIL, panel))
     mine = u * nv + v
     total = 0.0
-    for d in range(1, nu * nv):
+    for d in (2, 1, 3):
         chunk = lax.dynamic_index_in_dim(partial, mine ^ d, 0, keepdims=False)
         chunk = jnp.concatenate([(chunk * grown).astype(jnp.float16), tail], axis=0)
         got = lax.ppermute(chunk, ("u", "v"), [(a, a ^ d) for a in range(nu * nv)])

time: 140 us -> 138 us (0.986)
  waiting for transfers between devices: 45.3 us -> 43.1 us
  local copies, waits for them, and re-layouts: 6.06 us -> 4.46 us
  Pallas kernels: 2.28 us -> 3.74 us
    ppermute x3, waiting for transfers between devices: 11.8 us -> 9.63 us  [body(): got = lax.ppermute(chunk, ('u', 'v'), [(a, a ^ d) for a in range(nu * nv)])]
    unnamed x7 -> x5, local copies, waits for them, and re-layouts: 2.71 us -> 1.12 us
    pallas_call x1, Pallas kernels: 2.28 us -> 3.74 us  [product(): pl.pallas_call(product_kernel, grid_spec=pltpu.PrefetchScalarGridSpec(num...]
  transfers between devices with their start and end apart: 8 -> 8, of which waited for: 5 -> 3; matrix products, arithmetic and copies ran while one was open for 5% -> 5% of each run, Pallas kernels for 0% -> 0%
where the time goes in v13:
time: 138 us; the launch traced here: 137 us
  starting transfers between devices  58.6 us (42%)
  waiting for transfers between devices  43.1 us (31%)
  between operations  14.4 us (10%)
  other arithmetic  7.2 us (5%)
  blocking collectives  5.53 us (4%)
  local copies, waits for them, and re-layouts  4.46 us (3%)
  Pallas kernels  3.74 us (3%)
    all_to_all x1, waiting for transfers between devices, body(): right = lax.all_to_all(right, 'z', split_axis=0, concat_axis=0, tiled=True)  29.2 us
    all_to_all x1, starting transfers between devices, body(): right = lax.all_to_all(right, 'z', split_axis=0, concat_axis=0, tiled=True)  28.4 us
    all_to_all x1, starting transfers between devices, body(): lax.all_to_all(turned, ('u', 'v', 'core'), split_axis=0, concat_axis=0, t...  17.5 us
    ppermute x3, starting transfers between devices, body(): got = lax.ppermute(chunk, ('u', 'v'), [(a, a ^ d) for a in range(nu * nv)])  11.4 us
    ppermute x3, waiting for transfers between devices, body(): got = lax.ppermute(chunk, ('u', 'v'), [(a, a ^ d) for a in range(nu * nv)])  9.63 us
    all_to_all x1, blocking collectives, body(): lax.all_to_all(partial, 'core', split_axis=0, concat_axis=0, tiled=True)  5.53 us
    all_to_all x1, waiting for transfers between devices, body(): lax.all_to_all(turned, ('u', 'v', 'core'), split_axis=0, concat_axis=0, t...  4.21 us
    pallas_call x1, Pallas kernels, product(): pl.pallas_call(product_kernel, grid_spec=pltpu.PrefetchScalarGridSpec(num...  3.74 us
  transfers between devices with their start and end apart: 8, of which 3 were waited for; matrix products, arithmetic and copies ran while one was open for 5% of the time, Pallas kernels for 0%

profile of v13, /device:TPU:1, one launch (start us, length us, event | category | flops | bytes accessed | tf_op | source)
XLA Modules:
  0.0 137.0 jit_solution(6771749044795482533)
XLA Ops:
  6.5 1.0 constant_dynamic-slice_fusion.1
  7.5 0.8 copy.14
  8.3 17.5 %all-to-all-start = ((bf16[8,128,128]{2,1,0:T(8,128)(2,1)}), bf16[8,128,128]{2,1,0:T(8,128)(2,1)S(1)}, u32[]{:S(2)}, u32[]{:S(2)}) async-start(bf16[8,128,128]{2,1,0:T(8,128)(2,1)} %bitcast.2), calls=%async_computation | async-start | bytes 524288 | tf_op jit(solution)/shard_map/all_to_all | solution.py:94
  25.8 0.0 all-gather.2.cloned.1.call-start
  25.8 1.1 copy.12
  27.0 0.7 collective-permute-start
  27.7 0.9 fusion.6
  28.6 0.8 compare_bitcast_fusion.1
  29.3 0.9 fusion.13
  30.2 0.8 compare_bitcast_fusion
  31.0 0.1 broadcast_bitcast_fusion
  31.0 0.1 broadcast_bitcast_fusion.2
  31.1 0.1 broadcast_bitcast_fusion.3
  31.2 0.1 broadcast_bitcast_fusion.1
  31.3 4.2 %all-to-all-done = bf16[8,128,128]{2,1,0:T(8,128)(2,1)S(1)} async-done(((bf16[8,128,128]{2,1,0:T(8,128)(2,1)}), bf16[8,128,128]{2,1,0:T(8,128)(2,1)S(1)}, u32[]{:S(2)}, u32[]{:S(2)}) %all-to-all-start) | async-done | bytes 262176 | tf_op jit(solution)/shard_map/all_to_all | solution.py:94
  35.5 0.0 collective-permute-done
  35.6 0.9 fusion
  36.5 0.0 all-gather.2.cloned.1.call-update
  36.6 0.7 collective-permute-start.1
  37.3 0.0 collective-permute-done.1
  37.3 1.0 fusion.2
  38.4 1.1 broadcast_in_dim.84
  39.5 28.4 %all-to-all-start.1 = ((bf16[8,128,512]{2,1,0:T(8,128)(2,1)}), bf16[8,128,512]{2,1,0:T(8,128)(2,1)S(1)}, u32[]{:S(2)}, u32[]{:S(2)}) async-start(bf16[8,128,512]{2,1,0:T(8,128)(2,1)} %broadcast_in_dim.84), calls=%async_computation.1 | async-start | bytes 2097152 | tf_op jit(solution)/shard_map/all_to_all | solution.py:120
  67.9 29.2 %all-to-all-done.1.right_ref = bf16[8,128,512]{2,1,0:T(8,128)(2,1)S(1)} async-done(((bf16[8,128,512]{2,1,0:T(8,128)(2,1)}), bf16[8,128,512]{2,1,0:T(8,128)(2,1)S(1)}, u32[]{:S(2)}, u32[]{:S(2)}) %all-to-all-start.1) | async-done | bytes 1048608 | tf_op jit(solution)/shard_map/all_to_all | solution.py:120
  97.1 0.0 all-gather.2.cloned.1.call-done
  97.1 3.7 %product.1 = f32[2,4,128,512]{3,2,1,0:T(8,128)S(1)} custom-call(s32[1]{0:T(128)} %bitcast.z_ref, bf16[8,8,128,128]{3,2,1,0:T(8,128)(2,1)} %bitcast.53, bf16[8,128,512]{2,1,0:T(8,128)(2,1)S(1)} %all-to-all-done.1.right_ref), custom_call_target="tpu_custom_call" | custom-call | flops 1073741824 | bytes 5242880 | tf_op jit(solution)/shard_map/product/pallas_call | solution.py:36
  100.9 5.5 %all_to_all.15 = f32[2,4,128,512]{3,2,1,0:T(8,128)S(1)} all-to-all(f32[2,4,128,512]{3,2,1,0:T(8,128)S(1)} %product.1), channel_id=1, replica_groups=mesh['z'=8,'y'=8,'w'=2,'u'=2,'v'=2,'core'=2] {'core'}, dimensions={0} | all-to-all | bytes 4194304 | tf_op jit(solution)/shard_map/all_to_all | solution.py:123
  106.4 0.3 reduce_sum.9
  106.7 0.7 abs_reduce_fusion
  108.1 0.1 fusion.3
  108.2 7.2 %collective-permute-start.2 = (f16[144,512]{1,0:T(8,128)(2,1)S(1)}, f16[144,512]{1,0:T(8,128)(2,1)S(1)}, u32[]{:S(2)}, u32[]{:S(2)}) collective-permute-start(f16[144,512]{1,0:T(8,128)(2,1)S(1)} %concatenate.9), channel_id=1, source_target_pairs={{0,4},{2,6},{4,0},{6,2},{1,5},{3,7},{5,1},{7,3},{8,12},{10,14},{12... | collective-permute-start | bytes 442376 | tf_op jit(solution)/shard_map/ppermute | solution.py:134
  115.4 2.2 %collective-permute-start.3 = (f16[144,512]{1,0:T(8,128)(2,1)S(1)}, f16[144,512]{1,0:T(8,128)(2,1)S(1)}, u32[]{:S(2)}, u32[]{:S(2)}) collective-permute-start(f16[144,512]{1,0:T(8,128)(2,1)S(1)} %concatenate.10), channel_id=1, source_target_pairs={{0,2},{2,0},{4,6},{6,4},{1,3},{3,1},{5,7},{7,5},{8,10},{10,8},{12,... | collective-permute-start | bytes 442376 | tf_op jit(solution)/shard_map/ppermute | solution.py:134
  117.7 2.0 %collective-permute-start.4 = (f16[144,512]{1,0:T(8,128)(2,1)S(1)}, f16[144,512]{1,0:T(8,128)(2,1)S(1)}, u32[]{:S(2)}, u32[]{:S(2)}) collective-permute-start(f16[144,512]{1,0:T(8,128)(2,1)S(1)} %concatenate.11), channel_id=1, source_target_pairs={{0,6},{2,4},{4,2},{6,0},{1,7},{3,5},{5,3},{7,1},{8,14},{10,12},{12... | collective-permute-start | bytes 442376 | tf_op jit(solution)/shard_map/ppermute | solution.py:134
  119.7 0.0 collective-permute-done.2
  119.7 9.6 %collective-permute-done.3 = f16[144,512]{1,0:T(8,128)(2,1)S(1)} collective-permute-done((f16[144,512]{1,0:T(8,128)(2,1)S(1)}, f16[144,512]{1,0:T(8,128)(2,1)S(1)}, u32[]{:S(2)}, u32[]{:S(2)}) %collective-permute-start.3) | collective-permute-done | bytes 147488 | tf_op jit(solution)/shard_map/ppermute | solution.py:134
  129.4 0.0 collective-permute-done.4
  129.4 0.8 fusion.1
  (18 shorter events, 0.3 us)
Async XLA Ops:
  8.3 27.2 %all-to-all-start = ((bf16[8,128,128]{2,1,0:T(8,128)(2,1)}), bf16[8,128,128]{2,1,0:T(8,128)(2,1)S(1)}, u32[]{:S(2)}, u32[]{:S(2)}) async-start(bf16[8,128,128]{2,1,0:T(8,128)(2,1)} %bitcast.2), calls=%async_computation | async-start | bytes 524288 | tf_op jit(solution)/shard_map/all_to_all | solution.py:94
  25.8 71.3 %all-gather.2.cloned.1.call-start = ((), (), s32[]{:S(2)}) async-start(), calls=%async_computation.3 | async-start | bytes 2359296 | tf_op jit(solution)/shard_map/all_gather | solution.py:109
  27.0 8.6 %collective-permute-start = (bf16[8,128,128]{2,1,0:T(8,128)(2,1)S(1)}, bf16[8,128,128]{2,1,0:T(8,128)(2,1)S(1)}, u32[]{:S(2)}, u32[]{:S(2)}) collective-permute-start(bf16[8,128,128]{2,1,0:T(8,128)(2,1)S(1)} %bitcast.54), channel_id=1, source_target_pairs={{16,144},{17,145},{18,146},{19,147},{20,148},{21,149},{22,150},{23... | collective-permute-start | bytes 786440 | tf_op jit(solution)/shard_map/ppermute | solution.py:92
  36.6 0.8 collective-permute-start.1
  39.5 57.6 %all-to-all-start.1 = ((bf16[8,128,512]{2,1,0:T(8,128)(2,1)}), bf16[8,128,512]{2,1,0:T(8,128)(2,1)S(1)}, u32[]{:S(2)}, u32[]{:S(2)}) async-start(bf16[8,128,512]{2,1,0:T(8,128)(2,1)} %broadcast_in_dim.84), calls=%async_computation.1 | async-start | bytes 2097152 | tf_op jit(solution)/shard_map/all_to_all | solution.py:120
  108.2 11.5 %collective-permute-start.2 = (f16[144,512]{1,0:T(8,128)(2,1)S(1)}, f16[144,512]{1,0:T(8,128)(2,1)S(1)}, u32[]{:S(2)}, u32[]{:S(2)}) collective-permute-start(f16[144,512]{1,0:T(8,128)(2,1)S(1)} %concatenate.9), channel_id=1, source_target_pairs={{0,4},{2,6},{4,0},{6,2},{1,5},{3,7},{5,1},{7,3},{8,12},{10,14},{12... | collective-permute-start | bytes 442376 | tf_op jit(solution)/shard_map/ppermute | solution.py:134
  115.4 13.9 %collective-permute-start.3 = (f16[144,512]{1,0:T(8,128)(2,1)S(1)}, f16[144,512]{1,0:T(8,128)(2,1)S(1)}, u32[]{:S(2)}, u32[]{:S(2)}) collective-permute-start(f16[144,512]{1,0:T(8,128)(2,1)S(1)} %concatenate.10), channel_id=1, source_target_pairs={{0,2},{2,0},{4,6},{6,4},{1,3},{3,1},{5,7},{7,5},{8,10},{10,8},{12,... | collective-permute-start | bytes 442376 | tf_op jit(solution)/shard_map/ppermute | solution.py:134
  117.7 11.7 %collective-permute-start.4 = (f16[144,512]{1,0:T(8,128)(2,1)S(1)}, f16[144,512]{1,0:T(8,128)(2,1)S(1)}, u32[]{:S(2)}, u32[]{:S(2)}) collective-permute-start(f16[144,512]{1,0:T(8,128)(2,1)S(1)} %concatenate.11), channel_id=1, source_target_pairs={{0,6},{2,4},{4,2},{6,0},{1,7},{3,5},{5,3},{7,1},{8,14},{10,12},{12... | collective-permute-start | bytes 442376 | tf_op jit(solution)/shard_map/ppermute | solution.py:134
Sparse Core Ops, SparseCore 0:
  36.6 51.6 all-gather.1

commit v14 on v13

--- a/solution.py
+++ b/solution.py
@@ -11,49 +11,47 @@
 TAIL = 16
 
 
-def product_kernel(z_ref, left_ref, right_ref, out_ref, ordered):
+def product_kernel(at_ref, left_ref, right_ref, out_ref, ordered):
     n, depth, _ = right_ref.shape
-    z = z_ref[0]
+    z = at_ref[0]
 
     @pl.when(pl.program_id(0) == 0)
     def _():
         for p in range(n):
             ordered[p * depth : (p + 1) * depth, :] = right_ref[lax.rem(p - z + n, n)]
 
-    for a in range(out_ref.shape[0]):
-        out_ref[a, 0] = lax.dot_general(
-            left_ref[:, a].reshape(n * depth, B),
-            ordered[...],
-            (((0,), (0,)), ((), ())),
-            preferred_element_type=jnp.float32,
-        )
+    out_ref[0] = lax.dot_general(
+        left_ref[:, 0].reshape(n * depth, B),
+        ordered[...],
+        (((0,), (0,)), ((), ())),
+        preferred_element_type=jnp.float32,
+    )
 
 
-def product(left, right, z, cores):
+def product(left, right, z, core, cores):
     n, depth, panel = right.shape
-    wide = left.shape[1] * B
-    step = cores * B
+    count = left.shape[1] // cores
     return pl.pallas_call(
         product_kernel,
         grid_spec=pltpu.PrefetchScalarGridSpec(
             num_scalar_prefetch=1,
-            grid=(wide // step,),
+            grid=(count,),
             in_specs=[
-                pl.BlockSpec((n, cores, depth, B), lambda m, _: (0, m, 0, 0)),
+                pl.BlockSpec((n, 1, depth, B), lambda m, at: (0, m * cores + at[1], 0, 0)),
                 pl.BlockSpec((n, depth, panel), lambda m, _: (0, 0, 0)),
             ],
-            out_specs=pl.BlockSpec((cores, 1, B, panel), lambda m, _: (0, m, 0, 0)),
+            out_specs=pl.BlockSpec((1, B, panel), lambda m, _: (m, 0, 0)),
             scratch_shapes=[pltpu.VMEM((n * depth, panel), left.dtype)],
         ),
-        out_shape=jax.ShapeDtypeStruct((cores, wide // step, B, panel), jnp.float32),
+        out_shape=jax.ShapeDtypeStruct((count, B, panel), jnp.float32),
         compiler_params=pltpu.CompilerParams(vmem_limit_bytes=50 * 1024 * 1024),
         cost_estimate=pl.CostEstimate(
-            flops=2 * n * depth * wide * panel,
-            bytes_accessed=2 * n * depth * (wide + panel) + 4 * wide * panel,
+            flops=2 * n * depth * count * B * panel,
+            bytes_accessed=2 * n * depth * (count * B + panel) + 4 * count * B * panel,
             transcendentals=0,
         ),
         name="product",
-    )(z.reshape(1), left, right)
+    )(jnp.stack([z, core]), left, right)
 
 
 def body(stored, pattern):
@@ -119,8 +117,9 @@
     right = jnp.broadcast_to(right[None], (nz, B, panel))
     right = lax.all_to_all(right, "z", split_axis=0, concat_axis=0, tiled=True)
 
-    partial = product(left, right, z, ncore)
-    partial = jnp.sum(lax.all_to_all(partial, "core", split_axis=0, concat_axis=0, tiled=True), axis=0)
+    partial = product(left, right, z, ncore - 1 - core, ncore)
+    partial = lax.ppermute(partial, "core", [(a, ncore - 1 - a) for a in range(ncore)])
+    partial = partial + product(left, right, z, core, ncore)
 
     most = jnp.max(jnp.abs(partial))
     power = jnp.clip(jnp.ceil(jnp.log2(jnp.maximum(most, 1e-30))) - 14.0, -100.0, 100.0)

time: 138 us -> 138 us (level)
  blocking collectives: 5.53 us -> 0 us
  Pallas kernels: 3.74 us -> 7.14 us
  starting transfers between devices: 58.6 us -> 61 us
    all_to_all x1 -> x0, blocking collectives: 5.53 us -> none  [body(): lax.all_to_all(partial, 'core', split_axis=0, concat_axis=0, tiled=True)]
    pallas_call x1 -> x2, Pallas kernels: 3.74 us -> 7.14 us  [product(): pl.pallas_call(product_kernel, grid_spec=pltpu.PrefetchScalarGridSpec(num...]
    ppermute x0 -> x1, starting transfers between devices: none -> 2.4 us  [body(): lax.ppermute(partial, 'core', [(a, ncore - 1 - a) for a in range(ncore)])]
  transfers between devices with their start and end apart: 8 -> 9, of which waited for: 3 -> 4; matrix products, arithmetic and copies ran while one was open for 5% -> 5% of each run, Pallas kernels for 0% -> 3%
where the time goes in v14:
time: 138 us; the launch traced here: 137 us
  starting transfers between devices  61 us (44%)
  waiting for transfers between devices  43.3 us (31%)
  between operations  14.4 us (10%)
  other arithmetic  7.21 us (5%)
  Pallas kernels  7.14 us (5%)
  local copies, waits for them, and re-layouts  4.46 us (3%)
    all_to_all x1, waiting for transfers between devices, body(): right = lax.all_to_all(right, 'z', split_axis=0, concat_axis=0, tiled=True)  29.2 us
    all_to_all x1, starting transfers between devices, body(): right = lax.all_to_all(right, 'z', split_axis=0, concat_axis=0, tiled=True)  28.4 us
    all_to_all x1, starting transfers between devices, body(): lax.all_to_all(turned, ('u', 'v', 'core'), split_axis=0, concat_axis=0, t...  17.5 us
    ppermute x3, starting transfers between devices, body(): got = lax.ppermute(chunk, ('u', 'v'), [(a, a ^ d) for a in range(nu * nv)])  11.4 us
    ppermute x3, waiting for transfers between devices, body(): got = lax.ppermute(chunk, ('u', 'v'), [(a, a ^ d) for a in range(nu * nv)])  9.9 us
    pallas_call x2, Pallas kernels, product(): pl.pallas_call(product_kernel, grid_spec=pltpu.PrefetchScalarGridSpec(num...  7.14 us
    all_to_all x1, waiting for transfers between devices, body(): lax.all_to_all(turned, ('u', 'v', 'core'), split_axis=0, concat_axis=0, t...  4.2 us
    gt x4, other arithmetic, here(): return jnp.repeat(found, B, axis=1) > 0  3.28 us
  transfers between devices with their start and end apart: 9, of which 4 were waited for; matrix products, arithmetic and copies ran while one was open for 5% of the time, Pallas kernels for 3%

profile of v14, /device:TPU:1, one launch (start us, length us, event | category | flops | bytes accessed | tf_op | source)
XLA Modules:
  0.0 137.5 jit_solution(2233456735241146851)
XLA Ops:
  6.5 1.0 constant_dynamic-slice_fusion.1
  7.5 0.8 copy.14
  8.3 17.5 %all-to-all-start = ((bf16[8,128,128]{2,1,0:T(8,128)(2,1)}), bf16[8,128,128]{2,1,0:T(8,128)(2,1)S(1)}, u32[]{:S(2)}, u32[]{:S(2)}) async-start(bf16[8,128,128]{2,1,0:T(8,128)(2,1)} %bitcast.3), calls=%async_computation | async-start | bytes 524288 | tf_op jit(solution)/shard_map/all_to_all | solution.py:92
  25.8 0.0 all-gather.2.cloned.1.call-start
  25.8 1.1 copy.12
  27.0 0.7 collective-permute-start
  27.7 0.9 fusion.6
  28.6 0.8 compare_bitcast_fusion.1
  29.3 0.9 fusion.13
  30.2 0.8 compare_bitcast_fusion
  31.0 0.1 broadcast_bitcast_fusion
  31.0 0.1 broadcast_bitcast_fusion.2
  31.1 0.1 broadcast_bitcast_fusion.3
  31.2 0.1 broadcast_bitcast_fusion.1
  31.3 4.2 %all-to-all-done = bf16[8,128,128]{2,1,0:T(8,128)(2,1)S(1)} async-done(((bf16[8,128,128]{2,1,0:T(8,128)(2,1)}), bf16[8,128,128]{2,1,0:T(8,128)(2,1)S(1)}, u32[]{:S(2)}, u32[]{:S(2)}) %all-to-all-start) | async-done | bytes 262176 | tf_op jit(solution)/shard_map/all_to_all | solution.py:92
  35.5 0.0 collective-permute-done
  35.6 0.9 fusion
  36.5 0.0 all-gather.2.cloned.1.call-update
  36.6 0.7 collective-permute-start.1
  37.3 0.0 collective-permute-done.1
  37.3 1.0 fusion.2
  38.4 1.1 broadcast_in_dim.84
  39.5 28.4 %all-to-all-start.1 = ((bf16[8,128,512]{2,1,0:T(8,128)(2,1)}), bf16[8,128,512]{2,1,0:T(8,128)(2,1)S(1)}, u32[]{:S(2)}, u32[]{:S(2)}) async-start(bf16[8,128,512]{2,1,0:T(8,128)(2,1)} %broadcast_in_dim.84), calls=%async_computation.1 | async-start | bytes 2097152 | tf_op jit(solution)/shard_map/all_to_all | solution.py:118
  67.9 0.1 pad_add_fusion.at_ref
  67.9 29.2 %all-to-all-done.1.right_ref = bf16[8,128,512]{2,1,0:T(8,128)(2,1)S(1)} async-done(((bf16[8,128,512]{2,1,0:T(8,128)(2,1)}), bf16[8,128,512]{2,1,0:T(8,128)(2,1)S(1)}, u32[]{:S(2)}, u32[]{:S(2)}) %all-to-all-start.1) | async-done | bytes 1048608 | tf_op jit(solution)/shard_map/all_to_all | solution.py:118
  97.1 0.0 all-gather.2.cloned.1.call-done
  97.1 3.6 %product.2 = f32[4,128,512]{2,1,0:T(8,128)S(1)} custom-call(s32[2]{0:T(128)S(1)} %pad_add_fusion.at_ref, bf16[8,8,128,128]{3,2,1,0:T(8,128)(2,1)} %bitcast.55, bf16[8,128,512]{2,1,0:T(8,128)(2,1)S(1)} %all-to-all-done.1.right_ref), custom_call_target="tpu_custom_call" | custom-call | flops 536870912 | bytes 3145728 | tf_op jit(solution)/shard_map/product/pallas_call | solution.py:34
  100.7 2.4 %collective-permute-start.2 = (f32[4,128,512]{2,1,0:T(8,128)S(1)}, f32[4,128,512]{2,1,0:T(8,128)S(1)}, u32[]{:S(2)}, u32[]{:S(2)}) collective-permute-start(f32[4,128,512]{2,1,0:T(8,128)S(1)} %product.2), channel_id=1, source_target_pairs={{0,1},{1,0},{2,3},{3,2},{4,5},{5,4},{6,7},{7,6},{8,9},{9,8},{10,11... | collective-permute-start | bytes 3145736 | tf_op jit(solution)/shard_map/ppermute | solution.py:121
  103.1 0.1 pad_add_fusion.1.at_ref
  103.2 3.6 %product.3 = f32[4,128,512]{2,1,0:T(8,128)S(1)} custom-call(s32[2]{0:T(128)S(1)} %pad_add_fusion.1.at_ref, bf16[8,8,128,128]{3,2,1,0:T(8,128)(2,1)} %bitcast.56, bf16[8,128,512]{2,1,0:T(8,128)(2,1)S(1)} %all-to-all-done.1.right_ref), custom_call_target="tpu_custom_call" | custom-call | flops 536870912 | bytes 3145728 | tf_op jit(solution)/shard_map/product/pallas_call | solution.py:34
  106.8 0.0 collective-permute-done.2
  106.8 0.8 abs_reduce_fusion
  108.3 0.1 fusion.3
  108.5 7.2 %collective-permute-start.3 = (f16[144,512]{1,0:T(8,128)(2,1)S(1)}, f16[144,512]{1,0:T(8,128)(2,1)S(1)}, u32[]{:S(2)}, u32[]{:S(2)}) collective-permute-start(f16[144,512]{1,0:T(8,128)(2,1)S(1)} %concatenate.9), channel_id=1, source_target_pairs={{0,4},{2,6},{4,0},{6,2},{1,5},{3,7},{5,1},{7,3},{8,12},{10,14},{12... | collective-permute-start | bytes 442376 | tf_op jit(solution)/shard_map/ppermute | solution.py:133
  115.7 2.2 %collective-permute-start.4 = (f16[144,512]{1,0:T(8,128)(2,1)S(1)}, f16[144,512]{1,0:T(8,128)(2,1)S(1)}, u32[]{:S(2)}, u32[]{:S(2)}) collective-permute-start(f16[144,512]{1,0:T(8,128)(2,1)S(1)} %concatenate.10), channel_id=1, source_target_pairs={{0,2},{2,0},{4,6},{6,4},{1,3},{3,1},{5,7},{7,5},{8,10},{10,8},{12,... | collective-permute-start | bytes 442376 | tf_op jit(solution)/shard_map/ppermute | solution.py:133
  117.9 2.0 %collective-permute-start.5 = (f16[144,512]{1,0:T(8,128)(2,1)S(1)}, f16[144,512]{1,0:T(8,128)(2,1)S(1)}, u32[]{:S(2)}, u32[]{:S(2)}) collective-permute-start(f16[144,512]{1,0:T(8,128)(2,1)S(1)} %concatenate.11), channel_id=1, source_target_pairs={{0,6},{2,4},{4,2},{6,0},{1,7},{3,5},{5,3},{7,1},{8,14},{10,12},{12... | collective-permute-start | bytes 442376 | tf_op jit(solution)/shard_map/ppermute | solution.py:133
  119.9 0.0 collective-permute-done.3
  120.0 9.7 %collective-permute-done.4 = f16[144,512]{1,0:T(8,128)(2,1)S(1)} collective-permute-done((f16[144,512]{1,0:T(8,128)(2,1)S(1)}, f16[144,512]{1,0:T(8,128)(2,1)S(1)}, u32[]{:S(2)}, u32[]{:S(2)}) %collective-permute-start.4) | collective-permute-done | bytes 147488 | tf_op jit(solution)/shard_map/ppermute | solution.py:133
  129.6 0.2 collective-permute-done.5
  129.9 0.8 fusion.1
  (18 shorter events, 0.3 us)
Async XLA Ops:
  8.3 27.2 %all-to-all-start = ((bf16[8,128,128]{2,1,0:T(8,128)(2,1)}), bf16[8,128,128]{2,1,0:T(8,128)(2,1)S(1)}, u32[]{:S(2)}, u32[]{:S(2)}) async-start(bf16[8,128,128]{2,1,0:T(8,128)(2,1)} %bitcast.3), calls=%async_computation | async-start | bytes 524288 | tf_op jit(solution)/shard_map/all_to_all | solution.py:92
  25.8 71.3 %all-gather.2.cloned.1.call-start = ((), (), s32[]{:S(2)}) async-start(), calls=%async_computation.2 | async-start | bytes 2359296 | tf_op jit(solution)/shard_map/all_gather | solution.py:107
  27.0 8.6 %collective-permute-start = (bf16[8,128,128]{2,1,0:T(8,128)(2,1)S(1)}, bf16[8,128,128]{2,1,0:T(8,128)(2,1)S(1)}, u32[]{:S(2)}, u32[]{:S(2)}) collective-permute-start(bf16[8,128,128]{2,1,0:T(8,128)(2,1)S(1)} %bitcast.57), channel_id=1, source_target_pairs={{16,144},{17,145},{18,146},{19,147},{20,148},{21,149},{22,150},{23... | collective-permute-start | bytes 786440 | tf_op jit(solution)/shard_map/ppermute | solution.py:90
  36.6 0.8 collective-permute-start.1
  39.5 57.6 %all-to-all-start.1 = ((bf16[8,128,512]{2,1,0:T(8,128)(2,1)}), bf16[8,128,512]{2,1,0:T(8,128)(2,1)S(1)}, u32[]{:S(2)}, u32[]{:S(2)}) async-start(bf16[8,128,512]{2,1,0:T(8,128)(2,1)} %broadcast_in_dim.84), calls=%async_computation.1 | async-start | bytes 2097152 | tf_op jit(solution)/shard_map/all_to_all | solution.py:118
  100.7 6.1 %collective-permute-start.2 = (f32[4,128,512]{2,1,0:T(8,128)S(1)}, f32[4,128,512]{2,1,0:T(8,128)S(1)}, u32[]{:S(2)}, u32[]{:S(2)}) collective-permute-start(f32[4,128,512]{2,1,0:T(8,128)S(1)} %product.2), channel_id=1, source_target_pairs={{0,1},{1,0},{2,3},{3,2},{4,5},{5,4},{6,7},{7,6},{8,9},{9,8},{10,11... | collective-permute-start | bytes 3145736 | tf_op jit(solution)/shard_map/ppermute | solution.py:121
  108.5 11.5 %collective-permute-start.3 = (f16[144,512]{1,0:T(8,128)(2,1)S(1)}, f16[144,512]{1,0:T(8,128)(2,1)S(1)}, u32[]{:S(2)}, u32[]{:S(2)}) collective-permute-start(f16[144,512]{1,0:T(8,128)(2,1)S(1)} %concatenate.9), channel_id=1, source_target_pairs={{0,4},{2,6},{4,0},{6,2},{1,5},{3,7},{5,1},{7,3},{8,12},{10,14},{12... | collective-permute-start | bytes 442376 | tf_op jit(solution)/shard_map/ppermute | solution.py:133
  115.7 13.9 %collective-permute-start.4 = (f16[144,512]{1,0:T(8,128)(2,1)S(1)}, f16[144,512]{1,0:T(8,128)(2,1)S(1)}, u32[]{:S(2)}, u32[]{:S(2)}) collective-permute-start(f16[144,512]{1,0:T(8,128)(2,1)S(1)} %concatenate.10), channel_id=1, source_target_pairs={{0,2},{2,0},{4,6},{6,4},{1,3},{3,1},{5,7},{7,5},{8,10},{10,8},{12,... | collective-permute-start | bytes 442376 | tf_op jit(solution)/shard_map/ppermute | solution.py:133
  117.9 12.0 %collective-permute-start.5 = (f16[144,512]{1,0:T(8,128)(2,1)S(1)}, f16[144,512]{1,0:T(8,128)(2,1)S(1)}, u32[]{:S(2)}, u32[]{:S(2)}) collective-permute-start(f16[144,512]{1,0:T(8,128)(2,1)S(1)} %concatenate.11), channel_id=1, source_target_pairs={{0,6},{2,4},{4,2},{6,0},{1,7},{3,5},{5,3},{7,1},{8,14},{10,12},{12... | collective-permute-start | bytes 442376 | tf_op jit(solution)/shard_map/ppermute | solution.py:133
Sparse Core Ops, SparseCore 0:
  36.6 51.6 all-gather.1

commit v15 on v13

--- a/solution.py
+++ b/solution.py
@@ -89,8 +89,9 @@
 
     k = lax.rem(y - z + nz, nz)
     band = columns(k * plane, plane).reshape(B, nl, B).transpose(1, 0, 2)
+    band = lax.optimization_barrier(band)
     straight = lax.ppermute(band, AXES, pairs(lambda a, b, c: (c, b), 1))
-    turned = columns(k * plane, plane).T.reshape(nl, B, B)
+    turned = band.transpose(0, 2, 1)
     crossed = lax.all_to_all(turned, ("u", "v", "core"), split_axis=0, concat_axis=0, tiled=True)
     first = y * nl + w * (nl // nw)
     present = (

time: 138 us -> 139 us (level)
  starting transfers between devices: 58.6 us -> 60.1 us
    ppermute x3, waiting for transfers between devices: 9.63 us -> 7.59 us  [body(): got = lax.ppermute(chunk, ('u', 'v'), [(a, a ^ d) for a in range(nu * nv)])]
    all_to_all x1, waiting for transfers between devices: 4.21 us -> 6.08 us  [body(): lax.all_to_all(turned, ('u', 'v', 'core'), split_axis=0, concat_axis=0, t...]
    all_to_all x1, starting transfers between devices: 28.4 us -> 29.9 us  [body(): right = lax.all_to_all(right, 'z', split_axis=0, concat_axis=0, tiled=True)]
  transfers between devices with their start and end apart: 8 -> 8, of which waited for: 3 -> 4; matrix products, arithmetic and copies ran while one was open for 5% -> 5% of each run, Pallas kernels for 0% -> 0%
where the time goes in v15:
time: 139 us; the launch traced here: 138 us
  starting transfers between devices  60.1 us (43%)
  waiting for transfers between devices  42.9 us (31%)
  between operations  14.3 us (10%)
  other arithmetic  6.86 us (5%)
  blocking collectives  5.54 us (4%)
  local copies, waits for them, and re-layouts  4.44 us (3%)
  Pallas kernels  3.73 us (3%)
    all_to_all x1, starting transfers between devices, body(): right = lax.all_to_all(right, 'z', split_axis=0, concat_axis=0, tiled=True)  29.9 us
    all_to_all x1, waiting for transfers between devices, body(): right = lax.all_to_all(right, 'z', split_axis=0, concat_axis=0, tiled=True)  29.2 us
    all_to_all x1, starting transfers between devices, body(): lax.all_to_all(turned, ('u', 'v', 'core'), split_axis=0, concat_axis=0, t...  17.5 us
    ppermute x3, starting transfers between devices, body(): got = lax.ppermute(chunk, ('u', 'v'), [(a, a ^ d) for a in range(nu * nv)])  11.4 us
    ppermute x3, waiting for transfers between devices, body(): got = lax.ppermute(chunk, ('u', 'v'), [(a, a ^ d) for a in range(nu * nv)])  7.59 us
    all_to_all x1, waiting for transfers between devices, body(): lax.all_to_all(turned, ('u', 'v', 'core'), split_axis=0, concat_axis=0, t...  6.08 us
    all_to_all x1, blocking collectives, body(): lax.all_to_all(partial, 'core', split_axis=0, concat_axis=0, tiled=True)  5.54 us
    pallas_call x1, Pallas kernels, product(): pl.pallas_call(product_kernel, grid_spec=pltpu.PrefetchScalarGridSpec(num...  3.73 us
  transfers between devices with their start and end apart: 8, of which 4 were waited for; matrix products, arithmetic and copies ran while one was open for 5% of the time, Pallas kernels for 0%

profile of v15, /device:TPU:1, one launch (start us, length us, event | category | flops | bytes accessed | tf_op | source)
XLA Modules:
  0.0 137.9 jit_solution(3839470285408311268)
XLA Ops:
  6.5 1.0 constant_dynamic-slice_fusion.1
  7.5 0.2 copy.14
  7.7 0.7 collective-permute-start
  8.4 0.8 copy.10
  9.2 17.5 %all-to-all-start = ((bf16[8,128,128]{1,2,0:T(8,128)(2,1)}), bf16[8,128,128]{1,2,0:T(8,128)(2,1)S(1)}, u32[]{:S(2)}, u32[]{:S(2)}) async-start(bf16[8,128,128]{1,2,0:T(8,128)(2,1)} %bitcast.3), calls=%async_computation | async-start | bytes 524288 | tf_op jit(solution)/shard_map/all_to_all | solution.py:95
  26.7 0.0 all-gather.2.cloned.1.call-start
  26.7 0.9 fusion.6
  27.5 0.8 compare_bitcast_fusion.1
  28.3 0.9 fusion.13
  29.2 0.8 compare_bitcast_fusion
  30.0 0.1 broadcast_bitcast_fusion
  30.0 0.1 broadcast_bitcast_fusion.2
  30.1 0.1 broadcast_bitcast_fusion.3
  30.2 0.1 broadcast_bitcast_fusion.1
  30.3 6.1 %all-to-all-done = bf16[8,128,128]{1,2,0:T(8,128)(2,1)S(1)} async-done(((bf16[8,128,128]{1,2,0:T(8,128)(2,1)}), bf16[8,128,128]{1,2,0:T(8,128)(2,1)S(1)}, u32[]{:S(2)}, u32[]{:S(2)}) %all-to-all-start) | async-done | bytes 262176 | tf_op jit(solution)/shard_map/all_to_all | solution.py:95
  36.4 0.0 collective-permute-done
  36.4 0.6 fusion
  37.0 0.9 copy.11
  37.9 0.0 all-gather.2.cloned.1.call-update
  37.9 0.1 copy.15
  38.1 0.7 collective-permute-start.1
  38.8 0.0 collective-permute-done.1
  38.8 1.0 fusion.2
  39.9 1.1 broadcast_in_dim.84
  41.0 29.9 %all-to-all-start.1 = ((bf16[8,128,512]{2,1,0:T(8,128)(2,1)}), bf16[8,128,512]{2,1,0:T(8,128)(2,1)S(1)}, u32[]{:S(2)}, u32[]{:S(2)}) async-start(bf16[8,128,512]{2,1,0:T(8,128)(2,1)} %broadcast_in_dim.84), calls=%async_computation.1 | async-start | bytes 2097152 | tf_op jit(solution)/shard_map/all_to_all | solution.py:121
  70.9 29.2 %all-to-all-done.1.right_ref = bf16[8,128,512]{2,1,0:T(8,128)(2,1)S(1)} async-done(((bf16[8,128,512]{2,1,0:T(8,128)(2,1)}), bf16[8,128,512]{2,1,0:T(8,128)(2,1)S(1)}, u32[]{:S(2)}, u32[]{:S(2)}) %all-to-all-start.1) | async-done | bytes 1048608 | tf_op jit(solution)/shard_map/all_to_all | solution.py:121
  100.1 0.0 all-gather.2.cloned.1.call-done
  100.1 3.7 %product.1 = f32[2,4,128,512]{3,2,1,0:T(8,128)S(1)} custom-call(s32[1]{0:T(128)} %bitcast.z_ref, bf16[8,8,128,128]{3,2,1,0:T(8,128)(2,1)} %bitcast.51, bf16[8,128,512]{2,1,0:T(8,128)(2,1)S(1)} %all-to-all-done.1.right_ref), custom_call_target="tpu_custom_call" | custom-call | flops 1073741824 | bytes 5242880 | tf_op jit(solution)/shard_map/product/pallas_call | solution.py:36
  103.8 5.5 %all_to_all.15 = f32[2,4,128,512]{3,2,1,0:T(8,128)S(1)} all-to-all(f32[2,4,128,512]{3,2,1,0:T(8,128)S(1)} %product.1), channel_id=1, replica_groups=mesh['z'=8,'y'=8,'w'=2,'u'=2,'v'=2,'core'=2] {'core'}, dimensions={0} | all-to-all | bytes 4194304 | tf_op jit(solution)/shard_map/all_to_all | solution.py:124
  109.4 0.3 reduce_sum.9
  109.7 0.7 abs_reduce_fusion
  111.1 0.1 fusion.3
  111.2 1.9 %collective-permute-start.2 = (f16[144,512]{1,0:T(8,128)(2,1)S(1)}, f16[144,512]{1,0:T(8,128)(2,1)S(1)}, u32[]{:S(2)}, u32[]{:S(2)}) collective-permute-start(f16[144,512]{1,0:T(8,128)(2,1)S(1)} %concatenate.9), channel_id=1, source_target_pairs={{0,4},{2,6},{4,0},{6,2},{1,5},{3,7},{5,1},{7,3},{8,12},{10,14},{12... | collective-permute-start | bytes 442376 | tf_op jit(solution)/shard_map/ppermute | solution.py:135
  113.2 2.9 %collective-permute-start.3 = (f16[144,512]{1,0:T(8,128)(2,1)S(1)}, f16[144,512]{1,0:T(8,128)(2,1)S(1)}, u32[]{:S(2)}, u32[]{:S(2)}) collective-permute-start(f16[144,512]{1,0:T(8,128)(2,1)S(1)} %concatenate.10), channel_id=1, source_target_pairs={{0,2},{2,0},{4,6},{6,4},{1,3},{3,1},{5,7},{7,5},{8,10},{10,8},{12,... | collective-permute-start | bytes 442376 | tf_op jit(solution)/shard_map/ppermute | solution.py:135
  116.1 6.6 %collective-permute-start.4 = (f16[144,512]{1,0:T(8,128)(2,1)S(1)}, f16[144,512]{1,0:T(8,128)(2,1)S(1)}, u32[]{:S(2)}, u32[]{:S(2)}) collective-permute-start(f16[144,512]{1,0:T(8,128)(2,1)S(1)} %concatenate.11), channel_id=1, source_target_pairs={{0,6},{2,4},{4,2},{6,0},{1,7},{3,5},{5,3},{7,1},{8,14},{10,12},{12... | collective-permute-start | bytes 442376 | tf_op jit(solution)/shard_map/ppermute | solution.py:135
  122.7 0.0 collective-permute-done.2
  122.7 4.4 %collective-permute-done.3 = f16[144,512]{1,0:T(8,128)(2,1)S(1)} collective-permute-done((f16[144,512]{1,0:T(8,128)(2,1)S(1)}, f16[144,512]{1,0:T(8,128)(2,1)S(1)}, u32[]{:S(2)}, u32[]{:S(2)}) %collective-permute-start.3) | collective-permute-done | bytes 147488 | tf_op jit(solution)/shard_map/ppermute | solution.py:135
  127.1 3.2 %collective-permute-done.4 = f16[144,512]{1,0:T(8,128)(2,1)S(1)} collective-permute-done((f16[144,512]{1,0:T(8,128)(2,1)S(1)}, f16[144,512]{1,0:T(8,128)(2,1)S(1)}, u32[]{:S(2)}, u32[]{:S(2)}) %collective-permute-start.4) | collective-permute-done | bytes 147488 | tf_op jit(solution)/shard_map/ppermute | solution.py:135
  130.3 0.8 fusion.1
  (17 shorter events, 0.3 us)
Async XLA Ops:
  7.7 28.7 %collective-permute-start = (bf16[8,128,128]{1,2,0:T(8,128)(2,1)S(1)}, bf16[8,128,128]{1,2,0:T(8,128)(2,1)S(1)}, u32[]{:S(2)}, u32[]{:S(2)}) collective-permute-start(bf16[8,128,128]{1,2,0:T(8,128)(2,1)S(1)} %bitcast.48), channel_id=1, source_target_pairs={{16,144},{17,145},{18,146},{19,147},{20,148},{21,149},{22,150},{23... | collective-permute-start | bytes 786440 | tf_op jit(solution)/shard_map/ppermute | solution.py:93
  9.2 27.2 %all-to-all-start = ((bf16[8,128,128]{1,2,0:T(8,128)(2,1)}), bf16[8,128,128]{1,2,0:T(8,128)(2,1)S(1)}, u32[]{:S(2)}, u32[]{:S(2)}) async-start(bf16[8,128,128]{1,2,0:T(8,128)(2,1)} %bitcast.3), calls=%async_computation | async-start | bytes 524288 | tf_op jit(solution)/shard_map/all_to_all | solution.py:95
  26.7 73.4 %all-gather.2.cloned.1.call-start = ((), (), s32[]{:S(2)}) async-start(), calls=%async_computation.3 | async-start | bytes 2359296 | tf_op jit(solution)/shard_map/all_gather | solution.py:110
  38.1 0.8 collective-permute-start.1
  41.0 59.1 %all-to-all-start.1 = ((bf16[8,128,512]{2,1,0:T(8,128)(2,1)}), bf16[8,128,512]{2,1,0:T(8,128)(2,1)S(1)}, u32[]{:S(2)}, u32[]{:S(2)}) async-start(bf16[8,128,512]{2,1,0:T(8,128)(2,1)} %broadcast_in_dim.84), calls=%async_computation.1 | async-start | bytes 2097152 | tf_op jit(solution)/shard_map/all_to_all | solution.py:121
  111.2 11.5 %collective-permute-start.2 = (f16[144,512]{1,0:T(8,128)(2,1)S(1)}, f16[144,512]{1,0:T(8,128)(2,1)S(1)}, u32[]{:S(2)}, u32[]{:S(2)}) collective-permute-start(f16[144,512]{1,0:T(8,128)(2,1)S(1)} %concatenate.9), channel_id=1, source_target_pairs={{0,4},{2,6},{4,0},{6,2},{1,5},{3,7},{5,1},{7,3},{8,12},{10,14},{12... | collective-permute-start | bytes 442376 | tf_op jit(solution)/shard_map/ppermute | solution.py:135
  113.2 13.9 %collective-permute-start.3 = (f16[144,512]{1,0:T(8,128)(2,1)S(1)}, f16[144,512]{1,0:T(8,128)(2,1)S(1)}, u32[]{:S(2)}, u32[]{:S(2)}) collective-permute-start(f16[144,512]{1,0:T(8,128)(2,1)S(1)} %concatenate.10), channel_id=1, source_target_pairs={{0,2},{2,0},{4,6},{6,4},{1,3},{3,1},{5,7},{7,5},{8,10},{10,8},{12,... | collective-permute-start | bytes 442376 | tf_op jit(solution)/shard_map/ppermute | solution.py:135
  116.1 14.2 %collective-permute-start.4 = (f16[144,512]{1,0:T(8,128)(2,1)S(1)}, f16[144,512]{1,0:T(8,128)(2,1)S(1)}, u32[]{:S(2)}, u32[]{:S(2)}) collective-permute-start(f16[144,512]{1,0:T(8,128)(2,1)S(1)} %concatenate.11), channel_id=1, source_target_pairs={{0,6},{2,4},{4,2},{6,0},{1,7},{3,5},{5,3},{7,1},{8,14},{10,12},{12... | collective-permute-start | bytes 442376 | tf_op jit(solution)/shard_map/ppermute | solution.py:135
Sparse Core Ops, SparseCore 0:
  38.0 47.1 all-gather.1
